TPU v7x, 32 devices: a whole 2x2x4 slice. The times are simulated.
32 devices in a mesh: seq: 8 (over z, x), batch: 4 (over y, core).
Axes of the slice: x: 2, y: 2, z: 4, core: 2. Of those that a mesh axis runs over, the one named last changes fastest.
Arguments:
- layer_input: bfloat16 [4, 2048, 768], P('batch', 'seq'), may hold values from -6 to 6
- cotangent: bfloat16 [4, 2048, 768], P('batch', 'seq'), may hold values from -6 to 6
- doc_lengths: int32 [4, 4], P('batch'), may hold values from 8 to 2024, as said below
- routes: int32 [3, 4, 256], P(None, 'batch', 'seq'), may hold values from 0 to 7
- norm_gains: bfloat16 [768, 2], P(('seq', 'batch')), may hold values from 0.5 to 1.5
- router: bfloat16 [768, 3], P(('seq', 'batch')), may hold values from -0.21875 to 0.21875
- light_qkv: bfloat16 [768, 2304], P(('seq', 'batch')), may hold values from -0.21875 to 0.21875
- light_out: bfloat16 [768, 768], P(('seq', 'batch')), may hold values from -0.875 to 0.875
- heavy_qkv: bfloat16 [768, 2304], P(('seq', 'batch')), may hold values from -0.21875 to 0.21875
- heavy_out: bfloat16 [768, 768], P(('seq', 'batch')), may hold values from -1.25 to 1.25
- light_in: bfloat16 [768, 2048], P(('seq', 'batch')), may hold values from -0.21875 to 0.21875
- light_down: bfloat16 [1024, 768], P(('seq', 'batch')), may hold values from -0.1875 to 0.1875
- heavy_in: bfloat16 [768, 8192], P(('seq', 'batch')), may hold values from -0.21875 to 0.21875
- heavy_down: bfloat16 [4096, 768], P(('seq', 'batch')), may hold values from -0.09375 to 0.09375
Outputs:
- layer_output: bfloat16 [4, 2048, 768], P('batch', 'seq')
- input_grad: float32 [4, 2048, 768], P('batch', 'seq')
- grad_norm_gains: float32 [768, 2], P(('seq', 'batch'))
- grad_router: float32 [768, 3], P(('seq', 'batch'))
- grad_light_qkv: float32 [768, 2304], P(('seq', 'batch'))
- grad_light_out: float32 [768, 768], P(('seq', 'batch'))
- grad_heavy_qkv: float32 [768, 2304], P(('seq', 'batch'))
- grad_heavy_out: float32 [768, 768], P(('seq', 'batch'))
- grad_light_in: float32 [768, 2048], P(('seq', 'batch'))
- grad_light_down: float32 [1024, 768], P(('seq', 'batch'))
- grad_heavy_in: float32 [768, 8192], P(('seq', 'batch'))
- grad_heavy_down: float32 [4096, 768], P(('seq', 'batch'))
Inputs may be any that keep to these rules, and one draw needn't show every extreme that they name: `doc_lengths`: every length is a multiple of 8 and the lengths of a group sum to its positions. The second document of every group starts within its first 256 positions and ends within its last 256; the other documents lie before or after it. Each branch routes exactly one token of every aligned block of 8 positions.
All inputs are finite; a program needn't handle non-finite values.
Results may differ from a plain program's by a relative error of at most 0.014.
Values may be sent and summed in bfloat16 or wider, within the bound.
No kernel may reach another device: no remote copies, remote signals or barrier semaphores. Data moves between devices by JAX's collectives and lax.ppermute only.
A program may use at most 320 MiB of HBM per device.

v0:
```python
from functools import reduce

import jax
import jax.numpy as jnp
from jax import lax
from jax.sharding import PartitionSpec as P

HL = 8
DL = 96
HH = 12
DH = 64
WIN = 128
ROUTE = 8


epsilon = 1e-06
highest = lax.Precision.HIGHEST


def with_halo(cells, sides, width):
    for axis, dim in sides:
        count = lax.axis_size(axis)
        ends = count - 1
        head = lax.slice_in_dim(cells, 0, width, axis=dim)
        tail = lax.slice_in_dim(cells, cells.shape[dim] - width, cells.shape[dim], axis=dim)
        cells = jnp.concatenate(
            [
                lax.ppermute(tail, axis, [(i, (i + 1) % count) for i in range(ends)]),
                cells,
                lax.ppermute(head, axis, [((i + 1) % count, i) for i in range(ends)]),
            ],
            axis=dim,
        )
    return cells


def passed_along(block, axis, distance):
    devices = range(lax.axis_size(axis))
    route = [(i - distance, i) for i in devices if i - distance in devices]
    return lax.ppermute(block, axis, route)


def rms_scale(values, gain):
    return values * lax.rsqrt(jnp.mean(values * values, axis=-1, keepdims=True) + epsilon) * gain


def geglu(both):
    half = both.shape[-1] // 2
    return jax.nn.gelu(both[:, :half]) * both[:, half:]


def document_of(positions, lengths):
    ends = jnp.cumsum(lengths)
    return jnp.sum((positions[:, None] >= ends[None, :]).astype(jnp.int32), axis=1)


def select_rows(rows, picks):
    routed = picks.shape[0]
    blocks = rows.reshape(routed, rows.shape[0] // routed, rows.shape[1])
    onehot = (
        lax.broadcasted_iota(jnp.int32, (routed, blocks.shape[1]), 1) == picks[:, None]
    ).astype(rows.dtype)
    return jnp.sum(blocks * onehot[:, :, None], axis=1).astype(rows.dtype)


def spread_rows(rows, picks):
    routed = picks.shape[0]
    onehot = (lax.broadcasted_iota(jnp.int32, (routed, ROUTE), 1) == picks[:, None]).astype(
        rows.dtype
    )
    return (onehot[:, :, None] * rows[:, None, :]).reshape(routed * ROUTE, rows.shape[1])


def attend(queries, keys, values, allowed, scale, with_total):
    scores = jnp.einsum("qhe,khe->hqk", queries, keys, preferred_element_type=jnp.float32) * scale
    masked = jnp.where(allowed[None], scores, -1e30)
    probs = jax.nn.softmax(masked, axis=-1)
    probs_low = probs.astype(jnp.bfloat16)
    mixed = jnp.einsum("hqk,khe->qhe", probs_low, values, preferred_element_type=jnp.float32)
    totals = jax.nn.logsumexp(masked, axis=-1) if with_total else None
    return (probs, probs_low, mixed.astype(jnp.bfloat16), totals)


def score_grads(probs, grad_mixed, values):
    grad_probs = jnp.einsum("qhe,khe->hqk", grad_mixed, values, preferred_element_type=jnp.float32)
    weighted = jnp.sum(probs * grad_probs, axis=-1)
    grad_scores = probs * (grad_probs - weighted[:, :, None])
    return (grad_scores.astype(jnp.bfloat16), weighted)


def attention_back(probs, probs_low, grad_mixed, queries, keys, values, scale):
    scores_low, unused = score_grads(probs, grad_mixed, values)
    grad_queries = (
        jnp.einsum("hqk,khe->qhe", scores_low, keys, preferred_element_type=jnp.float32) * scale
    )
    grad_keys = (
        jnp.einsum("hqk,qhe->khe", scores_low, queries, preferred_element_type=jnp.float32) * scale
    )
    grad_values = jnp.einsum(
        "hqk,qhe->khe", probs_low, grad_mixed, preferred_element_type=jnp.float32
    )
    return (grad_queries, grad_keys, grad_values)


def left_product(left, right):
    return jnp.einsum("ti,tj->ij", left, right, preferred_element_type=jnp.float32)


def right_product(left, right):
    return jnp.einsum("tj,ij->ti", left, right, preferred_element_type=jnp.float32)


def add_trees(first_tree, second_tree):
    return jax.tree.map(jnp.add, first_tree, second_tree)


def forward_group(inputs_low, lengths, picks, weights):
    (
        full_gains,
        full_router,
        full_light_qkv,
        full_light_out,
        full_heavy_qkv,
        full_heavy_out,
        full_light_in,
        full_light_down,
        full_heavy_in,
        full_heavy_down,
    ) = weights
    positions_dev = inputs_low.shape[0]
    features = inputs_low.shape[1]
    devices = lax.axis_size("seq")
    group_length = positions_dev * devices
    offset = lax.axis_index("seq") * positions_dev
    inputs = inputs_low.astype(jnp.float32)
    gains = full_gains.astype(jnp.float32)
    router_full = full_router.astype(jnp.float32)
    positions = offset + jnp.arange(positions_dev, dtype=jnp.int32)
    documents = document_of(positions, lengths)
    routed = positions_dev // ROUTE
    picks_query = picks[0]
    picks_key = picks[1]
    picks_ffn = picks[2]
    normed, norm_back = jax.vjp(rms_scale, inputs, gains[:, 0])
    normed_low = normed.astype(jnp.bfloat16)
    qkv = jnp.dot(normed_low, full_light_qkv, preferred_element_type=jnp.float32).astype(
        jnp.bfloat16
    )
    light_q = qkv[:, :features].reshape(positions_dev, HL, DL)
    extended = with_halo(qkv[:, features:], (("seq", 0),), WIN)
    light_k = extended[:, :features].reshape(-1, HL, DL)
    light_v = extended[:, features:].reshape(-1, HL, DL)
    key_pos = offset - WIN + jnp.arange(positions_dev + 2 * WIN, dtype=jnp.int32)
    key_docs = document_of(key_pos, lengths)
    inside = (key_pos >= 0) & (key_pos < group_length)
    nearby = jnp.abs(positions[:, None] - key_pos[None, :]) < WIN
    light_allowed = nearby & inside[None, :] & (documents[:, None] == key_docs[None, :])
    light_scale = DL ** (-0.5)
    light_probs, light_low, light_mixed, unused = attend(
        light_q, light_k, light_v, light_allowed, light_scale, False
    )
    light_mixed = light_mixed.reshape(positions_dev, features)
    light_branch = jnp.dot(light_mixed, full_light_out, preferred_element_type=jnp.float32)
    query_in = select_rows(normed_low, picks_query)
    key_in = select_rows(normed_low, picks_key)
    query_norm = select_rows(normed, picks_query)
    key_norm = select_rows(normed, picks_key)
    query_gate = jax.nn.sigmoid(jnp.dot(query_norm, router_full[:, 0], precision=highest))
    key_gate = jax.nn.sigmoid(jnp.dot(key_norm, router_full[:, 1], precision=highest))
    heavy_q = jnp.dot(
        query_in, full_heavy_qkv[:, :features], preferred_element_type=jnp.float32
    ).astype(jnp.bfloat16)
    key_raw = jnp.dot(key_in, full_heavy_qkv[:, features:], preferred_element_type=jnp.float32)
    heavy_kv = jnp.concatenate(
        [key_raw[:, :features], key_raw[:, features:] * key_gate[:, None]], axis=1
    ).astype(jnp.bfloat16)
    group_kv = lax.all_gather(heavy_kv, "seq", axis=0, tiled=True)
    heavy_k = group_kv[:, :features].reshape(-1, HH, DH)
    heavy_v = group_kv[:, features:].reshape(-1, HH, DH)
    routed_key_docs = document_of(jnp.arange(routed * devices, dtype=jnp.int32) * ROUTE, lengths)
    routed_query_docs = document_of(offset + jnp.arange(routed, dtype=jnp.int32) * ROUTE, lengths)
    heavy_allowed = routed_query_docs[:, None] == routed_key_docs[None, :]
    heavy_queries = heavy_q.reshape(routed, HH, DH)
    heavy_scale = DH ** (-0.5)
    heavy_probs, heavy_low, heavy_mixed, heavy_totals = attend(
        heavy_queries, heavy_k, heavy_v, heavy_allowed, heavy_scale, True
    )
    heavy_mixed = heavy_mixed.reshape(routed, features)
    heavy_raw = jnp.dot(heavy_mixed, full_heavy_out, preferred_element_type=jnp.float32)
    middle = inputs + light_branch + spread_rows(heavy_raw * query_gate[:, None], picks_query)
    normed2, norm2_back = jax.vjp(rms_scale, middle, gains[:, 1])
    normed2_low = normed2.astype(jnp.bfloat16)
    light_pair = jnp.dot(normed2_low, full_light_in, preferred_element_type=jnp.float32)
    light_hidden, light_hidden_back = jax.vjp(geglu, light_pair)
    light_hidden_low = light_hidden.astype(jnp.bfloat16)
    light_ffn = jnp.dot(light_hidden_low, full_light_down, preferred_element_type=jnp.float32)
    ffn_in = select_rows(normed2_low, picks_ffn)
    ffn_norm = select_rows(normed2, picks_ffn)
    ffn_gate = jax.nn.sigmoid(jnp.dot(ffn_norm, router_full[:, 2], precision=highest))
    heavy_pair = jnp.dot(ffn_in, full_heavy_in, preferred_element_type=jnp.float32)
    heavy_hidden, heavy_hidden_back = jax.vjp(geglu, heavy_pair)
    heavy_hidden_low = heavy_hidden.astype(jnp.bfloat16)
    heavy_ffn = jnp.dot(heavy_hidden_low, full_heavy_down, preferred_element_type=jnp.float32)
    output = middle + light_ffn + spread_rows(heavy_ffn * ffn_gate[:, None], picks_ffn)
    return dict(
        output=output,
        picks=picks,
        router_full=router_full,
        norm_back=norm_back,
        normed_low=normed_low,
        light_q=light_q,
        light_k=light_k,
        light_v=light_v,
        light_probs=light_probs,
        light_low=light_low,
        light_mixed=light_mixed,
        query_in=query_in,
        key_in=key_in,
        query_norm=query_norm,
        key_norm=key_norm,
        query_gate=query_gate,
        key_gate=key_gate,
        heavy_q=heavy_q,
        key_raw=key_raw,
        heavy_kv=heavy_kv,
        heavy_k=heavy_k,
        heavy_v=heavy_v,
        heavy_allowed=heavy_allowed,
        heavy_queries=heavy_queries,
        heavy_probs=heavy_probs,
        heavy_low=heavy_low,
        heavy_totals=heavy_totals,
        heavy_mixed=heavy_mixed,
        heavy_raw=heavy_raw,
        norm2_back=norm2_back,
        normed2_low=normed2_low,
        light_hidden_back=light_hidden_back,
        light_hidden_low=light_hidden_low,
        ffn_in=ffn_in,
        ffn_norm=ffn_norm,
        ffn_gate=ffn_gate,
        heavy_hidden_back=heavy_hidden_back,
        heavy_hidden_low=heavy_hidden_low,
        heavy_ffn=heavy_ffn,
    )


def ffn_backward(stored, cotangent_low, weights):
    full_light_in = weights[6]
    full_light_down = weights[7]
    full_heavy_in = weights[8]
    full_heavy_down = weights[9]
    picks_ffn = stored["picks"][2]
    ffn_gate = stored["ffn_gate"]
    grad_out = cotangent_low.astype(jnp.float32)
    grad_low = grad_out.astype(jnp.bfloat16)
    grad_light_down = left_product(stored["light_hidden_low"], grad_low)
    grad_light_pair = stored["light_hidden_back"](right_product(grad_low, full_light_down))[
        0
    ].astype(jnp.bfloat16)
    grad_light_in = left_product(stored["normed2_low"], grad_light_pair)
    grad_normed2 = right_product(grad_light_pair, full_light_in)
    ffn_rows_grad = select_rows(grad_out, picks_ffn)
    grad_heavy_ffn = (ffn_rows_grad * ffn_gate[:, None]).astype(jnp.bfloat16)
    grad_ffn_gate = jnp.sum(ffn_rows_grad * stored["heavy_ffn"], axis=1)
    grad_heavy_down = left_product(stored["heavy_hidden_low"], grad_heavy_ffn)
    grad_heavy_pair = stored["heavy_hidden_back"](right_product(grad_heavy_ffn, full_heavy_down))[
        0
    ].astype(jnp.bfloat16)
    grad_heavy_in = left_product(stored["ffn_in"], grad_heavy_pair)
    ffn_logit = grad_ffn_gate * ffn_gate * (1.0 - ffn_gate)
    router_ffn = jnp.dot(ffn_logit, stored["ffn_norm"], precision=highest)
    ffn_back = (
        right_product(grad_heavy_pair, full_heavy_in)
        + ffn_logit[:, None] * stored["router_full"][None, :, 2]
    )
    grad_normed2 = grad_normed2 + spread_rows(ffn_back, picks_ffn)
    grad_middle_norm, grad_gain_second = stored["norm2_back"](grad_normed2)
    grad_middle = grad_out + grad_middle_norm
    return (
        grad_middle,
        (grad_light_in, grad_light_down, grad_heavy_in, grad_heavy_down),
        (router_ffn, grad_gain_second),
    )


def attention_backward(stored, grad_middle, weights):
    full_light_qkv = weights[2]
    full_light_out = weights[3]
    full_heavy_qkv = weights[4]
    full_heavy_out = weights[5]
    router_full = stored["router_full"]
    picks_query = stored["picks"][0]
    picks_key = stored["picks"][1]
    positions_dev, features = grad_middle.shape
    routed = positions_dev // ROUTE
    light_scale = DL ** (-0.5)
    heavy_scale = DH ** (-0.5)
    middle_low = grad_middle.astype(jnp.bfloat16)
    grad_light_out = left_product(stored["light_mixed"], middle_low)
    grad_light_mixed = (
        right_product(middle_low, full_light_out)
        .astype(jnp.bfloat16)
        .reshape(positions_dev, HL, DL)
    )
    light_dq, light_dk, light_dv = attention_back(
        stored["light_probs"],
        stored["light_low"],
        grad_light_mixed,
        stored["light_q"],
        stored["light_k"],
        stored["light_v"],
        light_scale,
    )
    pair_grads = jnp.concatenate(
        [light_dk.reshape(-1, features), light_dv.reshape(-1, features)], axis=1
    )
    from_above = passed_along(pair_grads[:WIN].astype(jnp.bfloat16), "seq", -1).astype(jnp.float32)
    from_below = passed_along(
        pair_grads[positions_dev + WIN :].astype(jnp.bfloat16), "seq", 1
    ).astype(jnp.float32)
    own_rows = pair_grads[WIN : WIN + positions_dev]
    own_rows = (
        own_rows
        + jnp.pad(from_below, ((0, positions_dev - WIN), (0, 0)))
        + jnp.pad(from_above, ((positions_dev - WIN, 0), (0, 0)))
    )
    grad_qkv = jnp.concatenate(
        [light_dq.reshape(positions_dev, features), own_rows], axis=1
    ).astype(jnp.bfloat16)
    grad_light_qkv = left_product(stored["normed_low"], grad_qkv)
    grad_normed = right_product(grad_qkv, full_light_qkv)
    query_gate = stored["query_gate"]
    key_gate = stored["key_gate"]
    key_raw = stored["key_raw"]
    query_rows_grad = select_rows(grad_middle, picks_query)
    grad_heavy_raw = (query_rows_grad * query_gate[:, None]).astype(jnp.bfloat16)
    grad_query_gate = jnp.sum(query_rows_grad * stored["heavy_raw"], axis=1)
    grad_heavy_out = left_product(stored["heavy_mixed"], grad_heavy_raw)
    grad_heavy_flat = right_product(grad_heavy_raw, full_heavy_out).astype(jnp.bfloat16)
    grad_heavy_mixed = grad_heavy_flat.reshape(routed, HH, DH)
    heavy_dq, heavy_dk, heavy_dv = attention_back(
        stored["heavy_probs"],
        stored["heavy_low"],
        grad_heavy_mixed,
        stored["heavy_queries"],
        stored["heavy_k"],
        stored["heavy_v"],
        heavy_scale,
    )
    group_grads = jnp.concatenate(
        [heavy_dk.reshape(-1, features), heavy_dv.reshape(-1, features)], axis=1
    )
    routed_grads = lax.psum_scatter(group_grads, "seq", scatter_dimension=0, tiled=True)
    grad_key_low = routed_grads[:, :features].astype(jnp.bfloat16)
    grad_value = routed_grads[:, features:].astype(jnp.bfloat16).astype(jnp.float32)
    grad_key_gate = jnp.sum(grad_value * key_raw[:, features:], axis=1)
    grad_key_raw = jnp.concatenate(
        [grad_key_low, (grad_value * key_gate[:, None]).astype(jnp.bfloat16)], axis=1
    )
    grad_query = heavy_dq.reshape(routed, features).astype(jnp.bfloat16)
    grad_heavy_qkv = jnp.concatenate(
        [
            left_product(stored["query_in"], grad_query),
            left_product(stored["key_in"], grad_key_raw),
        ],
        axis=1,
    )
    query_logit = grad_query_gate * query_gate * (1.0 - query_gate)
    key_logit = grad_key_gate * key_gate * (1.0 - key_gate)
    query_back = (
        right_product(grad_query, full_heavy_qkv[:, :features])
        + query_logit[:, None] * router_full[None, :, 0]
    )
    key_back = (
        right_product(grad_key_raw, full_heavy_qkv[:, features:])
        + key_logit[:, None] * router_full[None, :, 1]
    )
    grad_normed = (
        grad_normed + spread_rows(query_back, picks_query) + spread_rows(key_back, picks_key)
    )
    router_query = jnp.dot(query_logit, stored["query_norm"], precision=highest)
    router_key = jnp.dot(key_logit, stored["key_norm"], precision=highest)
    grad_inputs_norm, grad_gain_first = stored["norm_back"](grad_normed)
    input_grad = grad_middle + grad_inputs_norm
    return (
        input_grad,
        (
            grad_gain_first,
            router_query,
            router_key,
            grad_light_qkv,
            grad_light_out,
            grad_heavy_qkv,
            grad_heavy_out,
        ),
    )


def local(
    layer_input,
    cotangent,
    doc_lengths,
    routes,
    norm_gains,
    router,
    light_qkv,
    light_out,
    heavy_qkv,
    heavy_out,
    light_in,
    light_down,
    heavy_in,
    heavy_down,
):
    gathered = (
        lax.all_gather(norm_gains, ("seq", "batch"), axis=0, tiled=True),
        lax.all_gather(router, ("seq", "batch"), axis=0, tiled=True),
        lax.all_gather(light_qkv, ("seq", "batch"), axis=0, tiled=True),
        lax.all_gather(light_out, ("seq", "batch"), axis=0, tiled=True),
        lax.all_gather(heavy_qkv, ("seq", "batch"), axis=0, tiled=True),
        lax.all_gather(heavy_out, ("seq", "batch"), axis=0, tiled=True),
        lax.all_gather(light_in, ("seq", "batch"), axis=0, tiled=True),
        lax.all_gather(light_down, ("seq", "batch"), axis=0, tiled=True),
        lax.all_gather(heavy_in, ("seq", "batch"), axis=0, tiled=True),
        lax.all_gather(heavy_down, ("seq", "batch"), axis=0, tiled=True),
    )
    weights = tuple(gathered)
    stored_all = [forward_group(layer_input[0], doc_lengths[0], routes[:, 0], weights)]
    outputs = jnp.stack([stored["output"].astype(jnp.bfloat16) for stored in stored_all])
    member = 0
    grad_middle, ffn_terms, small_terms = ffn_backward(
        stored_all[member], cotangent[member], weights
    )
    middles = [grad_middle]
    ffn_parts = [ffn_terms]
    small_parts = [small_terms]
    ffn_sum = reduce(add_trees, ffn_parts)
    router_ffn, gain_second = reduce(add_trees, small_parts)
    member = 0
    input_grad, attention_terms = attention_backward(stored_all[member], middles[member], weights)
    input_grads = [input_grad]
    attention_parts = [attention_terms]
    (
        gain_first,
        router_query,
        router_key,
        grad_light_qkv,
        grad_light_out,
        grad_heavy_qkv,
        grad_heavy_out,
    ) = reduce(add_trees, attention_parts)
    grad_gains = jnp.stack([gain_first, gain_second], axis=1)
    grad_router = jnp.stack([router_query, router_key, router_ffn], axis=1)
    shards = (
        lax.psum_scatter(grad_gains, ("seq", "batch"), scatter_dimension=0, tiled=True),
        lax.psum_scatter(grad_router, ("seq", "batch"), scatter_dimension=0, tiled=True),
        lax.psum_scatter(grad_light_qkv, ("seq", "batch"), scatter_dimension=0, tiled=True),
        lax.psum_scatter(grad_light_out, ("seq", "batch"), scatter_dimension=0, tiled=True),
        lax.psum_scatter(grad_heavy_qkv, ("seq", "batch"), scatter_dimension=0, tiled=True),
        lax.psum_scatter(grad_heavy_out, ("seq", "batch"), scatter_dimension=0, tiled=True),
        lax.psum_scatter(ffn_sum[0], ("seq", "batch"), scatter_dimension=0, tiled=True),
        lax.psum_scatter(ffn_sum[1], ("seq", "batch"), scatter_dimension=0, tiled=True),
        lax.psum_scatter(ffn_sum[2], ("seq", "batch"), scatter_dimension=0, tiled=True),
        lax.psum_scatter(ffn_sum[3], ("seq", "batch"), scatter_dimension=0, tiled=True),
    )
    return (
        outputs,
        jnp.stack(input_grads),
        shards[0],
        shards[1],
        shards[2],
        shards[3],
        shards[4],
        shards[5],
        shards[6],
        shards[7],
        shards[8],
        shards[9],
    )


def solution(mesh):
    return jax.shard_map(
        local,
        mesh=mesh,
        in_specs=(
            P("batch", "seq", None),
            P("batch", "seq", None),
            P("batch", None),
            P(None, "batch", "seq"),
            P(("seq", "batch"), None),
            P(("seq", "batch"), None),
            P(("seq", "batch"), None),
            P(("seq", "batch"), None),
            P(("seq", "batch"), None),
            P(("seq", "batch"), None),
            P(("seq", "batch"), None),
            P(("seq", "batch"), None),
            P(("seq", "batch"), None),
            P(("seq", "batch"), None),
        ),
        out_specs=(
            P("batch", "seq", None),
            P("batch", "seq", None),
            P(("seq", "batch"), None),
            P(("seq", "batch"), None),
            P(("seq", "batch"), None),
            P(("seq", "batch"), None),
            P(("seq", "batch"), None),
            P(("seq", "batch"), None),
            P(("seq", "batch"), None),
            P(("seq", "batch"), None),
            P(("seq", "batch"), None),
            P(("seq", "batch"), None),
        ),
        check_vma=False,
    )
```

profile of v0, /device:TPU:10, one launch (start us, length us, event | category | flops | bytes accessed | tf_op | source)
XLA Modules:
  0.0 1755.5 jit_solution(6861508171142506566)
XLA Ops:
  14.5 31.7 %all-gather = bf16[32,24,2]{1,2,0:T(2,128)(2,1)S(1)} all-gather(bf16[1,24,2]{1,2,0:T(2,128)(2,1)} %bitcast.276), channel_id=1, replica_groups=mesh['seq'=8,'batch'=4] {'seq','batch'}, dimensions={0}, use_global_device_ids=true | all-gather | bytes 3168 | tf_op jit(solution)/shard_map/all_gather | solution.py:417
  48.7 36.9 %all-gather.1 = bf16[32,24,3]{1,2,0:T(4,128)(2,1)S(1)} all-gather(bf16[1,24,3]{1,2,0:T(4,128)(2,1)} %bitcast.275), channel_id=1, replica_groups=mesh['seq'=8,'batch'=4] {'seq','batch'}, dimensions={0}, use_global_device_ids=true | all-gather | bytes 4752 | tf_op jit(solution)/shard_map/all_gather | solution.py:418
  91.8 3.1 convolution_convert_fusion
  95.0 38.8 %all-gather.15.cloned.1.call-done = bf16[768,2304]{1,0:T(8,128)(2,1)} async-done(((bf16[24,2304]{1,0:T(8,128)(2,1)}), bf16[768,2304]{1,0:T(8,128)(2,1)}) %all-gather.15.cloned.1.call-update) | async-done | bytes 3538960 | tf_op jit(solution)/shard_map/all_gather | solution.py:421
  137.9 29.0 %all_gather.38 = bf16[256,1536]{1,0:T(8,128)(2,1)S(1)} all-gather(bf16[32,1536]{1,0:T(8,128)(2,1)S(1)} %pad_maximum_fusion.7), channel_id=1, replica_groups=mesh['seq'=8,'batch'=4] {'seq'}, dimensions={0}, use_global_device_ids=true | all-gather | bytes 884736 | tf_op jit(solution)/shard_map/all_gather | solution.py:177
  168.3 3.0 collective-permute-start
  171.3 3.1 collective-permute-start.1
  176.7 16.8 all-gather.17.cloned.1.call-done
  197.9 3.7 fusion.144
  202.2 3.1 convolution_convert_fusion.2
  205.4 44.0 %all-gather.13.cloned.1.call-done = bf16[768,768]{1,0:T(8,128)(2,1)} async-done(((bf16[24,768]{1,0:T(8,128)(2,1)}), bf16[768,768]{1,0:T(8,128)(2,1)}) %all-gather.13.cloned.1.call-update) | async-done | bytes 1179664 | tf_op jit(solution)/shard_map/all_gather | solution.py:420
  252.5 57.6 %all-gather.19.cloned.1.call-done = bf16[768,2048]{1,0:T(8,128)(2,1)} async-done(((bf16[24,2048]{1,0:T(8,128)(2,1)}), bf16[768,2048]{1,0:T(8,128)(2,1)}) %all-gather.19.cloned.1.call-update) | async-done | bytes 3145744 | tf_op jit(solution)/shard_map/all_gather | solution.py:423
  310.1 4.2 fusion.146
  314.3 52.5 %all-gather.21.cloned.1.call-done = bf16[1024,768]{1,0:T(8,128)(2,1)} async-done(((bf16[32,768]{1,0:T(8,128)(2,1)}), bf16[1024,768]{1,0:T(8,128)(2,1)}) %all-gather.21.cloned.1.call-update) | async-done | bytes 1572880 | tf_op jit(solution)/shard_map/all_gather | solution.py:424
  366.7 4.7 fusion.90
  371.4 93.5 %all-gather.23.cloned.1.call-done = bf16[768,8192]{1,0:T(8,128)(2,1)} async-done(((bf16[24,8192]{1,0:T(8,128)(2,1)}), bf16[768,8192]{1,0:T(8,128)(2,1)}) %all-gather.23.cloned.1.call-update) | async-done | bytes 12582928 | tf_op jit(solution)/shard_map/all_gather | solution.py:425
  464.9 7.8 fusion.147
  472.7 63.5 %all-gather.25.cloned.1.call-done = bf16[4096,768]{1,0:T(8,128)(2,1)} async-done(((bf16[128,768]{1,0:T(8,128)(2,1)}), bf16[4096,768]{1,0:T(8,128)(2,1)}) %all-gather.25.cloned.1.call-update) | async-done | bytes 6291472 | tf_op jit(solution)/shard_map/all_gather | solution.py:426
  536.2 5.1 fusion.96
  541.4 5.3 multiply_reduce_fusion.8
  546.8 4.0 convolution_add_fusion.5
  550.9 4.4 multiply_reduce_fusion.1
  559.2 3.0 fusion.102
  562.2 2.7 multiply_reduce_fusion.4
  576.3 3.4 fusion.85
  579.8 5.2 fusion.97
  594.4 6.2 multiply_reduce_fusion
  600.7 4.1 multiply_convert_fusion
  607.2 2.8 collective-permute-start.2
  609.9 3.3 collective-permute-start.3
  614.1 15.6 collective-permute-done.2
  630.9 4.1 fusion.76
  638.0 2.8 fusion.148
  640.7 7.2 reduce-scatter.12.cloned.1.call-done
  650.8 3.4 pad_maximum_fusion
  655.1 6.5 fusion.136
  661.6 10.4 fusion.105
  675.6 2.8 fusion.21
  679.3 3.6 fusion.60
  683.1 40.6 %all-reduce.8 = (f32[768,2]{0,1:T(2,128)S(1)}, f32[768,3]{0,1:T(4,128)S(1)}) all-reduce(f32[768,2]{0,1:T(2,128)S(1)} %pad_maximum_fusion.12, f32[768,3]{0,1:T(4,128)S(1)} %pad_maximum_fusion.11), channel_id=3, replica_groups=mesh['seq'=8,'batch'=4] {'seq','batch'}, use_global_device_ids=true, to_apply=%region_29.30.clone | all-reduce | flops 3840 | bytes 30720
  726.2 29.2 %reduce-scatter.24.cloned.1.call-done = f32[32,768]{1,0:T(8,128)} async-done(((f32[1024,768]{1,0:T(8,128)}), f32[32,768]{1,0:T(8,128)}) %reduce-scatter.24.cloned.1.call-update) | async-done | bytes 98320 | tf_op jit(solution)/shard_map/reduce_scatter | solution.py:463
  755.4 120.6 %reduce-scatter.22.cloned.1.call-done = f32[24,2048]{1,0:T(8,128)} async-done(((f32[768,2048]{1,0:T(8,128)}), f32[24,2048]{1,0:T(8,128)}) %reduce-scatter.22.cloned.1.call-update) | async-done | bytes 196624 | tf_op jit(solution)/shard_map/reduce_scatter | solution.py:462
  876.0 103.9 %reduce-scatter.16.cloned.1.call-done = f32[24,768]{1,0:T(8,128)} async-done(((f32[768,768]{1,0:T(8,128)}), f32[24,768]{1,0:T(8,128)}) %reduce-scatter.16.cloned.1.call-update) | async-done | bytes 73744 | tf_op jit(solution)/shard_map/reduce_scatter | solution.py:459
  979.9 104.8 %reduce-scatter.20.cloned.1.call-done = f32[24,768]{1,0:T(8,128)} async-done(((f32[768,768]{1,0:T(8,128)}), f32[24,768]{1,0:T(8,128)}) %reduce-scatter.20.cloned.1.call-update) | async-done | bytes 73744 | tf_op jit(solution)/shard_map/reduce_scatter | solution.py:461
  1084.7 124.4 %reduce-scatter.14.cloned.1.call-done = f32[24,2304]{1,0:T(8,128)} async-done(((f32[768,2304]{1,0:T(8,128)}), f32[24,2304]{1,0:T(8,128)}) %reduce-scatter.14.cloned.1.call-update) | async-done | bytes 221200 | tf_op jit(solution)/shard_map/reduce_scatter | solution.py:458
  1209.1 125.3 %reduce-scatter.18.cloned.1.call-done = f32[24,2304]{1,0:T(8,128)} async-done(((f32[768,2304]{1,0:T(8,128)}), f32[24,2304]{1,0:T(8,128)}) %reduce-scatter.18.cloned.1.call-update) | async-done | bytes 221200 | tf_op jit(solution)/shard_map/reduce_scatter | solution.py:460
  1334.5 161.1 %reduce-scatter.28.cloned.1.call-done = f32[128,768]{1,0:T(8,128)} async-done(((f32[4096,768]{1,0:T(8,128)}), f32[128,768]{1,0:T(8,128)}) %reduce-scatter.28.cloned.1.call-update) | async-done | bytes 393232 | tf_op jit(solution)/shard_map/reduce_scatter | solution.py:465
  1495.6 252.9 %reduce-scatter.26.cloned.1.call-done = f32[24,8192]{1,0:T(8,128)} async-done(((f32[768,8192]{1,0:T(8,128)}), f32[24,8192]{1,0:T(8,128)}) %reduce-scatter.26.cloned.1.call-update) | async-done | bytes 786448 | tf_op jit(solution)/shard_map/reduce_scatter | solution.py:464
  (343 shorter events, 73.7 us)
Async XLA Ops:
  7.2 82.6 %copy-start.1 = (bf16[1,256,768]{2,1,0:T(8,128)(2,1)S(1)}, bf16[1,256,768]{2,1,0:T(8,128)(2,1)}, u32[]{:S(2)}) copy-start(bf16[1,256,768]{2,1,0:T(8,128)(2,1)} %param.14) | copy-start | bytes 1179652
  7.2 84.6 %all-gather.11.cloned.1.call-start = ((), (), s32[]{:S(2)}) async-start(), calls=%async_computation.9 | async-start | bytes 3649536 | tf_op jit(solution)/shard_map/all_gather | solution.py:419
  7.9 125.8 %all-gather.15.cloned.1.call-start = ((), (), s32[]{:S(2)}) async-start(), calls=%async_computation.11 | async-start | bytes 3649536 | tf_op jit(solution)/shard_map/all_gather | solution.py:421
  8.7 184.8 %all-gather.17.cloned.1.call-start = ((), (), s32[]{:S(2)}) async-start(), calls=%async_computation.12 | async-start | bytes 1216512 | tf_op jit(solution)/shard_map/all_gather | solution.py:422
  9.4 240.0 %all-gather.13.cloned.1.call-start = ((), (), s32[]{:S(2)}) async-start(), calls=%async_computation.10 | async-start | bytes 1216512 | tf_op jit(solution)/shard_map/all_gather | solution.py:420
  10.0 300.1 %all-gather.19.cloned.1.call-start = ((), (), s32[]{:S(2)}) async-start(), calls=%async_computation.13 | async-start | bytes 3244032 | tf_op jit(solution)/shard_map/all_gather | solution.py:423
  10.6 356.1 %all-gather.21.cloned.1.call-start = ((), (), s32[]{:S(2)}) async-start(), calls=%async_computation.14 | async-start | bytes 1622016 | tf_op jit(solution)/shard_map/all_gather | solution.py:424
  11.1 453.7 %all-gather.23.cloned.1.call-start = ((), (), s32[]{:S(2)}) async-start(), calls=%async_computation.15 | async-start | bytes 12976128 | tf_op jit(solution)/shard_map/all_gather | solution.py:425
  11.9 524.3 %all-gather.25.cloned.1.call-start = ((), (), s32[]{:S(2)}) async-start(), calls=%async_computation.16 | async-start | bytes 6488064 | tf_op jit(solution)/shard_map/all_gather | solution.py:426
  12.6 635.3 %reduce-scatter.12.cloned.1.call-start = ((), (), s32[]{:S(2)}) async-start(), calls=%async_computation.17 | async-start | bytes 1769472 | tf_op jit(solution)/shard_map/reduce_scatter | solution.py:354
  14.4 80.5 %copy-start.70 = (f32[256]{0:T(256)}, f32[256]{0:T(256)S(1)}, u32[]{:S(2)}) copy-start(f32[256]{0:T(256)S(1)} %fusion.121) | copy-start | bytes 3076
  48.6 41.2 %copy-start.51 = (f32[32,8]{1,0:T(8,128)}, f32[32,8]{1,0:T(8,128)S(1)}, u32[]{:S(2)}) copy-start(f32[32,8]{1,0:T(8,128)S(1)} %get-tuple-element.60) | copy-start | bytes 3076
  48.7 200.7 %copy-start.98 = (f32[256]{0:T(256)}, f32[256]{0:T(256)S(1)}, u32[]{:S(2)}) copy-start(f32[256]{0:T(256)S(1)} %reshape.551) | copy-start | bytes 3076
  90.4 43.4 %copy-start.57 = (bf16[32,768]{1,0:T(8,128)(2,1)}, bf16[32,768]{1,0:T(8,128)(2,1)S(1)}, u32[]{:S(2)}) copy-start(bf16[32,768]{1,0:T(8,128)(2,1)S(1)} %get-tuple-element.18) | copy-start | bytes 147460
  90.4 45.1 %copy-start.37 = (bf16[32,768]{1,0:T(8,128)(2,1)}, bf16[32,768]{1,0:T(8,128)(2,1)S(1)}, u32[]{:S(2)}) copy-start(bf16[32,768]{1,0:T(8,128)(2,1)S(1)} %get-tuple-element.19) | copy-start | bytes 147460
  90.6 102.9 %copy-start.84 = (f32[32]{0:T(128)}, f32[32]{0:T(128)S(1)}, u32[]{:S(2)}) copy-start(f32[32]{0:T(128)S(1)} %fusion.37) | copy-start | bytes 388
  90.9 46.9 %copy-start.88 = (f32[32]{0:T(128)}, f32[32]{0:T(128)S(1)}, u32[]{:S(2)}) copy-start(f32[32]{0:T(128)S(1)} %fusion.41) | copy-start | bytes 388
  95.0 72.3 %copy-start.10 = (bf16[256,2304]{1,0:T(8,128)(2,1)}, bf16[256,2304]{1,0:T(8,128)(2,1)S(1)}, u32[]{:S(2)}) copy-start(bf16[256,2304]{1,0:T(8,128)(2,1)S(1)} %convolution_convert_fusion) | copy-start | bytes 3538948
  135.5 38.9 %copy-start.35 = (bf16[32,12,64]{2,1,0:T(8,128)(2,1)}, bf16[32,12,64]{2,1,0:T(8,128)(2,1)S(1)}, u32[]{:S(2)}) copy-start(bf16[32,12,64]{2,1,0:T(8,128)(2,1)S(1)} %reshape.537) | copy-start | bytes 147460
  137.8 29.1 %copy-start.27 = (f32[32,1536]{1,0:T(8,128)}, f32[32,1536]{1,0:T(8,128)S(1)}, u32[]{:S(2)}) copy-start(f32[32,1536]{1,0:T(8,128)S(1)} %fusion.9) | copy-start | bytes 589828
  168.3 27.5 %collective-permute-start = (bf16[128,1536]{1,0:T(8,128)(2,1)}, bf16[128,1536]{1,0:T(8,128)(2,1)S(1)}, u32[]{:S(2)}, u32[]{:S(2)}) collective-permute-start(bf16[128,1536]{1,0:T(8,128)(2,1)} %get-tuple-element.44), channel_id=1, source_target_pairs={{0,4},{4,8},{8,12},{12,16},{16,20},{20,24},{24,28},{1,5},{5,9},{9,... | collective-permute-start | bytes 1179656 | tf_op jit(solution)/shard_map/ppermute | solution.py:28
  171.3 24.5 %collective-permute-start.1 = (bf16[128,1536]{1,0:T(8,128)(2,1)}, bf16[128,1536]{1,0:T(8,128)(2,1)}, u32[]{:S(2)}, u32[]{:S(2)}) collective-permute-start(bf16[128,1536]{1,0:T(8,128)(2,1)} %get-tuple-element.45), channel_id=1, source_target_pairs={{4,0},{8,4},{12,8},{16,12},{20,16},{24,20},{28,24},{5,1},{9,5},{13... | collective-permute-start | bytes 1179656 | tf_op jit(solution)/shard_map/ppermute | solution.py:30
  174.6 21.2 %copy-start.24 = (f32[12,32,256]{2,1,0:T(8,128)}, f32[12,32,256]{2,1,0:T(8,128)S(1)}, u32[]{:S(2)}) copy-start(f32[12,32,256]{2,1,0:T(8,128)S(1)} %fusion.23) | copy-start | bytes 1179652
  175.5 20.3 %slice-start.1 = ((bf16[256,2304]{1,0:T(8,128)(2,1)}), bf16[256,1536]{1,0:T(8,128)(2,1)S(1)}, s32[]{:S(2)}) async-start(bf16[256,2304]{1,0:T(8,128)(2,1)} %copy-done.10), calls=%async_computation.27 | async-start | bytes 1572864 | tf_op jit(solution)/shard_map/slice | solution.py:150
  176.5 19.3 %copy-start.40 = (bf16[32,768]{1,0:T(8,128)(2,1)}, bf16[32,768]{1,0:T(8,128)(2,1)S(1)}, u32[]{:S(2)}) copy-start(bf16[32,768]{1,0:T(8,128)(2,1)S(1)} %reshape.539) | copy-start | bytes 147460
  176.7 21.0 %copy-start.25 = (bf16[256,768]{0,1:T(8,128)(2,1)}, bf16[256,768]{0,1:T(8,128)(2,1)S(1)}, u32[]{:S(2)}) copy-start(bf16[256,768]{0,1:T(8,128)(2,1)S(1)} %copy.99) | copy-start | bytes 1179652
  202.2 47.2 %copy-start.65 = (f32[32,768]{1,0:T(8,128)S(1)}, f32[32,768]{1,0:T(8,128)}, u32[]{:S(2)}) copy-start(f32[32,768]{1,0:T(8,128)} %get-tuple-element.66) | copy-start | bytes 294916
  205.3 46.0 %copy-start.42 = (bf16[8,96,256]{2,1,0:T(8,128)(2,1)}, bf16[8,96,256]{2,1,0:T(8,128)(2,1)S(1)}, u32[]{:S(2)}) copy-start(bf16[8,96,256]{2,1,0:T(8,128)(2,1)S(1)} %convolution_convert_fusion.2) | copy-start | bytes 1179652
  205.3 46.0 %copy-start.66 = (f32[768]{0:T(1024)S(1)}, f32[768]{0:T(1024)}, u32[]{:S(2)}) copy-start(f32[768]{0:T(1024)} %get-tuple-element.25) | copy-start | bytes 9220
  205.3 46.0 %copy-start.69 = (bf16[32,8]{1,0:T(8,128)(2,1)S(1)}, bf16[32,8]{1,0:T(8,128)(2,1)}, u32[]{:S(2)}) copy-start(bf16[32,8]{1,0:T(8,128)(2,1)} %get-tuple-element.57) | copy-start | bytes 1540
  205.3 46.4 %copy-start.8 = (bf16[1,256,768]{2,1,0:T(8,128)(2,1)S(1)}, bf16[1,256,768]{2,1,0:T(8,128)(2,1)}, u32[]{:S(2)}) copy-start(bf16[1,256,768]{2,1,0:T(8,128)(2,1)} %param.15) | copy-start | bytes 1179652
  205.4 46.4 %copy-start.61 = (f32[32,8]{1,0:T(8,128)S(1)}, f32[32,8]{1,0:T(8,128)}, u32[]{:S(2)}) copy-start(f32[32,8]{1,0:T(8,128)} %copy-done.60) | copy-start | bytes 3076
  251.3 62.9 %copy-start.93 = (f32[256]{0:T(256)}, f32[256]{0:T(256)S(1)}, u32[]{:S(2)}) copy-start(f32[256]{0:T(256)S(1)} %get-tuple-element.68) | copy-start | bytes 3076
  251.3 62.9 %copy-start.74 = (f32[256]{0:T(256)}, f32[256]{0:T(256)S(1)}, u32[]{:S(2)}) copy-start(f32[256]{0:T(256)S(1)} %fusion.122) | copy-start | bytes 3076
  252.3 61.9 %copy-start.33 = (f32[32,768]{1,0:T(8,128)}, f32[32,768]{1,0:T(8,128)S(1)}, u32[]{:S(2)}) copy-start(f32[32,768]{1,0:T(8,128)S(1)} %get-tuple-element.21) | copy-start | bytes 294916
  252.5 294.2 %copy-start.79 = (f32[32]{0:T(128)}, f32[32]{0:T(128)S(1)}, u32[]{:S(2)}) copy-start(f32[32]{0:T(128)S(1)} %fusion.33) | copy-start | bytes 388
  576.3 179.1 %reduce-scatter.24.cloned.1.call-start = ((), (), s32[]{:S(2)}) async-start(), calls=%async_computation.23 | async-start | bytes 3244032 | tf_op jit(solution)/shard_map/reduce_scatter | solution.py:463
  579.8 296.2 %reduce-scatter.22.cloned.1.call-start = ((), (), s32[]{:S(2)}) async-start(), calls=%async_computation.22 | async-start | bytes 6488064 | tf_op jit(solution)/shard_map/reduce_scatter | solution.py:462
  585.0 394.9 %reduce-scatter.16.cloned.1.call-start = ((), (), s32[]{:S(2)}) async-start(), calls=%async_computation.19 | async-start | bytes 2433024 | tf_op jit(solution)/shard_map/reduce_scatter | solution.py:459
  587.9 496.8 %reduce-scatter.20.cloned.1.call-start = ((), (), s32[]{:S(2)}) async-start(), calls=%async_computation.21 | async-start | bytes 2433024 | tf_op jit(solution)/shard_map/reduce_scatter | solution.py:461
  600.6 608.5 %reduce-scatter.14.cloned.1.call-start = ((), (), s32[]{:S(2)}) async-start(), calls=%async_computation.18 | async-start | bytes 7299072 | tf_op jit(solution)/shard_map/reduce_scatter | solution.py:458
  607.2 22.5 %collective-permute-start.2 = (bf16[128,1536]{0,1:T(8,128)(2,1)S(1)}, bf16[128,1536]{0,1:T(8,128)(2,1)S(1)}, u32[]{:S(2)}, u32[]{:S(2)}) collective-permute-start(bf16[128,1536]{0,1:T(8,128)(2,1)S(1)} %get-tuple-element.38), channel_id=1, source_target_pairs={{0,4},{4,8},{8,12},{12,16},{16,20},{20,24},{24,28},{1,5},{5,9},{9,... | collective-permute-start | bytes 1179656 | tf_op jit(solution)/shard_map/ppermute | solution.py:40
  609.9 19.8 %collective-permute-start.3 = (bf16[128,1536]{0,1:T(8,128)(2,1)S(1)}, bf16[128,1536]{0,1:T(8,128)(2,1)S(1)}, u32[]{:S(2)}, u32[]{:S(2)}) collective-permute-start(bf16[128,1536]{0,1:T(8,128)(2,1)S(1)} %get-tuple-element.39), channel_id=1, source_target_pairs={{4,0},{8,4},{12,8},{16,12},{20,16},{24,20},{28,24},{5,1},{9,5},{13... | collective-permute-start | bytes 1179656 | tf_op jit(solution)/shard_map/ppermute | solution.py:40
  614.1 16.8 copy-start.49
  635.0 699.5 %reduce-scatter.18.cloned.1.call-start = ((), (), s32[]{:S(2)}) async-start(), calls=%async_computation.20 | async-start | bytes 7299072 | tf_op jit(solution)/shard_map/reduce_scatter | solution.py:460
  654.1 841.5 %reduce-scatter.28.cloned.1.call-start = ((), (), s32[]{:S(2)}) async-start(), calls=%async_computation.25 | async-start | bytes 12976128 | tf_op jit(solution)/shard_map/reduce_scatter | solution.py:465
  661.6 1086.9 %reduce-scatter.26.cloned.1.call-start = ((), (), s32[]{:S(2)}) async-start(), calls=%async_computation.24 | async-start | bytes 25952256 | tf_op jit(solution)/shard_map/reduce_scatter | solution.py:464
  679.3 45.7 %copy-start.78 = (f32[256]{0:T(256)S(1)}, f32[256]{0:T(256)}, u32[]{:S(2)}) copy-start(f32[256]{0:T(256)} %copy-done.77) | copy-start | bytes 3076
  (75 other events, 292.8 us)
Sparse Core Ops, SparseCore 0:
  10.9 60.7 all-gather.10
  74.7 59.0 all-gather.14
  136.7 56.7 all-gather.16
  196.3 53.0 all-gather.12
  252.1 57.9 all-gather.18
  312.8 53.8 all-gather.20
  369.6 95.2 all-gather.22
  467.8 68.4 all-gather.24
  576.4 71.5 reduce-scatter.11
  654.7 100.6 reduce-scatter.23
  762.5 113.4 reduce-scatter.21
  881.7 98.1 reduce-scatter.15
  986.6 98.0 reduce-scatter.19
  1090.8 118.2 reduce-scatter.13
  1216.2 118.2 reduce-scatter.17
  1340.9 154.6 reduce-scatter.27
  1503.6 244.8 reduce-scatter.25
where the time goes:
time: 1760 us
  waiting for transfers between devices  1420 us (81%)
  blocking collectives  138 us (8%)
  matrix products  122 us (7%)
  local copies, waits for them, and re-layouts  25.3 us (1%)
  other arithmetic  24 us (1%)
    reduce_scatter x1, waiting for transfers between devices, local(): lax.psum_scatter(ffn_sum[2], ('seq', 'batch'), scatter_dimension=0, tiled...  253 us
    reduce_scatter x1, waiting for transfers between devices, local(): lax.psum_scatter(ffn_sum[3], ('seq', 'batch'), scatter_dimension=0, tiled...  161 us
    reduce_scatter x1, waiting for transfers between devices, local(): lax.psum_scatter(grad_heavy_qkv, ('seq', 'batch'), scatter_dimension=0, t...  125 us
    reduce_scatter x1, waiting for transfers between devices, local(): lax.psum_scatter(grad_light_qkv, ('seq', 'batch'), scatter_dimension=0, t...  124 us
    reduce_scatter x1, waiting for transfers between devices, local(): lax.psum_scatter(ffn_sum[0], ('seq', 'batch'), scatter_dimension=0, tiled...  121 us
    reduce_scatter x1, waiting for transfers between devices, local(): lax.psum_scatter(grad_heavy_out, ('seq', 'batch'), scatter_dimension=0, t...  105 us
    reduce_scatter x1, waiting for transfers between devices, local(): lax.psum_scatter(grad_light_out, ('seq', 'batch'), scatter_dimension=0, t...  104 us
    all_gather x1, waiting for transfers between devices, local(): lax.all_gather(heavy_in, ('seq', 'batch'), axis=0, tiled=True)  93.5 us
  transfers between devices with their start and end apart: 21, of which 17 were waited for; matrix products, arithmetic and copies ran while one was open for 7% of the time, Pallas kernels for 0%

commit v1 on v0

v1 whole, which is shorter than its diff:
```python
import functools

import jax
import jax.numpy as jnp
import numpy as np
from jax import lax
from jax.experimental import pallas as pl
from jax.experimental.pallas import tpu as pltpu
from jax.sharding import PartitionSpec as P

HL = 8
DL = 96
HH = 12
DH = 64
WIN = 128
ROUTE = 8
SMALL = 128
CHUNK = 256
PARTS = 4
LANES = 256
EPS = 1e-06
BF = jnp.bfloat16
F32 = jnp.float32
BOTH = ("seq", "batch")
highest = lax.Precision.HIGHEST
VMEM_LIMIT = 60 * 1024 * 1024


def nn(left, right):
    return jnp.dot(left, right, preferred_element_type=F32)


def nt(left, right):
    return lax.dot_general(left, right, (((1,), (1,)), ((), ())), preferred_element_type=F32)


def tn(left, right):
    return lax.dot_general(left, right, (((0,), (0,)), ((), ())), preferred_element_type=F32)


def exact(left, right):
    return jnp.dot(left, right, precision=highest, preferred_element_type=F32)


def low(values):
    return values.astype(BF)


def row_sum(values):
    return jnp.sum(values, axis=-1, keepdims=True)


def rms_inverse(values):
    return lax.rsqrt(jnp.mean(values * values, axis=-1, keepdims=True) + EPS)


def rms_back(grad, values, inverse, gain):
    scaled = grad * gain
    inner = jnp.mean(scaled * values, axis=-1, keepdims=True)
    return inverse * scaled - values * (inverse * inverse * inverse * inner)


def geglu_parts(pair):
    half = pair.shape[-1] // 2
    u = pair[:, :half]
    up = pair[:, half:]
    c = 0.7978845608028654
    t = jnp.tanh(c * (u + 0.044715 * (u * u * u)))
    gelu = 0.5 * u * (1.0 + t)
    slope = 0.5 * (1.0 + t) + 0.5 * u * (1.0 - t * t) * (c * (1.0 + 3.0 * 0.044715 * (u * u)))
    return gelu, slope, up


def documents(positions, meta):
    found = (positions >= meta[0]).astype(jnp.int32)
    for i in range(1, 4):
        found = found + (positions >= meta[i]).astype(jnp.int32)
    return found


def head_rows(width, size):
    lanes = lax.broadcasted_iota(jnp.int32, (1, width), 1)
    inside = [(lanes >= i * size) & (lanes < (i + 1) * size) for i in range(width // size)]
    return [jnp.where(one, 1.0, 0.0) for one in inside]


def stack_heads(rows, masks):
    return jnp.concatenate([rows * low(mask) for mask in masks], axis=0)


def merge_heads(stacked, masks):
    count = stacked.shape[0] // len(masks)
    total = stacked[:count] * masks[0]
    for i in range(1, len(masks)):
        total = total + stacked[i * count : (i + 1) * count] * masks[i]
    return total


def softmax(scores):
    weights = jnp.exp(scores - jnp.max(scores, axis=-1, keepdims=True))
    return weights * (1.0 / row_sum(weights))


def light_bias(meta, block, tokens):
    query = meta[4] + block * WIN + lax.broadcasted_iota(jnp.int32, (WIN, 1), 0)
    key = meta[4] + (block - 1) * WIN + lax.broadcasted_iota(jnp.int32, (1, 3 * WIN), 1)
    key_doc = jnp.where((key >= 0) & (key < meta[5]), documents(key, meta), -1)
    seen = (jnp.abs(query - key) < WIN) & (documents(query, meta) == key_doc)
    return jnp.where(seen, 0.0, -1e30)


def heavy_bias(meta, count, keys):
    query = (meta[6] + lax.broadcasted_iota(jnp.int32, (count, 1), 0)) * ROUTE
    key = lax.broadcasted_iota(jnp.int32, (1, keys), 1) * ROUTE
    return jnp.where(documents(query, meta) == documents(key, meta), 0.0, -1e30)


def light_units(tokens):
    return [(block, part) for block in range(tokens // WIN) for part in range(2)]


def sigmoid_dot(rows, vector):
    return jax.nn.sigmoid(row_sum(rows * vector))


def load(full_ref, places, sems):
    copies = []
    for i, ((first, last), buffer) in enumerate(places):
        copies.append(pltpu.make_async_copy(full_ref.at[:, first:last], buffer, sems.at[i]))
        copies[-1].start()
    return copies


def two_lanes(column):
    lanes = lax.broadcasted_iota(jnp.int32, (column.shape[0], SMALL), 1)
    high = low(column).astype(F32)
    return low(jnp.where(lanes == 0, high, jnp.where(lanes == 1, column - high, 0.0)))


def from_two_lanes(block):
    lanes = lax.broadcasted_iota(jnp.int32, block.shape, 1)
    return row_sum(jnp.where(lanes < 2, block.astype(F32), 0.0))


def sum_blocks(ref, count):
    total = ref[0:count].astype(F32)
    for i in range(1, ref.shape[0] // count):
        total = total + ref[i * count : (i + 1) * count].astype(F32)
    return total


def heavy_forward(
    meta,
    xq_ref,
    xk_ref,
    wx_ref,
    out_ref,
    raw_ref,
    q_ref,
    kv_ref,
    mixed_ref,
    small_ref,
):
    count = xq_ref.shape[0]
    keys = xk_ref.shape[0]
    at = 0
    small = jnp.transpose(wx_ref[:, 3 * LANES :].astype(F32))[:8]
    small_ref[...] = small
    gain_1 = small[0:1]
    xq = xq_ref[...].astype(F32)
    q_norm = xq * rms_inverse(xq) * gain_1
    q_ref[...] = low(nn(low(q_norm), wx_ref[:, at : at + LANES]))
    size = min(CHUNK, keys)
    for start in range(0, keys, size):
        xk = xk_ref[start : start + size].astype(F32)
        k_norm = xk * rms_inverse(xk) * gain_1
        k_gate = sigmoid_dot(k_norm, small[3:4])
        raw = nn(low(k_norm), wx_ref[:, at + LANES : at + 3 * LANES])
        kv_ref[start : start + size, :LANES] = low(raw[:, :LANES])
        kv_ref[start : start + size, LANES:] = low(raw[:, LANES:] * k_gate)
    masks = head_rows(LANES, DH)[: HH // PARTS]
    bias = jnp.concatenate([heavy_bias(meta, count, keys)] * len(masks), axis=0)
    stacked = stack_heads(q_ref[...], masks)
    probs = softmax(nt(stacked, kv_ref[:, :LANES]) * DH ** (-0.5) + bias)
    mixed = low(merge_heads(nn(low(probs), kv_ref[:, LANES:]), masks))
    mixed_ref[...] = mixed
    raw_ref[...] = jnp.zeros_like(raw_ref)
    raw_ref[pl.ds(pl.multiple_of(meta[6], count), count)] = low(nn(mixed, out_ref[...]))


def light_forward(
    layout,
    meta,
    below_ref,
    x_ref,
    above_ref,
    xq_ref,
    raw_ref,
    pq_t_ref,
    pf_ref,
    small_ref,
    full_ref,
    q_ref,
    kv_ref,
    mixed_ref,
    heavy_raw_ref,
    middle_ref,
    normed2_ref,
    f_norm_ref,
    f_sent_ref,
    w_qkv,
    w_lo,
    sems,
):
    tokens, features = x_ref.shape
    routed = xq_ref.shape[0]
    copies = load(full_ref, [(layout["light_qkv"], w_qkv), (layout["light_out"], w_lo)], sems)
    small = small_ref[...]
    gain_1, gain_2 = small[0:1], small[1:2]
    xe = jnp.concatenate([below_ref[...], x_ref[...], above_ref[...]], axis=0).astype(F32)
    ne = low(xe * rms_inverse(xe) * gain_1)
    xq = xq_ref[...].astype(F32)
    q_gate = sigmoid_dot(xq * rms_inverse(xq) * gain_1, small[2:3])
    heavy_raw = sum_blocks(raw_ref, routed)
    heavy_raw_ref[...] = heavy_raw
    base = x_ref[...].astype(F32) + exact(pq_t_ref[...], heavy_raw * q_gate)
    copies[0].wait()
    q_ref[...] = low(nn(ne[WIN : WIN + tokens], w_qkv[:, :features]))
    kv_ref[...] = low(nn(ne, w_qkv[:, features:]))
    width = features // 2
    masks = head_rows(width, DL)
    scale = DL ** (-0.5)
    for block, part in light_units(tokens):
        cols = slice(part * width, (part + 1) * width)
        rows = slice(block * WIN, (block + 1) * WIN)
        key_rows = slice(block * WIN, (block + 3) * WIN)
        bias = jnp.concatenate([light_bias(meta, block, tokens)] * len(masks), axis=0)
        stacked = stack_heads(q_ref[rows, cols], masks)
        probs = softmax(nt(stacked, kv_ref[key_rows, cols]) * scale + bias)
        values = kv_ref[key_rows, features + part * width : features + (part + 1) * width]
        mixed_ref[rows, cols] = low(merge_heads(nn(low(probs), values), masks))
    copies[1].wait()
    middle = base + nn(mixed_ref[...], w_lo[...])
    middle_ref[...] = middle
    normed2 = middle * rms_inverse(middle) * gain_2
    normed2_ref[...] = low(normed2)
    f_norm = exact(pf_ref[...], normed2)
    f_norm_ref[...] = f_norm
    sent = jnp.concatenate([low(f_norm), two_lanes(sigmoid_dot(f_norm, small[4:5]))], axis=1)
    for i in range(f_sent_ref.shape[0] // routed):
        f_sent_ref[i * routed : (i + 1) * routed] = sent


def unpack_down(packed, down_ref, work_ref, devices):
    features = down_ref.shape[1]
    rows = packed.shape[0] // devices
    more = down_ref.shape[0] // devices - rows
    width = packed.shape[1] - features
    if rows % 8 == 0 and more % 8 == 0:
        work_ref[...] = packed.astype(F32)
        for i in range(devices):
            own = work_ref[i * rows : (i + 1) * rows, :features]
            parts = [
                work_ref[i * rows + j * more : i * rows + (j + 1) * more, features:]
                for j in range(rows // more)
            ]
            whole = jnp.concatenate([own, jnp.concatenate(parts, axis=1)], axis=0)
            down_ref[i * (rows + more) : (i + 1) * (rows + more)] = low(whole)
    else:
        for j in range(rows // more):
            cols = slice(j * width, (j + 1) * width)
            first, second = down_places(down_ref.shape[0], packed.shape[0], rows, more, j)
            down_ref[:, cols] = low(nn(first, packed[:, cols]) + nn(second, packed[:, features:]))


def down_places(units, packed_rows, rows, more, j):
    unit = lax.broadcasted_iota(jnp.int32, (units, packed_rows), 0)
    row = lax.broadcasted_iota(jnp.int32, (units, packed_rows), 1)
    total = rows + more
    device, inner = unit // total, unit % total
    first = (inner < rows) & (row == device * rows + inner)
    second = (inner >= rows) & (row == device * rows + j * more + inner - rows)
    return low(jnp.where(first, 1.0, 0.0)), low(jnp.where(second, 1.0, 0.0))


def pack_down(grad, out_ref, at, devices, rows):
    features = grad.shape[1]
    more = grad.shape[0] // devices - rows
    width = features * more // rows
    if rows % 8 == 0 and more % 8 == 0:
        pieces = []
        for i in range(devices):
            start = i * (rows + more)
            rest = grad[start + rows : start + rows + more]
            parts = [rest[:, j * width : (j + 1) * width] for j in range(rows // more)]
            pieces.append(
                jnp.concatenate([grad[start : start + rows], jnp.concatenate(parts, axis=0)], axis=1)
            )
        out_ref[:, at:] = low(jnp.concatenate(pieces, axis=0))
    else:
        total = None
        for j in range(rows // more):
            cols = slice(j * width, (j + 1) * width)
            first, second = down_places(grad.shape[0], devices * rows, rows, more, j)
            block = low(grad[:, cols])
            out_ref[:, at + j * width : at + (j + 1) * width] = low(tn(first, block))
            part = tn(second, block)
            total = part if total is None else total + part
        out_ref[:, at + features :] = low(total)


def light_ffn(
    layout,
    devices,
    normed2_ref,
    g_ref,
    order_ref,
    full_ref,
    ffn_ref,
    grad_ref,
    send_ref,
    keep_ref,
    w_in,
    w_packed,
    w_down,
    work_ref,
    pack_ref,
    sems,
):
    features = normed2_ref.shape[1]
    half = features // 2
    order = order_ref[...]
    copies = []
    for i, (name, buffer) in enumerate([("light_in", w_in), ("light_down", w_packed)]):
        first, last = layout[name]
        copy = pltpu.make_async_copy(full_ref.at[:, first:last], buffer, sems.at[i])
        copy.start()
        copies.append(copy)
    copies[0].wait()
    copies[1].wait()
    unpack_down(w_packed[...], w_down, work_ref, devices)
    gelu, slope, up = geglu_parts(nn(normed2_ref[...], w_in[...]))
    hidden = low(gelu * up)
    ffn_ref[...] = nn(hidden, w_down[...])
    grad_hidden = nt(g_ref[...], w_down[...])
    grad_pair = low(jnp.concatenate([grad_hidden * up * slope, grad_hidden * gelu], axis=1))
    grad_ref[...] = nt(grad_pair, w_in[...])
    wide = w_in.shape[1]
    left = low(nn(normed2_ref[...], order))
    for at in range(0, wide, 512):
        block = low(tn(left, grad_pair[:, at : at + 512]))
        send_ref[:, at : at + 512] = block[:half]
        keep_ref[:, at : at + 512] = block[half:]
    pack_down(tn(hidden, g_ref[...]), pack_ref, 0, devices, features // devices)
    block = low(tn(order, pack_ref[...]))
    send_ref[:, wide:] = block[:half]
    keep_ref[:, wide:] = block[half:]


def heavy_ffn(
    batch_n,
    sent_ref,
    t_ref,
    in_ref,
    down_ref,
    order_ref,
    order_units_ref,
    back_ref,
    ffn_ref,
    send_ref,
    keep_ref,
):
    features = in_ref.shape[0]
    hidden_n = down_ref.shape[0]
    w_in = in_ref[...]
    f_in = sent_ref[:, :features]
    gate = from_two_lanes(sent_ref[:, features:])
    t = t_ref[...].astype(F32)
    grad_ffn = low(t * gate)
    gelu, slope, up = geglu_parts(nn(f_in, w_in))
    hidden = low(gelu * up)
    ffn = nn(hidden, down_ref[...])
    ffn_ref[...] = low(ffn)
    grad_hidden = nt(grad_ffn, down_ref[...])
    grad_pair = low(jnp.concatenate([grad_hidden * up * slope, grad_hidden * gelu], axis=1))
    back_ref[:, :features] = low(nt(grad_pair, w_in))
    back_ref[:, features:] = two_lanes(row_sum(t * ffn))
    grad_in = low(tn(low(nn(f_in, order_ref[...])), grad_pair))
    grad_down = low(tn(low(nn(hidden, order_units_ref[...])), grad_ffn))
    put_blocks(send_ref, keep_ref, batch_n, grad_in, grad_down)


def put_blocks(send_ref, keep_ref, batch_n, upper, lower):
    upper_rows = upper.shape[0] // batch_n
    lower_rows = lower.shape[0] // batch_n
    total = upper_rows + lower_rows
    width = send_ref.shape[1]
    for i in range(batch_n):
        ref = send_ref if i < batch_n // 2 else keep_ref
        start = i % (batch_n // 2) * total
        places = [(start, upper_rows, upper), (start + upper_rows, lower_rows, lower)]
        for first, count, values in places:
            ref[first : first + count, : values.shape[1]] = values[i * count : (i + 1) * count]
            if values.shape[1] < width:
                ref[first : first + count, values.shape[1] :] = jnp.zeros(
                    (count, width - values.shape[1]), BF
                )


def light_backward(
    layout,
    meta,
    below_ref,
    x_ref,
    above_ref,
    xq_ref,
    pq_ref,
    pq_t_ref,
    pf_t_ref,
    g_ref,
    order_ref,
    q_ref,
    kv_ref,
    mixed_ref,
    heavy_raw_ref,
    middle_ref,
    f_norm_ref,
    small_ref,
    grad_n2_ref,
    back_ref,
    full_ref,
    grad_middle_ref,
    grad_normed_ref,
    halo_below_ref,
    halo_above_ref,
    grad_raw_ref,
    small_grad_ref,
    send_ref,
    keep_ref,
    w_qkv,
    w_lo,
    dq_ref,
    dkv_ref,
    stage,
    sems,
    out_sems,
):
    tokens, features = x_ref.shape
    routed = xq_ref.shape[0]
    half = features // 2
    copies = load(full_ref, [(layout["light_out"], w_lo), (layout["light_qkv"], w_qkv)], sems)
    small = small_ref[...]
    gain_1, gain_2 = small[0:1], small[1:2]
    started = []

    def put(at, grad):
        width = grad.shape[1]
        slot = len(started) % stage.shape[0]
        if len(started) >= stage.shape[0]:
            for copy in started[-stage.shape[0]]:
                copy.wait()
        stage[slot, :, :width] = low(grad)
        both = []
        for i, ref in enumerate((send_ref, keep_ref)):
            source = stage.at[slot, i * half : (i + 1) * half, :width]
            both.append(
                pltpu.make_async_copy(source, ref.at[:, at : at + width], out_sems.at[slot, i])
            )
            both[-1].start()
        started.append(both)

    sums = sum_blocks(back_ref, routed)
    f_norm = f_norm_ref[...]
    f_gate = sigmoid_dot(f_norm, small[4:5])
    f_logit = (sums[:, features : features + 1] + sums[:, features + 1 : features + 2]) * (
        f_gate * (1.0 - f_gate)
    )
    router_f = jnp.sum(f_norm * f_logit, axis=0, keepdims=True)
    f_back = sums[:, :features] + f_logit * small[4:5]
    middle = middle_ref[...]
    grad_n2 = grad_n2_ref[...] + exact(pf_t_ref[...], f_back)
    inverse_2 = rms_inverse(middle)
    gain_2_grad = jnp.sum(grad_n2 * (middle * inverse_2), axis=0, keepdims=True)
    grad_middle = g_ref[...].astype(F32) + rms_back(grad_n2, middle, inverse_2, gain_2)
    grad_middle_ref[...] = grad_middle
    middle_low = low(grad_middle)

    q_rows = exact(pq_ref[...], grad_middle)
    xq = xq_ref[...].astype(F32)
    q_plain = xq * rms_inverse(xq)
    q_norm = q_plain * gain_1
    q_gate = sigmoid_dot(q_norm, small[2:3])
    grad_raw = low(q_rows * q_gate)
    for i in range(grad_raw_ref.shape[0] // routed):
        grad_raw_ref[i * routed : (i + 1) * routed] = grad_raw
    q_logit = row_sum(q_rows * heavy_raw_ref[...]) * q_gate * (1.0 - q_gate)
    q_back = q_logit * small[2:3]
    router_q = jnp.sum(q_norm * q_logit, axis=0, keepdims=True)
    gain_1_grad = jnp.sum(q_back * q_plain, axis=0, keepdims=True)

    copies[0].wait()
    order = order_ref[...]
    put(3 * features, tn(low(nn(mixed_ref[...], order)), middle_low))
    do = low(nt(middle_low, w_lo[...]))
    width = features // 2
    masks = head_rows(width, DL)
    scale = DL ** (-0.5)
    dkv_ref[...] = jnp.zeros_like(dkv_ref)
    for block, part in light_units(tokens):
        cols = slice(part * width, (part + 1) * width)
        value_cols = slice(features + part * width, features + (part + 1) * width)
        rows = slice(block * WIN, (block + 1) * WIN)
        key_rows = slice(block * WIN, (block + 3) * WIN)
        bias = jnp.concatenate([light_bias(meta, block, tokens)] * len(masks), axis=0)
        stacked = stack_heads(q_ref[rows, cols], masks)
        do_stacked = stack_heads(do[rows, cols], masks)
        key = kv_ref[key_rows, cols]
        probs = softmax(nt(stacked, key) * scale + bias)
        grad_probs = nt(do_stacked, kv_ref[key_rows, value_cols])
        ds = low(probs * (grad_probs - row_sum(probs * grad_probs)))
        dq_ref[rows, cols] = low(merge_heads(nn(ds, key), masks) * scale)
        dkv_ref[key_rows, cols] += tn(ds, stacked) * scale
        dkv_ref[key_rows, value_cols] += tn(low(probs), do_stacked)

    copies[1].wait()
    xe = jnp.concatenate([below_ref[...], x_ref[...], above_ref[...]], axis=0).astype(F32)
    plain = xe * rms_inverse(xe)
    left = low(nn(low(plain * gain_1), order))
    dk = low(dkv_ref[:, :features])
    dv = low(dkv_ref[:, features:])
    inner = slice(WIN, WIN + tokens)
    put(0, tn(left[inner], dq_ref[...]))
    put(features, tn(left, dk))
    put(2 * features, tn(left, dv))
    back = nt(dk, w_qkv[:, features : 2 * features]) + nt(dv, w_qkv[:, 2 * features :])
    own = back[inner] + nt(dq_ref[...], w_qkv[:, :features])
    halo_below_ref[...] = low(back[:WIN])
    halo_above_ref[...] = low(back[WIN + tokens :])
    gain_1_grad = gain_1_grad + jnp.sum(own * plain[inner], axis=0, keepdims=True)
    gain_1_grad = gain_1_grad + jnp.sum(back[:WIN] * plain[:WIN], axis=0, keepdims=True)
    gain_1_grad = gain_1_grad + jnp.sum(
        back[WIN + tokens :] * plain[WIN + tokens :], axis=0, keepdims=True
    )
    grad_normed_ref[...] = own + exact(pq_t_ref[...], q_back)
    rest = jnp.zeros((4, features), F32)
    small_grad_ref[...] = jnp.concatenate(
        [gain_1_grad, gain_2_grad, router_q, router_f, rest], axis=0
    )
    for both in started[-stage.shape[0] :]:
        for copy in both:
            copy.wait()


def heavy_backward(
    batch_n,
    meta,
    xq_ref,
    xk_ref,
    grad_raw_ref,
    q_ref,
    kv_ref,
    mixed_ref,
    small_ref,
    small_grad_ref,
    wx_ref,
    out_ref,
    order_ref,
    order_out_ref,
    backs_ref,
    send_ref,
    keep_ref,
):
    at = 0
    count = xq_ref.shape[0]
    keys = xk_ref.shape[0]
    features = wx_ref.shape[0]
    small = small_ref[...]
    gain_1 = small[0:1]
    place = pl.ds(pl.multiple_of(meta[6], count), count)
    grad_raw = grad_raw_ref[place]
    do = low(nt(grad_raw, out_ref[...]))
    masks = head_rows(LANES, DH)[: HH // PARTS]
    scale = DH ** (-0.5)
    bias = jnp.concatenate([heavy_bias(meta, count, keys)] * len(masks), axis=0)
    stacked = stack_heads(q_ref[...], masks)
    do_stacked = stack_heads(do, masks)
    probs = softmax(nt(stacked, kv_ref[:, :LANES]) * scale + bias)
    grad_probs = nt(do_stacked, kv_ref[:, LANES:])
    ds = low(probs * (grad_probs - row_sum(probs * grad_probs)))
    probs = low(probs)
    dq = low(merge_heads(nn(ds, kv_ref[:, :LANES]), masks) * scale)
    q_back = nt(dq, wx_ref[:, at : at + LANES])
    backs_ref[:, :features] = jnp.zeros((keys, features), BF)
    backs_ref[place, :features] = low(q_back)
    xq = xq_ref[...].astype(F32)
    q_plain = xq * rms_inverse(xq)
    order = order_ref[...]
    gain_1_grad = jnp.sum(q_back * q_plain, axis=0, keepdims=True)
    q_grads = tn(low(nn(low(q_plain * gain_1), order)), dq)
    router_k = None
    size = min(CHUNK, keys)
    for start in range(0, keys, size):
        rows = slice(start, start + size)
        xk = xk_ref[rows].astype(F32)
        k_plain = xk * rms_inverse(xk)
        k_norm = k_plain * gain_1
        k_low = low(k_norm)
        k_gate = sigmoid_dot(k_norm, small[3:4])
        dk = tn(ds[:, rows], stacked) * scale
        dv = tn(probs[:, rows], do_stacked)
        raw = nn(k_low, wx_ref[:, at + 2 * LANES : at + 3 * LANES])
        k_logit = row_sum(dv * raw) * k_gate * (1.0 - k_gate)
        grad_raw_k = low(jnp.concatenate([dk, dv * k_gate], axis=1))
        k_back = nt(grad_raw_k, wx_ref[:, at + LANES : at + 3 * LANES]) + k_logit * small[3:4]
        backs_ref[rows, features:] = low(k_back)
        one_router = jnp.sum(k_norm * k_logit, axis=0, keepdims=True)
        gain_1_grad = gain_1_grad + jnp.sum(k_back * k_plain, axis=0, keepdims=True)
        one_grads = tn(low(nn(k_low, order)), grad_raw_k)
        router_k = one_router if router_k is None else router_k + one_router
        kv_grads = one_grads if start == 0 else kv_grads + one_grads
    out_grads = low(tn(low(nn(mixed_ref[...], order_out_ref[...])), grad_raw))
    start_grads = small_grad_ref[...]
    vectors = [start_grads[0:1] + gain_1_grad, start_grads[1:2], start_grads[2:3], router_k]
    vectors += [start_grads[3:4], jnp.zeros((SMALL - 5, features), F32)]
    vectors = low(jnp.concatenate(vectors, axis=0))
    small_cols = low(jnp.transpose(nn(vectors, order)))
    upper = jnp.concatenate([low(q_grads), low(kv_grads), small_cols], axis=1)
    put_blocks(send_ref, keep_ref, batch_n, upper, out_grads[: HH * DH // PARTS])


def finish(
    x_ref,
    small_ref,
    grad_middle_ref,
    grad_normed_ref,
    from_below_ref,
    from_above_ref,
    backs_ref,
    pq_t_ref,
    pk_t_ref,
    pf_t_ref,
    middle_ref,
    light_ref,
    f_norm_ref,
    ffn_ref,
    output_ref,
    input_grad_ref,
):
    tokens, features = x_ref.shape
    routed = f_norm_ref.shape[0]
    small = small_ref[...]
    gate = sigmoid_dot(f_norm_ref[...], small[4:5])
    heavy = exact(pf_t_ref[...], sum_blocks(ffn_ref, routed) * gate)
    output_ref[...] = low(middle_ref[...] + light_ref[...] + heavy)
    backs = sum_blocks(backs_ref, routed)
    grad = grad_normed_ref[...] + exact(pq_t_ref[...], backs[:, :features])
    grad = grad + exact(pk_t_ref[...], backs[:, features:])
    below = from_below_ref[...].astype(F32)
    above = from_above_ref[...].astype(F32)
    grad = grad + jnp.concatenate([below, above], axis=0)
    x = x_ref[...].astype(F32)
    input_grad_ref[...] = grad_middle_ref[...] + rms_back(grad, x, rms_inverse(x), small[0:1])


def pair_sum(keep_ref, got_ref, send_out_ref, keep_out_ref):
    count = send_out_ref.shape[0]
    total = keep_ref[...].astype(F32) + got_ref[...].astype(F32)
    send_out_ref[...] = low(total[:count])
    keep_out_ref[...] = low(total[count:])


def sum_leading(ref, cols):
    total = ref[0, :, cols].astype(F32)
    for i in range(1, ref.shape[0]):
        total = total + ref[i, :, cols].astype(F32)
    return total


def pack_blocks(*refs):
    out = refs[-1]
    at = 0
    for ref in refs[:-1]:
        out[:, at : at + ref.shape[1]] = ref[...]
        at += ref.shape[1]


def call(kernel, args, memory, outs, scratch, flops, name, far=0):
    spaces = {"v": pltpu.VMEM, "s": pltpu.SMEM, "h": pl.ANY}
    return pl.pallas_call(
        kernel,
        out_shape=[jax.ShapeDtypeStruct(shape, kind) for shape, kind in outs],
        in_specs=[pl.BlockSpec(memory_space=spaces[one]) for one in memory],
        out_specs=[pl.BlockSpec(memory_space=pltpu.VMEM)] * (len(outs) - far)
        + [pl.BlockSpec(memory_space=pl.ANY)] * far,
        scratch_shapes=scratch,
        compiler_params=pltpu.CompilerParams(vmem_limit_bytes=VMEM_LIMIT),
        cost_estimate=pl.CostEstimate(flops=flops, bytes_accessed=20_000_000, transcendentals=0),
        name=name,
    )(*args)


def select_rows(rows, mask):
    blocks = rows.astype(F32).reshape(mask.shape[0], ROUTE, rows.shape[1])
    return jnp.sum(jnp.where(mask[:, :, None], blocks, 0.0), axis=1)


def shifted(block, axis, distance):
    devices = range(lax.axis_size(axis))
    route = [(i - distance, i) for i in devices if i - distance in devices]
    return lax.ppermute(block, axis, route)


def swapped(block, distance):
    return lax.ppermute(block, "batch", [(i, i ^ distance) for i in range(lax.axis_size("batch"))])


def exchange(blocks, axis):
    return lax.all_to_all(blocks, axis, 0, 0, tiled=True)


def spread_to_all(block, axis):
    count = lax.axis_size(axis)
    return exchange(jnp.broadcast_to(block[None], (count,) + block.shape), axis)


def presum(blocks):
    if blocks.shape[0] > 16:
        return jnp.sum(blocks.astype(F32), axis=0)
    return blocks.reshape(-1, blocks.shape[2])


def summed(blocks, axis):
    return jnp.sum(exchange(blocks, axis).astype(F32), axis=0)


def pack_rows(down, rows):
    width = down.shape[1] * (down.shape[0] - rows) // rows
    rest = down[rows:]
    pieces = [rest[:, i : i + width] for i in range(0, down.shape[1], width)]
    return jnp.concatenate([down[:rows], jnp.concatenate(pieces, axis=0)], axis=1)


def halves_summed(keep, got, height, width):
    count = height // 2
    steps = width // 128
    block = 128 * max(i for i in range(1, 7) if steps % i == 0)
    rows_in = pl.BlockSpec((height, block), lambda i: (0, i))
    rows_out = pl.BlockSpec((count, block), lambda i: (0, i))
    return pl.pallas_call(
        pair_sum,
        grid=(width // block,),
        out_shape=[jax.ShapeDtypeStruct((count, width), BF)] * 2,
        in_specs=[rows_in] * 2,
        out_specs=[rows_out] * 2,
        compiler_params=pltpu.CompilerParams(vmem_limit_bytes=VMEM_LIMIT),
        cost_estimate=pl.CostEstimate(
            flops=height * width, bytes_accessed=6 * height * width, transcendentals=0
        ),
        name="pair_sum",
    )(keep, got)


def batch_summed(send, keep):
    height, width = keep.shape
    send, keep = halves_summed(keep, swapped(send, 1), height, width)
    return low(keep.astype(F32) + swapped(send, 2).astype(F32))


def canonical(piece, core, pair):
    other = swapped(piece, 2)
    piece = jnp.where(pair == 0, jnp.stack([piece, other]), jnp.stack([other, piece]))
    other = swapped(piece, 1)
    piece = jnp.where(core == 0, jnp.stack([piece, other], 1), jnp.stack([other, piece], 1))
    return piece.reshape((4,) + piece.shape[2:])


def unpack_rows(packed, features):
    rows = packed.shape[0]
    width = packed.shape[1] - features
    count = features // width
    rest = packed[:, features:].reshape(count, rows // count, width)
    rest = jnp.concatenate([rest[i] for i in range(count)], axis=1)
    return jnp.concatenate([packed[:, :features], rest], axis=0)


def pad_cols(block, width):
    return jnp.pad(block, ((0, 0), (0, width - block.shape[1])))


def order_matrix(order):
    size = order.shape[0]
    return low((lax.broadcasted_iota(jnp.int32, (size, size), 0) == order[None, :]).astype(F32))


def other_first(index, axis, own):
    flipped = np.flip(index, axis)
    return jnp.where(own == 0, jnp.asarray(flipped), jnp.asarray(index))


def local(
    layer_input,
    cotangent,
    doc_lengths,
    routes,
    norm_gains,
    router,
    light_qkv,
    light_out,
    heavy_qkv,
    heavy_out,
    light_in,
    light_down,
    heavy_in,
    heavy_down,
):
    seq_n = lax.axis_size("seq")
    batch_n = lax.axis_size("batch")
    devices = seq_n * batch_n
    rows = light_qkv.shape[0]
    x = layer_input[0]
    g = cotangent[0]
    tokens, features = x.shape
    routed = tokens // ROUTE
    keys = routed * seq_n
    wide = light_qkv.shape[1]
    seq = lax.axis_index("seq")
    own = lax.axis_index("batch")
    core, pair = own % 2, own // 2
    offset = seq * tokens

    small = pad_cols(jnp.concatenate([norm_gains, router], axis=1), SMALL)
    sources = [
        ("light_qkv", light_qkv),
        ("light_out", light_out),
        ("light_in", light_in),
        ("light_down", pack_rows(light_down, rows)),
    ]
    layout = {}
    at = 0
    for name, block in sources:
        layout[name] = (at, at + block.shape[1])
        at += block.shape[1]
    packed = call(
        pack_blocks,
        [block for _, block in sources],
        "v" * len(sources),
        [((rows, at), BF)],
        [],
        1_000_000,
        "pack",
    )[0]
    full = lax.all_gather(packed, BOTH, axis=0, tiled=True)

    masks = [
        lax.broadcasted_iota(jnp.int32, (routed, ROUTE), 1) == routes[i, 0][:, None]
        for i in range(3)
    ]
    xq = low(select_rows(x, masks[0]))
    xk = low(select_rows(x, masks[1]))
    t = low(select_rows(g, masks[2]))
    query_parts = seq_n // PARTS
    count = keys // query_parts
    part = seq // query_parts
    query_first = (seq % query_parts) * count
    head_width = features // PARTS
    head_all = 3 * LANES + SMALL
    hidden = heavy_in.shape[1] // 2 // seq_n
    in_rows = features // batch_n
    every = lambda block: jnp.broadcast_to(block[None], (seq_n,) + block.shape)
    tall = lambda blocks: jnp.pad(blocks, ((0, 0), (0, routed - rows), (0, 0)))
    head_cols = heavy_qkv.reshape(rows, 3, PARTS, head_width)
    head_cols = jnp.pad(head_cols, ((0, 0), (0, 0), (0, 0), (0, LANES - head_width)))
    head_cols = head_cols.transpose(2, 0, 1, 3).reshape(PARTS, rows, 3 * LANES)
    head_cols = jnp.repeat(head_cols, query_parts, axis=0)
    head_cols = jnp.concatenate([head_cols, every(small)], axis=2)
    sent = jnp.concatenate([every(jnp.concatenate([xq, xk], axis=1)), tall(head_cols)], axis=2)
    travel = exchange(sent, "seq")
    in_cols = heavy_in.reshape(rows, 2, seq_n, hidden).transpose(2, 0, 1, 3)
    in_cols = in_cols.reshape(seq_n, rows, 2 * hidden)
    late = exchange(jnp.concatenate([every(t), tall(in_cols)], axis=2), "seq")
    if query_parts == 2:
        other = lax.ppermute(heavy_out, "seq", [(i, i ^ 1) for i in range(seq_n)])
        out_rows = jnp.where(
            seq % 2 == 0, jnp.stack([heavy_out, other]), jnp.stack([other, heavy_out])
        )
    else:
        groups = [list(range(i, i + query_parts)) for i in range(0, seq_n, query_parts)]
        out_rows = jnp.broadcast_to(heavy_out[None], (query_parts,) + heavy_out.shape)
        out_rows = lax.all_to_all(out_rows, "seq", 0, 0, tiled=True, axis_index_groups=groups)
    out_count = query_parts * rows
    out_rows = pad_cols(out_rows.reshape(out_count, features), head_all)
    piece = travel[:, :rows, 2 * features :].reshape(in_rows, head_all)
    piece = canonical(jnp.concatenate([piece, out_rows], axis=0), core, pair)
    index = np.arange(features).reshape(seq_n, 2, 2, rows)
    order_h = order_matrix(jnp.asarray(index.transpose(1, 2, 0, 3).reshape(-1)))
    wx = low(nn(order_h, piece[:, :in_rows].reshape(features, head_all)))
    h_out = piece[:, in_rows:, :features].reshape(batch_n, query_parts, rows, features)
    h_out = h_out.transpose(1, 0, 2, 3).reshape(head_width, features)
    h_out = jnp.pad(h_out, ((0, LANES - head_width), (0, 0)))
    pack_width = max(2 * hidden, features)
    piece = late[:, :rows, features:].reshape(in_rows, 2 * hidden)
    piece = [pad_cols(piece, pack_width), pad_cols(heavy_down, pack_width)]
    piece = canonical(jnp.concatenate(piece, axis=0), core, pair)
    h_in = low(nn(order_h, piece[:, :in_rows, : 2 * hidden].reshape(features, 2 * hidden)))
    h_down = piece[:, in_rows:, :features].reshape(hidden, features)
    t_all = late[:, :, :features].reshape(keys, features)
    below = shifted(x[tokens - WIN :], "seq", 1)
    above = shifted(x[:WIN], "seq", -1)

    def relative(array):
        array = jnp.where(core == 0, np.flip(array, 0), array)
        return jnp.where(pair == 0, jnp.flip(array, 1), array).reshape(-1)

    order = order_matrix(relative(index.transpose(2, 1, 0, 3)))
    units = np.arange(hidden).reshape(2, 2, -1)
    order_units = order_matrix(relative(units.transpose(1, 0, 2)))
    out_index = np.arange(head_width).reshape(query_parts, 2, 2, rows)
    out_index = relative(out_index.transpose(2, 1, 0, 3))
    rest = jnp.arange(head_width, LANES, dtype=out_index.dtype)
    order_out = order_matrix(jnp.concatenate([out_index, rest]))
    ends = jnp.cumsum(doc_lengths[0])
    meta = jnp.stack([ends[0], ends[1], ends[2], ends[3], offset, tokens * seq_n, query_first])
    meta = meta.astype(jnp.int32)
    place = lax.broadcasted_iota(jnp.int32, (routed, tokens), 1)
    first = lax.broadcasted_iota(jnp.int32, (routed, tokens), 0) * ROUTE
    picks = [(place == first + routes[i, 0][:, None]).astype(F32) for i in range(3)]
    place_t = lax.broadcasted_iota(jnp.int32, (tokens, routed), 0)
    first_t = lax.broadcasted_iota(jnp.int32, (tokens, routed), 1) * ROUTE
    picks_t = [(place_t == first_t + routes[i, 0][None, :]).astype(F32) for i in range(3)]

    xq_all = travel[:, :, :features].reshape(keys, features)
    xq_part = lax.dynamic_slice_in_dim(xq_all, query_first, count, 0)
    xk_all = travel[:, :, features : 2 * features].reshape(keys, features)
    raw, heavy_q, heavy_kv, heavy_mixed, small_rows = call(
        heavy_forward,
        (meta, xq_part, xk_all, wx, h_out),
        "svvvv",
        [
            ((keys, features), BF),
            ((count, LANES), BF),
            ((keys, 2 * LANES), BF),
            ((count, LANES), BF),
            ((8, features), F32),
        ],
        [],
        2_000_000_000,
        "heavy_forward",
    )
    raw = presum(exchange(raw.reshape(seq_n, routed, features), "seq"))

    weight = lambda columns: pltpu.VMEM((features, columns), BF)
    q, kv, mixed, heavy_raw, middle, normed2, f_norm, f_sent = call(
        functools.partial(light_forward, layout),
        (meta, below, x, above, xq, raw, picks_t[0], picks[2], small_rows, full),
        "svvvvvvvvh",
        [
            ((tokens, features), BF),
            ((tokens + 2 * WIN, 2 * features), BF),
            ((tokens, features), BF),
            ((routed, features), F32),
            ((tokens, features), F32),
            ((tokens, features), BF),
            ((routed, features), F32),
            ((keys, features + SMALL), BF),
        ],
        [weight(wide), weight(features), pltpu.SemaphoreType.DMA((2,))],
        8_000_000_000,
        "light_forward",
    )
    f_sent = exchange(f_sent.reshape(seq_n, routed, features + SMALL), "seq")
    light_hidden = light_in.shape[1] // 2
    down_width = layout["light_down"][1] - layout["light_down"][0]
    half = features // 2
    ffn_width = light_in.shape[1] + down_width
    ffn, grad_n2, light_send, light_keep = call(
        functools.partial(light_ffn, layout, devices),
        (normed2, g, order, full),
        "vvvh",
        [
            ((tokens, features), F32),
            ((tokens, features), F32),
            ((half, ffn_width), BF),
            ((half, ffn_width), BF),
        ],
        [
            weight(light_in.shape[1]),
            weight(down_width),
            pltpu.VMEM((light_hidden, features), BF),
            pltpu.VMEM((features, down_width), F32),
            weight(down_width),
            pltpu.SemaphoreType.DMA((2,)),
        ],
        8_000_000_000,
        "light_ffn",
    )
    down_rows = hidden // batch_n
    back, ffn_part, ffn_send, ffn_keep = call(
        functools.partial(heavy_ffn, batch_n),
        (f_sent.reshape(keys, features + SMALL), t_all, h_in, h_down, order, order_units),
        "vvvvvv",
        [
            ((keys, features + SMALL), BF),
            ((keys, features), BF),
            ((batch_n // 2 * (in_rows + down_rows), pack_width), BF),
            ((batch_n // 2 * (in_rows + down_rows), pack_width), BF),
        ],
        [],
        4_000_000_000,
        "heavy_ffn",
    )
    back = presum(exchange(back.reshape(seq_n, routed, features + SMALL), "seq"))

    ffn_total = batch_summed(ffn_send, ffn_keep)
    light_total = batch_summed(light_send, light_keep)
    ffn_rows = ffn_total[:in_rows, : 2 * hidden].reshape(seq_n, rows, 2 * hidden)
    light_rows = light_total.reshape(seq_n, rows, ffn_width)
    ffn_rows = exchange(jnp.concatenate([light_rows, ffn_rows], axis=2), "seq").astype(F32)
    grad_h_down = ffn_total[in_rows:, :features].astype(F32)
    grad_h_in = ffn_rows[:, :, ffn_width:].reshape(seq_n, rows, 2, hidden).transpose(1, 2, 0, 3)
    grad_h_in = grad_h_in.reshape(rows, 2 * hidden * seq_n)
    shard_f = jnp.sum(ffn_rows[:, :, :ffn_width], axis=0)

    (
        grad_middle,
        grad_normed,
        halo_below,
        halo_above,
        grad_raw,
        small_grad,
        light_send,
        light_keep,
    ) = call(
        functools.partial(light_backward, layout),
        (
            meta,
            below,
            x,
            above,
            xq,
            picks[0],
            picks_t[0],
            picks_t[2],
            g,
            order,
            q,
            kv,
            mixed,
            heavy_raw,
            middle,
            f_norm,
            small_rows,
            grad_n2,
            back,
            full,
        ),
        "s" + "v" * 18 + "h",
        [
            ((tokens, features), F32),
            ((tokens, features), F32),
            ((WIN, features), BF),
            ((WIN, features), BF),
            ((keys, features), BF),
            ((8, features), F32),
            ((half, wide + features), BF),
            ((half, wide + features), BF),
        ],
        [
            weight(wide),
            weight(features),
            pltpu.VMEM((tokens, features), BF),
            pltpu.VMEM((tokens + 2 * WIN, 2 * features), F32),
            pltpu.VMEM((3, features, features), BF),
            pltpu.SemaphoreType.DMA((2,)),
            pltpu.SemaphoreType.DMA((3, 2)),
        ],
        16_000_000_000,
        "light_backward",
        2,
    )

    light_total = batch_summed(light_send, light_keep)

    both = jnp.concatenate([grad_raw, ffn_part], axis=1).reshape(seq_n, routed, 2 * features)
    both = exchange(both, "seq")
    grad_raw = both[:, :, :features].reshape(keys, features)
    ffn_part = presum(both[:, :, features:])
    head_rows_n = head_width // batch_n
    backs, head_send, head_keep = call(
        functools.partial(heavy_backward, batch_n),
        (
            meta,
            xq_part,
            xk_all,
            grad_raw,
            heavy_q,
            heavy_kv,
            heavy_mixed,
            small_rows,
            small_grad,
            wx,
            h_out,
            order,
            order_out,
        ),
        "s" + "v" * 12,
        [
            ((keys, 2 * features), BF),
            ((batch_n // 2 * (in_rows + head_rows_n), head_all), BF),
            ((batch_n // 2 * (in_rows + head_rows_n), head_all), BF),
        ],
        [],
        4_000_000_000,
        "heavy_backward",
    )
    backs = presum(exchange(backs.reshape(seq_n, routed, 2 * features), "seq"))

    head_total = batch_summed(head_send, head_keep)
    out_grads = head_total[in_rows:, :features].reshape(query_parts, rows, features)
    out_grads = lax.dynamic_update_slice(
        jnp.zeros((seq_n, rows, features), BF), out_grads, (part * query_parts, 0, 0)
    )
    light_width = wide + features
    total = jnp.concatenate(
        [
            light_total.reshape(seq_n, rows, light_width),
            head_total[:in_rows].reshape(seq_n, rows, head_all),
            out_grads,
        ],
        axis=2,
    )
    total = exchange(total, "seq").astype(F32)
    grad_light = jnp.sum(total[:, :, :light_width], axis=0)
    head_grads = total[:, :, light_width:]
    grad_heavy_out = jnp.sum(head_grads[:, :, head_all:], axis=0)
    grad_small = jnp.sum(head_grads[:, :, 3 * LANES : head_all], axis=0)
    grad_heads = head_grads[:, :, : 3 * LANES].reshape(PARTS, query_parts, rows, 3, LANES)
    grad_heads = jnp.sum(grad_heads, axis=1)[:, :, :, :head_width]
    grad_heads = grad_heads.transpose(1, 2, 0, 3).reshape(rows, wide)

    from_above = shifted(halo_below, "seq", -1)
    from_below = shifted(halo_above, "seq", 1)
    output, input_grad = call(
        finish,
        (
            x,
            small_rows,
            grad_middle,
            grad_normed,
            from_below,
            from_above,
            backs,
            picks_t[0],
            picks_t[1],
            picks_t[2],
            middle,
            ffn,
            f_norm,
            ffn_part,
        ),
        "v" * 14,
        [((tokens, features), BF), ((tokens, features), F32)],
        [],
        1_000_000_000,
        "finish",
    )
    return (
        output[None],
        input_grad[None],
        grad_small[:, :2],
        grad_small[:, 2:5],
        grad_light[:, :wide],
        grad_light[:, wide:],
        grad_heads,
        grad_heavy_out,
        shard_f[:, : light_in.shape[1]],
        unpack_rows(shard_f[:, light_in.shape[1] :], features),
        grad_h_in,
        grad_h_down,
    )


def solution(mesh):
    weight = P(BOTH, None)
    rows = P("batch", "seq", None)
    return jax.shard_map(
        local,
        mesh=mesh,
        in_specs=(rows, rows, P("batch", None), P(None, "batch", "seq")) + (weight,) * 10,
        out_specs=(rows, rows) + (weight,) * 10,
        check_vma=False,
    )
```

time: 1760 us -> 404 us (0.23)
  waiting for transfers between devices: 1420 us -> 143 us
  blocking collectives: 138 us -> 0 us
  matrix products: 122 us -> 5.05 us
  Pallas kernels: 0 us -> 84.1 us
  starting transfers between devices: 12.9 us -> 83.1 us
    reduce_scatter x9 -> x0, waiting for transfers between devices: 1030 us -> none  [the longest x1 253 us: local(): lax.psum_scatter(ffn_sum[2], ('seq', 'batch'), scatter_dimension=0, tiled...]
    all_gather x8 -> x1, waiting for transfers between devices: 367 us -> 0.01 us  [local(): full = lax.all_gather(packed, BOTH, axis=0, tiled=True)]
    dot_general x44 -> x2, matrix products: 118 us -> 5.05 us  [nn(): return jnp.dot(left, right, preferred_element_type=F32)]
    all_gather x3 -> x0, blocking collectives: 97.6 us -> none  [the longest x1 36.9 us: local(): lax.all_gather(router, ('seq', 'batch'), axis=0, tiled=True)]
    pallas_call x0 -> x12, Pallas kernels: none -> 84.1 us  [the longest x8 67.5 us: call(): pl.pallas_call(kernel, out_shape=[jax.ShapeDtypeStruct(shape, kind) for s...]
    ppermute x4 -> x17, waiting for transfers between devices: 15.6 us -> 86.5 us  [the longest x12 51.1 us: swapped(): lax.ppermute(block, 'batch', [(i, i ^ distance) for i in range(lax.axis_s...]
    all_to_all x0 -> x9, starting transfers between devices: none -> 62.6 us  [exchange(): return lax.all_to_all(blocks, axis, 0, 0, tiled=True)]
    all_to_all x0 -> x9, waiting for transfers between devices: none -> 56.9 us  [exchange(): return lax.all_to_all(blocks, axis, 0, 0, tiled=True)]
  transfers between devices with their start and end apart: 21 -> 27, of which waited for: 17 -> 10; matrix products, arithmetic and copies ran while one was open for 7% -> 14% of each run, Pallas kernels for 0% -> 19%
where the time goes in v1:
time: 404 us; the launch traced here: 397 us
  waiting for transfers between devices  143 us (35%)
  Pallas kernels  84.1 us (21%)
  starting transfers between devices  83.1 us (21%)
  other arithmetic  34.8 us (9%)
  local copies, waits for them, and re-layouts  31.4 us (8%)
  between operations  15.2 us (4%)
  matrix products  5.05 us (1%)
    pallas_call x8, Pallas kernels, call(): pl.pallas_call(kernel, out_shape=[jax.ShapeDtypeStruct(shape, kind) for s...  67.5 us
    all_to_all x9, starting transfers between devices, exchange(): return lax.all_to_all(blocks, axis, 0, 0, tiled=True)  62.6 us
    all_to_all x9, waiting for transfers between devices, exchange(): return lax.all_to_all(blocks, axis, 0, 0, tiled=True)  56.9 us
    ppermute x12, waiting for transfers between devices, swapped(): lax.ppermute(block, 'batch', [(i, i ^ distance) for i in range(lax.axis_s...  51.1 us
    ppermute x4, waiting for transfers between devices, shifted(): return lax.ppermute(block, axis, route)  35.4 us
    pallas_call x4, Pallas kernels, halves_summed(): pl.pallas_call(pair_sum, grid=(width // block,), out_shape=[jax.ShapeDtyp...  16.6 us
    ppermute x4, starting transfers between devices, shifted(): return lax.ppermute(block, axis, route)  12.1 us
    unnamed x73, local copies, waits for them, and re-layouts  10.7 us
  transfers between devices with their start and end apart: 27, of which 10 were waited for; matrix products, arithmetic and copies ran while one was open for 14% of the time, Pallas kernels for 19%

profile of v1, /device:TPU:10, one launch (start us, length us, event | category | flops | bytes accessed | tf_op | source)
XLA Modules:
  0.0 397.0 jit_solution(7025809072499976755)
XLA Ops:
  9.4 1.7 pack.1
  14.8 6.4 %all-to-all-start = ((bf16[8,32,2432]{2,1,0:T(8,128)(2,1)}), bf16[8,32,2432]{2,1,0:T(8,128)(2,1)S(1)}, u32[]{:S(2)}, u32[]{:S(2)}) async-start(bf16[8,32,2432]{2,1,0:T(8,128)(2,1)} %pad_maximum_fusion.2), calls=%async_computation | async-start | bytes 2490368 | tf_op jit(solution)/shard_map/all_to_all | solution.py:718
  22.6 4.4 %collective-permute-start.3 = (bf16[128,768]{1,0:T(8,128)(2,1)}, bf16[128,768]{1,0:T(8,128)(2,1)}, u32[]{:S(2)}, u32[]{:S(2)}) collective-permute-start(bf16[128,768]{1,0:T(8,128)(2,1)} %get-tuple-element.133), channel_id=1, source_target_pairs={{0,4},{4,8},{8,12},{12,16},{16,20},{20,24},{24,28},{1,5},{5,9},{9,... | collective-permute-start | bytes 589832 | tf_op jit(solution)/shard_map/ppermute | solution.py:710
  27.0 1.9 collective-permute-start.4
  31.2 29.1 %all-to-all-done = bf16[8,32,2432]{2,1,0:T(8,128)(2,1)S(1)} async-done(((bf16[8,32,2432]{2,1,0:T(8,128)(2,1)}), bf16[8,32,2432]{2,1,0:T(8,128)(2,1)S(1)}, u32[]{:S(2)}, u32[]{:S(2)}) %all-to-all-start) | async-done | bytes 1245216 | tf_op jit(solution)/shard_map/all_to_all | solution.py:718
  60.4 9.4 %all-to-all-start.3 = ((bf16[8,32,1792]{2,1,0:T(8,128)(2,1)}), bf16[8,32,1792]{2,1,0:T(8,128)(2,1)S(1)}, u32[]{:S(2)}, u32[]{:S(2)}) async-start(bf16[8,32,1792]{2,1,0:T(8,128)(2,1)} %fusion.6), calls=%async_computation.3 | async-start | bytes 1835008 | tf_op jit(solution)/shard_map/all_to_all | solution.py:718
  71.9 1.5 collective-permute-start.1
  74.4 6.5 %collective-permute-done.1 = bf16[240,896]{1,0:T(8,128)(2,1)S(1)} collective-permute-done((bf16[240,896]{1,0:T(8,128)(2,1)S(1)}, bf16[240,896]{1,0:T(8,128)(2,1)S(1)}, u32[]{:S(2)}, u32[]{:S(2)}) %collective-permute-start.1) | collective-permute-done | bytes 430112 | tf_op jit(solution)/shard_map/ppermute | solution.py:714
  82.8 3.2 stack.93.meta
  86.0 19.3 %all-to-all-done.3 = bf16[8,32,1792]{2,1,0:T(8,128)(2,1)S(1)} async-done(((bf16[8,32,1792]{2,1,0:T(8,128)(2,1)}), bf16[8,32,1792]{2,1,0:T(8,128)(2,1)S(1)}, u32[]{:S(2)}, u32[]{:S(2)}) %all-to-all-start.3) | async-done | bytes 917536 | tf_op jit(solution)/shard_map/all_to_all | solution.py:718
  105.4 2.0 fusion.27
  107.4 1.5 collective-permute-start.5
  110.6 1.8 maximum_select_fusion.1
  113.4 2.5 fusion.2.wx_ref
  115.9 3.7 heavy_forward.1
  119.6 9.4 %all-to-all-start.1 = ((bf16[8,32,768]{2,1,0:T(8,128)(2,1)}), bf16[8,32,768]{2,1,0:T(8,128)(2,1)S(1)}, u32[]{:S(2)}, u32[]{:S(2)}) async-start(bf16[8,32,768]{2,1,0:T(8,128)(2,1)} %bitcast.137), calls=%async_computation.1 | async-start | bytes 786432 | tf_op jit(solution)/shard_map/all_to_all | solution.py:718
  130.6 2.5 maximum_select_fusion.3
  133.8 2.6 all-to-all-done.1
  137.1 10.8 %light_forward.1 = (bf16[256,768]{1,0:T(8,128)(2,1)}, bf16[512,1536]{1,0:T(8,128)(2,1)}, bf16[256,768]{1,0:T(8,128)(2,1)}, f32[32,768]{1,0:T(8,128)}, f32[256,76...) custom-call(s32[7]{0:T(128)} %stack.93.meta, ...), custom_call_target="tpu_custom_call" | custom-call | flops 8000000000 | bytes 20000000 | tf_op jit(solution)/shard_map/light_forward/pallas_call | solution.py:689
  147.9 5.7 %all-to-all-start.2 = ((bf16[8,32,896]{2,1,0:T(8,128)(2,1)}), bf16[8,32,896]{2,1,0:T(8,128)(2,1)S(1)}, u32[]{:S(2)}, u32[]{:S(2)}) async-start(bf16[8,32,896]{2,1,0:T(8,128)(2,1)} %bitcast.130), calls=%async_computation.2 | async-start | bytes 917504 | tf_op jit(solution)/shard_map/all_to_all | solution.py:718
  155.0 1.5 maximum_select_fusion.2
  156.5 2.1 maximum_select_fusion
  159.7 2.5 convolution_convert_fusion.in_ref
  163.2 7.0 %heavy_ffn.1 = (bf16[256,896]{1,0:T(8,128)(2,1)}, bf16[256,768]{1,0:T(8,128)(2,1)}, bf16[640,1024]{1,0:T(8,128)(2,1)}, bf16[640,1024]{1,0:T(8,128)(2,1)}) custom-call(bf16[256,896]{1,0:T(8,128)(2,1)} %bitcast.131, bf16[256,768]{1,0:T(8,128)(2,1)} %bitcast.138, bf16[768,1024]{1,0:T(8,128)(2,1)} %convolution_convert_fusion.in_ref, bf16[512,768]{1,0:T(8,128)(2,1)} %bitcast.128, ...), custom_call_target="tpu_custom_call" | custom-call | flops 4000000000 | bytes 20000000 | tf_op jit(solution)/shard_map/heavy_ffn/pallas_call | solution.py:689
  170.2 6.5 %all-to-all-start.4 = ((bf16[8,32,896]{2,1,0:T(8,128)(2,1)}), bf16[8,32,896]{2,1,0:T(8,128)(2,1)S(1)}, u32[]{:S(2)}, u32[]{:S(2)}) async-start(bf16[8,32,896]{2,1,0:T(8,128)(2,1)} %bitcast.132), calls=%async_computation.4 | async-start | bytes 917504 | tf_op jit(solution)/shard_map/all_to_all | solution.py:718
  177.4 11.8 %light_ffn.1 = (f32[256,768]{1,0:T(8,128)}, f32[256,768]{1,0:T(8,128)}, bf16[384,3072]{1,0:T(8,128)(2,1)}, bf16[384,3072]{1,0:T(8,128)(2,1)}) custom-call(bf16[256,768]{1,0:T(8,128)(2,1)} %get-tuple-element.62.normed2_ref, bf16[256,768]{1,0:T(8,128)(2,1)} %bitcast.134, bf16[768,768]{1,0:T(8,128)(2,1)} %convert_convert_fusion.order_ref, ...), custom_call_target="tpu_custom_call" | custom-call | flops 8000000000 | bytes 20000000 | tf_op jit(solution)/shard_map/light_ffn/pallas_call | solution.py:689
  190.6 20.2 %light_backward.1 = (f32[256,768]{1,0:T(8,128)}, f32[256,768]{1,0:T(8,128)}, bf16[128,768]{1,0:T(8,128)(2,1)}, bf16[128,768]{1,0:T(8,128)(2,1)}, bf16[256,768]{1...) custom-call(s32[7]{0:T(128)} %stack.93.meta, ...), custom_call_target="tpu_custom_call" | custom-call | flops 16000000000 | bytes 20000000 | tf_op jit(solution)/shard_map/light_backward/pallas_call | solution.py:689
  210.8 1.9 pad_maximum_fusion.3
  212.7 6.0 %all-to-all-start.5 = ((bf16[8,32,1536]{2,1,0:T(8,128)(2,1)}), bf16[8,32,1536]{2,1,0:T(8,128)(2,1)S(1)}, u32[]{:S(2)}, u32[]{:S(2)}) async-start(bf16[8,32,1536]{2,1,0:T(8,128)(2,1)} %bitcast.53), calls=%async_computation.5 | async-start | bytes 1572864 | tf_op jit(solution)/shard_map/all_to_all | solution.py:718
  220.2 4.5 %pair_sum.6 = (bf16[192,3072]{1,0:T(8,128)(2,1)}, bf16[192,3072]{1,0:T(8,128)(2,1)}) custom-call(bf16[384,3072]{1,0:T(8,128)(2,1)} %get-tuple-element.88.keep_ref, bf16[384,3072]{1,0:T(8,128)(2,1)} %copy-done.3), custom_call_target="tpu_custom_call" | custom-call | flops 1179648 | bytes 7077888 | tf_op jit(solution)/shard_map/pair_sum/pallas_call | solution.py:749
  225.4 2.6 pair_sum.7
  230.1 5.6 %all-to-all-done.5 = bf16[8,32,1536]{2,1,0:T(8,128)(2,1)S(1)} async-done(((bf16[8,32,1536]{2,1,0:T(8,128)(2,1)}), bf16[8,32,1536]{2,1,0:T(8,128)(2,1)S(1)}, u32[]{:S(2)}, u32[]{:S(2)}) %all-to-all-start.5) | async-done | bytes 786464 | tf_op jit(solution)/shard_map/all_to_all | solution.py:718
  236.8 6.6 %heavy_backward.1 = (bf16[256,1536]{1,0:T(8,128)(2,1)}, bf16[480,896]{1,0:T(8,128)(2,1)}, bf16[480,896]{1,0:T(8,128)(2,1)}) custom-call(s32[7]{0:T(128)} %stack.93.meta, bf16[128,768]{1,0:T(8,128)(2,1)} %constant_dynamic-slice_fusion.xq_ref, bf16[256,768]{1,0:T(8,128)(2,1)} %bitcast.140, bf16[256,768]{1,0:T(8,128)(2,1)} %bitcast.141, ...), custom_call_target="tpu_custom_call" | custom-call | flops 4000000000 | bytes 20000000 | tf_op jit(solution)/shard_map/heavy_backward/pallas_call | solution.py:689
  243.4 7.0 %all-to-all-start.6 = ((bf16[8,32,1536]{2,1,0:T(8,128)(2,1)}), bf16[8,32,1536]{2,1,0:T(8,128)(2,1)S(1)}, u32[]{:S(2)}, u32[]{:S(2)}) async-start(bf16[8,32,1536]{2,1,0:T(8,128)(2,1)} %bitcast.127), calls=%async_computation.6 | async-start | bytes 1572864 | tf_op jit(solution)/shard_map/all_to_all | solution.py:718
  250.4 15.9 %collective-permute-done.16 = bf16[320,1024]{1,0:T(8,128)(2,1)S(1)} collective-permute-done((bf16[320,1024]{1,0:T(8,128)(2,1)}, bf16[320,1024]{1,0:T(8,128)(2,1)S(1)}, u32[]{:S(2)}, u32[]{:S(2)}) %collective-permute-start.16) | collective-permute-done | bytes 655392 | tf_op jit(solution)/shard_map/ppermute | solution.py:714
  270.0 6.0 %all-to-all-start.8 = ((bf16[8,24,4096]{2,1,0:T(8,128)(2,1)}), bf16[8,24,4096]{2,1,0:T(8,128)(2,1)S(1)}, u32[]{:S(2)}, u32[]{:S(2)}) async-start(bf16[8,24,4096]{2,1,0:T(8,128)(2,1)} %pad_maximum_fusion.1), calls=%async_computation.8 | async-start | bytes 3145728 | tf_op jit(solution)/shard_map/all_to_all | solution.py:718
  276.0 4.5 %pair_sum.4 = (bf16[192,3072]{1,0:T(8,128)(2,1)}, bf16[192,3072]{1,0:T(8,128)(2,1)}) custom-call(bf16[384,3072]{1,0:T(8,128)(2,1)} %get-tuple-element.80.keep_ref, bf16[384,3072]{1,0:T(8,128)(2,1)} %collective-permute-done.9.got_ref), custom_call_target="tpu_custom_call" | custom-call | flops 1179648 | bytes 7077888 | tf_op jit(solution)/shard_map/pair_sum/pallas_call | solution.py:749
  282.1 5.0 %pair_sum.5 = (bf16[240,896]{1,0:T(8,128)(2,1)}, bf16[240,896]{1,0:T(8,128)(2,1)}) custom-call(bf16[480,896]{1,0:T(8,128)(2,1)} %get-tuple-element.84.keep_ref, bf16[480,896]{1,0:T(8,128)(2,1)} %copy-done.11), custom_call_target="tpu_custom_call" | custom-call | flops 430080 | bytes 2580480 | tf_op jit(solution)/shard_map/pair_sum/pallas_call | solution.py:749
  288.4 28.6 %collective-permute-done.12 = bf16[240,896]{1,0:T(8,128)(2,1)S(1)} collective-permute-done((bf16[240,896]{1,0:T(8,128)(2,1)}, bf16[240,896]{1,0:T(8,128)(2,1)S(1)}, u32[]{:S(2)}, u32[]{:S(2)}) %collective-permute-start.12) | collective-permute-done | bytes 430112 | tf_op jit(solution)/shard_map/ppermute | solution.py:714
  318.3 1.7 add_convert_fusion.1
  321.3 6.3 %all-to-all-start.7 = ((bf16[8,24,4736]{2,1,0:T(8,128)(2,1)}), bf16[8,24,4736]{2,1,0:T(8,128)(2,1)S(1)}, u32[]{:S(2)}, u32[]{:S(2)}) async-start(bf16[8,24,4736]{2,1,0:T(8,128)(2,1)} %pad_maximum_fusion), calls=%async_computation.7 | async-start | bytes 3637248 | tf_op jit(solution)/shard_map/all_to_all | solution.py:718
  328.3 3.4 collective-permute-start.7
  331.6 2.5 collective-permute-start.8
  334.1 1.7 slice_convert_fusion
  335.8 33.4 %collective-permute-done.7.from_below_ref = bf16[128,768]{1,0:T(8,128)(2,1)S(1)} collective-permute-done((bf16[128,768]{1,0:T(8,128)(2,1)}, bf16[128,768]{1,0:T(8,128)(2,1)S(1)}, u32[]{:S(2)}, u32[]{:S(2)}) %collective-permute-start.7) | collective-permute-done | bytes 196640 | tf_op jit(solution)/shard_map/ppermute | solution.py:710
  369.2 2.1 collective-permute-done.8.from_above_ref
  371.9 5.7 %finish.1 = (bf16[256,768]{1,0:T(8,128)(2,1)}, f32[256,768]{1,0:T(8,128)}) custom-call(bf16[256,768]{1,0:T(8,128)(2,1)} %bitcast.109, f32[8,768]{1,0:T(8,128)} %get-tuple-element.54.small_ref, f32[256,768]{1,0:T(8,128)} %get-tuple-element.66.grad_middle_ref, f32[256,768]{1,0:T(8,128)} %get-tuple-element.67.grad_normed_ref, bf16[128,768]{1,0:T(8,128)(2,1)} %copy-done.19, ...), custom_call_target="tpu_custom_call" | custom-call | flops 1000000000 | bytes 20000000 | tf_op jit(solution)/shard_map/finish/pallas_call | solution.py:689
  379.9 1.8 reshape.417
  (199 shorter events, 51.5 us)
Async XLA Ops:
  7.2 5.4 %copy-start.31 = (bf16[24,2]{0,1:T(2,128)(2,1)S(1)}, bf16[24,2]{0,1:T(2,128)(2,1)}, u32[]{:S(2)}) copy-start(bf16[24,2]{0,1:T(2,128)(2,1)} %param.25) | copy-start | bytes 292
  7.2 5.4 %copy-start.30 = (bf16[24,3]{0,1:T(4,128)(2,1)S(1)}, bf16[24,3]{0,1:T(4,128)(2,1)}, u32[]{:S(2)}) copy-start(bf16[24,3]{0,1:T(4,128)(2,1)} %param.26) | copy-start | bytes 436
  7.2 129.2 %all-gather.2.cloned.1.call-start = ((), (), s32[]{:S(2)}) async-start(), calls=%async_computation.9 | async-start | bytes 9732096 | tf_op jit(solution)/shard_map/all_gather | solution.py:852
  11.1 1.9 copy-start
  14.8 6.4 %copy-start.22 = (bf16[24,768]{1,0:T(8,128)(2,1)S(1)}, bf16[24,768]{1,0:T(8,128)(2,1)}, u32[]{:S(2)}) copy-start(bf16[24,768]{1,0:T(8,128)(2,1)} %param.30) | copy-start | bytes 110596
  14.8 14.1 %copy-start.32 = (s32[1,4]{1,0:T(1,128)S(1)}, s32[1,4]{1,0:T(1,128)}, u32[]{:S(2)}) copy-start(s32[1,4]{1,0:T(1,128)} %param.23) | copy-start | bytes 52
  14.8 14.3 %copy-start.15 = (bf16[24,8192]{1,0:T(8,128)(2,1)S(1)}, bf16[24,8192]{1,0:T(8,128)(2,1)}, u32[]{:S(2)}) copy-start(bf16[24,8192]{1,0:T(8,128)(2,1)} %param.33) | copy-start | bytes 1179652
  14.8 45.6 %all-to-all-start = ((bf16[8,32,2432]{2,1,0:T(8,128)(2,1)}), bf16[8,32,2432]{2,1,0:T(8,128)(2,1)S(1)}, u32[]{:S(2)}, u32[]{:S(2)}) async-start(bf16[8,32,2432]{2,1,0:T(8,128)(2,1)} %pad_maximum_fusion.2), calls=%async_computation | async-start | bytes 2490368 | tf_op jit(solution)/shard_map/all_to_all | solution.py:718
  21.2 8.6 %copy-start.16 = (bf16[1,256,768]{2,1,0:T(8,128)(2,1)S(1)}, bf16[1,256,768]{2,1,0:T(8,128)(2,1)}, u32[]{:S(2)}) copy-start(bf16[1,256,768]{2,1,0:T(8,128)(2,1)} %param.22) | copy-start | bytes 1179652
  21.2 49.9 %collective-permute-start = (bf16[24,768]{1,0:T(8,128)(2,1)S(1)}, bf16[24,768]{1,0:T(8,128)(2,1)S(1)}, u32[]{:S(2)}, u32[]{:S(2)}) collective-permute-start(bf16[24,768]{1,0:T(8,128)(2,1)S(1)} %copy-done.22), channel_id=1, source_target_pairs={{0,4},{4,0},{8,12},{12,8},{16,20},{20,16},{24,28},{28,24},{1,5},{5... | collective-permute-start | bytes 110600 | tf_op jit(solution)/shard_map/ppermute | solution.py:882
  22.6 7.6 %copy-start.25 = (s32[2,2,128]{2,1,0:T(2,128)S(1)}, s32[2,2,128]{2,1,0:T(2,128)}, u32[]{:S(2)}) copy-start(s32[2,2,128]{2,1,0:T(2,128)} %constant.84.clone) | copy-start | bytes 6148
  22.6 7.6 %copy-start.26 = (s32[2,2,128]{2,1,0:T(2,128)S(1)}, s32[2,2,128]{2,1,0:T(2,128)}, u32[]{:S(2)}) copy-start(s32[2,2,128]{2,1,0:T(2,128)} %constant.85.clone) | copy-start | bytes 6148
  22.6 111.2 %collective-permute-start.3 = (bf16[128,768]{1,0:T(8,128)(2,1)}, bf16[128,768]{1,0:T(8,128)(2,1)}, u32[]{:S(2)}, u32[]{:S(2)}) collective-permute-start(bf16[128,768]{1,0:T(8,128)(2,1)} %get-tuple-element.133), channel_id=1, source_target_pairs={{0,4},{4,8},{8,12},{12,16},{16,20},{20,24},{24,28},{1,5},{5,9},{9,... | collective-permute-start | bytes 589832 | tf_op jit(solution)/shard_map/ppermute | solution.py:710
  27.0 106.8 %collective-permute-start.4 = (bf16[128,768]{1,0:T(8,128)(2,1)}, bf16[128,768]{1,0:T(8,128)(2,1)}, u32[]{:S(2)}, u32[]{:S(2)}) collective-permute-start(bf16[128,768]{1,0:T(8,128)(2,1)} %get-tuple-element.132), channel_id=1, source_target_pairs={{4,0},{8,4},{12,8},{16,12},{20,16},{24,20},{28,24},{5,1},{9,5},{13... | collective-permute-start | bytes 589832 | tf_op jit(solution)/shard_map/ppermute | solution.py:710
  60.4 44.9 %all-to-all-start.3 = ((bf16[8,32,1792]{2,1,0:T(8,128)(2,1)}), bf16[8,32,1792]{2,1,0:T(8,128)(2,1)S(1)}, u32[]{:S(2)}, u32[]{:S(2)}) async-start(bf16[8,32,1792]{2,1,0:T(8,128)(2,1)} %fusion.6), calls=%async_computation.3 | async-start | bytes 1835008 | tf_op jit(solution)/shard_map/all_to_all | solution.py:718
  71.9 14.1 %copy-start.23 = (s32[2,2,8,24]{3,2,1,0:T(8,128)S(1)}, s32[2,2,8,24]{3,2,1,0:T(8,128)}, u32[]{:S(2)}) copy-start(s32[2,2,8,24]{3,2,1,0:T(8,128)} %constant.82.clone) | copy-start | bytes 9220
  71.9 14.1 %copy-start.24 = (s32[2,2,8,24]{3,2,1,0:T(8,128)S(1)}, s32[2,2,8,24]{3,2,1,0:T(8,128)}, u32[]{:S(2)}) copy-start(s32[2,2,8,24]{3,2,1,0:T(8,128)} %constant.83.clone) | copy-start | bytes 9220
  71.9 9.0 %collective-permute-start.1 = (bf16[240,896]{1,0:T(8,128)(2,1)S(1)}, bf16[240,896]{1,0:T(8,128)(2,1)S(1)}, u32[]{:S(2)}, u32[]{:S(2)}) collective-permute-start(bf16[240,896]{1,0:T(8,128)(2,1)S(1)} %get-tuple-element.131), channel_id=1, source_target_pairs={{0,2},{1,3},{2,0},{3,1},{4,6},{5,7},{6,4},{7,5},{8,10},{9,11},{10,... | collective-permute-start | bytes 1290248 | tf_op jit(solution)/shard_map/ppermute | solution.py:714
  82.8 27.8 %collective-permute-start.2 = (bf16[2,240,896]{2,1,0:T(8,128)(2,1)}, bf16[2,240,896]{2,1,0:T(8,128)(2,1)}, u32[]{:S(2)}, u32[]{:S(2)}) collective-permute-start(bf16[2,240,896]{2,1,0:T(8,128)(2,1)} %maximum_select_fusion.5), channel_id=1, source_target_pairs={{0,1},{1,0},{2,3},{3,2},{4,5},{5,4},{6,7},{7,6},{8,9},{9,8},{10,11... | collective-permute-start | bytes 2580488 | tf_op jit(solution)/shard_map/ppermute | solution.py:714
  107.4 3.0 copy-start.5
  107.4 3.0 copy-start.6
  107.4 23.2 %collective-permute-start.5 = (bf16[320,1024]{1,0:T(8,128)(2,1)}, bf16[320,1024]{1,0:T(8,128)(2,1)}, u32[]{:S(2)}, u32[]{:S(2)}) collective-permute-start(bf16[320,1024]{1,0:T(8,128)(2,1)} %get-tuple-element.128), channel_id=1, source_target_pairs={{0,2},{1,3},{2,0},{3,1},{4,6},{5,7},{6,4},{7,5},{8,10},{9,11},{10,... | collective-permute-start | bytes 1966088 | tf_op jit(solution)/shard_map/ppermute | solution.py:714
  119.6 16.8 %all-to-all-start.1 = ((bf16[8,32,768]{2,1,0:T(8,128)(2,1)}), bf16[8,32,768]{2,1,0:T(8,128)(2,1)S(1)}, u32[]{:S(2)}, u32[]{:S(2)}) async-start(bf16[8,32,768]{2,1,0:T(8,128)(2,1)} %bitcast.137), calls=%async_computation.1 | async-start | bytes 786432 | tf_op jit(solution)/shard_map/all_to_all | solution.py:718
  133.1 23.4 %collective-permute-start.6 = (bf16[2,320,1024]{2,1,0:T(8,128)(2,1)}, bf16[2,320,1024]{2,1,0:T(8,128)(2,1)}, u32[]{:S(2)}, u32[]{:S(2)}) collective-permute-start(bf16[2,320,1024]{2,1,0:T(8,128)(2,1)} %maximum_select_fusion.3), channel_id=1, source_target_pairs={{0,1},{1,0},{2,3},{3,2},{4,5},{5,4},{6,7},{7,6},{8,9},{9,8},{10,11... | collective-permute-start | bytes 3932168 | tf_op jit(solution)/shard_map/ppermute | solution.py:714
  147.9 14.5 %all-to-all-start.2 = ((bf16[8,32,896]{2,1,0:T(8,128)(2,1)}), bf16[8,32,896]{2,1,0:T(8,128)(2,1)S(1)}, u32[]{:S(2)}, u32[]{:S(2)}) async-start(bf16[8,32,896]{2,1,0:T(8,128)(2,1)} %bitcast.130), calls=%async_computation.2 | async-start | bytes 917504 | tf_op jit(solution)/shard_map/all_to_all | solution.py:718
  170.2 19.6 %all-to-all-start.4 = ((bf16[8,32,896]{2,1,0:T(8,128)(2,1)}), bf16[8,32,896]{2,1,0:T(8,128)(2,1)S(1)}, u32[]{:S(2)}, u32[]{:S(2)}) async-start(bf16[8,32,896]{2,1,0:T(8,128)(2,1)} %bitcast.132), calls=%async_computation.4 | async-start | bytes 917504 | tf_op jit(solution)/shard_map/all_to_all | solution.py:718
  189.2 29.6 %collective-permute-start.13 = (bf16[384,3072]{1,0:T(8,128)(2,1)}, bf16[384,3072]{1,0:T(8,128)(2,1)S(1)}, u32[]{:S(2)}, u32[]{:S(2)}) collective-permute-start(bf16[384,3072]{1,0:T(8,128)(2,1)} %get-tuple-element.89), channel_id=1, source_target_pairs={{0,1},{1,0},{2,3},{3,2},{4,5},{5,4},{6,7},{7,6},{8,9},{9,8},{10,11... | collective-permute-start | bytes 7077896 | tf_op jit(solution)/shard_map/ppermute | solution.py:714
  189.3 36.1 %collective-permute-start.15 = (bf16[640,1024]{1,0:T(8,128)(2,1)}, bf16[640,1024]{1,0:T(8,128)(2,1)}, u32[]{:S(2)}, u32[]{:S(2)}) collective-permute-start(bf16[640,1024]{1,0:T(8,128)(2,1)} %get-tuple-element.93), channel_id=1, source_target_pairs={{0,1},{1,0},{2,3},{3,2},{4,5},{5,4},{6,7},{7,6},{8,9},{9,8},{10,11... | collective-permute-start | bytes 3932168 | tf_op jit(solution)/shard_map/ppermute | solution.py:714
  190.6 20.2 %copy-start.18 = (bf16[256,768]{1,0:T(8,128)(2,1)S(1)}, bf16[256,768]{1,0:T(8,128)(2,1)}, u32[]{:S(2)}) copy-start(bf16[256,768]{1,0:T(8,128)(2,1)} %get-tuple-element.71) | copy-start | bytes 1179652
  210.7 8.0 %copy-start.28 = (s32[2,2,2,24]{3,2,1,0:T(2,128)S(1)}, s32[2,2,2,24]{3,2,1,0:T(2,128)}, u32[]{:S(2)}) copy-start(s32[2,2,2,24]{3,2,1,0:T(2,128)} %constant.86.clone) | copy-start | bytes 2308
  210.8 8.0 %copy-start.29 = (s32[2,2,2,24]{3,2,1,0:T(2,128)S(1)}, s32[2,2,2,24]{3,2,1,0:T(2,128)}, u32[]{:S(2)}) copy-start(s32[2,2,2,24]{3,2,1,0:T(2,128)} %constant.87.clone) | copy-start | bytes 2308
  212.7 23.1 %all-to-all-start.5 = ((bf16[8,32,1536]{2,1,0:T(8,128)(2,1)}), bf16[8,32,1536]{2,1,0:T(8,128)(2,1)S(1)}, u32[]{:S(2)}, u32[]{:S(2)}) async-start(bf16[8,32,1536]{2,1,0:T(8,128)(2,1)} %bitcast.53), calls=%async_computation.5 | async-start | bytes 1572864 | tf_op jit(solution)/shard_map/all_to_all | solution.py:718
  224.7 42.0 %collective-permute-start.14 = (bf16[192,3072]{1,0:T(8,128)(2,1)}, bf16[192,3072]{1,0:T(8,128)(2,1)S(1)}, u32[]{:S(2)}, u32[]{:S(2)}) collective-permute-start(bf16[192,3072]{1,0:T(8,128)(2,1)} %get-tuple-element.91), channel_id=1, source_target_pairs={{0,2},{1,3},{2,0},{3,1},{4,6},{5,7},{6,4},{7,5},{8,10},{9,11},{10,... | collective-permute-start | bytes 3538952 | tf_op jit(solution)/shard_map/ppermute | solution.py:714
  225.4 50.6 %collective-permute-start.9 = (bf16[384,3072]{1,0:T(8,128)(2,1)}, bf16[384,3072]{1,0:T(8,128)(2,1)}, u32[]{:S(2)}, u32[]{:S(2)}) collective-permute-start(bf16[384,3072]{1,0:T(8,128)(2,1)} %get-tuple-element.81), channel_id=1, source_target_pairs={{0,1},{1,0},{2,3},{3,2},{4,5},{5,4},{6,7},{7,6},{8,9},{9,8},{10,11... | collective-permute-start | bytes 7077896 | tf_op jit(solution)/shard_map/ppermute | solution.py:714
  228.1 38.3 %collective-permute-start.16 = (bf16[320,1024]{1,0:T(8,128)(2,1)}, bf16[320,1024]{1,0:T(8,128)(2,1)S(1)}, u32[]{:S(2)}, u32[]{:S(2)}) collective-permute-start(bf16[320,1024]{1,0:T(8,128)(2,1)} %get-tuple-element.95), channel_id=1, source_target_pairs={{0,2},{1,3},{2,0},{3,1},{4,6},{5,7},{6,4},{7,5},{8,10},{9,11},{10,... | collective-permute-start | bytes 1966088 | tf_op jit(solution)/shard_map/ppermute | solution.py:714
  243.4 23.0 %copy-start.12 = (bf16[320,1024]{1,0:T(8,128)(2,1)S(1)}, bf16[320,1024]{1,0:T(8,128)(2,1)}, u32[]{:S(2)}) copy-start(bf16[320,1024]{1,0:T(8,128)(2,1)} %get-tuple-element.94) | copy-start | bytes 1966084
  243.4 25.8 %all-to-all-start.6 = ((bf16[8,32,1536]{2,1,0:T(8,128)(2,1)}), bf16[8,32,1536]{2,1,0:T(8,128)(2,1)S(1)}, u32[]{:S(2)}, u32[]{:S(2)}) async-start(bf16[8,32,1536]{2,1,0:T(8,128)(2,1)} %bitcast.127), calls=%async_computation.6 | async-start | bytes 1572864 | tf_op jit(solution)/shard_map/all_to_all | solution.py:718
  250.4 17.0 %copy-start.7 = (bf16[192,3072]{1,0:T(8,128)(2,1)S(1)}, bf16[192,3072]{1,0:T(8,128)(2,1)}, u32[]{:S(2)}) copy-start(bf16[192,3072]{1,0:T(8,128)(2,1)} %get-tuple-element.90) | copy-start | bytes 3538948
  266.6 14.5 %collective-permute-start.11 = (bf16[480,896]{1,0:T(8,128)(2,1)}, bf16[480,896]{1,0:T(8,128)(2,1)S(1)}, u32[]{:S(2)}, u32[]{:S(2)}) collective-permute-start(bf16[480,896]{1,0:T(8,128)(2,1)} %get-tuple-element.85), channel_id=1, source_target_pairs={{0,1},{1,0},{2,3},{3,2},{4,5},{5,4},{6,7},{7,6},{8,9},{9,8},{10,11... | collective-permute-start | bytes 2580488 | tf_op jit(solution)/shard_map/ppermute | solution.py:714
  270.0 51.3 %all-to-all-start.8 = ((bf16[8,24,4096]{2,1,0:T(8,128)(2,1)}), bf16[8,24,4096]{2,1,0:T(8,128)(2,1)S(1)}, u32[]{:S(2)}, u32[]{:S(2)}) async-start(bf16[8,24,4096]{2,1,0:T(8,128)(2,1)} %pad_maximum_fusion.1), calls=%async_computation.8 | async-start | bytes 3145728 | tf_op jit(solution)/shard_map/all_to_all | solution.py:718
  280.5 37.7 %collective-permute-start.10 = (bf16[192,3072]{1,0:T(8,128)(2,1)}, bf16[192,3072]{1,0:T(8,128)(2,1)}, u32[]{:S(2)}, u32[]{:S(2)}) collective-permute-start(bf16[192,3072]{1,0:T(8,128)(2,1)} %get-tuple-element.83), channel_id=1, source_target_pairs={{0,2},{1,3},{2,0},{3,1},{4,6},{5,7},{6,4},{7,5},{8,10},{9,11},{10,... | collective-permute-start | bytes 3538952 | tf_op jit(solution)/shard_map/ppermute | solution.py:714
  287.0 31.2 %copy-start.8 = (bf16[192,3072]{1,0:T(8,128)(2,1)S(1)}, bf16[192,3072]{1,0:T(8,128)(2,1)}, u32[]{:S(2)}) copy-start(bf16[192,3072]{1,0:T(8,128)(2,1)} %get-tuple-element.82) | copy-start | bytes 3538948
  287.0 30.0 %collective-permute-start.12 = (bf16[240,896]{1,0:T(8,128)(2,1)}, bf16[240,896]{1,0:T(8,128)(2,1)S(1)}, u32[]{:S(2)}, u32[]{:S(2)}) collective-permute-start(bf16[240,896]{1,0:T(8,128)(2,1)} %get-tuple-element.87), channel_id=1, source_target_pairs={{0,2},{1,3},{2,0},{3,1},{4,6},{5,7},{6,4},{7,5},{8,10},{9,11},{10,... | collective-permute-start | bytes 1290248 | tf_op jit(solution)/shard_map/ppermute | solution.py:714
  321.3 62.9 %all-to-all-start.7 = ((bf16[8,24,4736]{2,1,0:T(8,128)(2,1)}), bf16[8,24,4736]{2,1,0:T(8,128)(2,1)S(1)}, u32[]{:S(2)}, u32[]{:S(2)}) async-start(bf16[8,24,4736]{2,1,0:T(8,128)(2,1)} %pad_maximum_fusion), calls=%async_computation.7 | async-start | bytes 3637248 | tf_op jit(solution)/shard_map/all_to_all | solution.py:718
  328.3 40.9 %collective-permute-start.7 = (bf16[128,768]{1,0:T(8,128)(2,1)}, bf16[128,768]{1,0:T(8,128)(2,1)S(1)}, u32[]{:S(2)}, u32[]{:S(2)}) collective-permute-start(bf16[128,768]{1,0:T(8,128)(2,1)} %get-tuple-element.68), channel_id=1, source_target_pairs={{0,4},{4,8},{8,12},{12,16},{16,20},{20,24},{24,28},{1,5},{5,9},{9,... | collective-permute-start | bytes 589832 | tf_op jit(solution)/shard_map/ppermute | solution.py:710
  331.6 39.6 %collective-permute-start.8 = (bf16[128,768]{1,0:T(8,128)(2,1)}, bf16[128,768]{1,0:T(8,128)(2,1)S(1)}, u32[]{:S(2)}, u32[]{:S(2)}) collective-permute-start(bf16[128,768]{1,0:T(8,128)(2,1)} %get-tuple-element.69), channel_id=1, source_target_pairs={{4,0},{8,4},{12,8},{16,12},{20,16},{24,20},{28,24},{5,1},{9,5},{13... | collective-permute-start | bytes 589832 | tf_op jit(solution)/shard_map/ppermute | solution.py:710
  369.2 2.1 copy-start.19
  381.7 1.8 copy-start.10
  (14 other events, 14.3 us)
Sparse Core Ops, SparseCore 0:
  11.2 106.2 all-gather.1

commit v2 on v1

--- a/solution.py
+++ b/solution.py
@@ -142,10 +142,10 @@
     return row_sum(jnp.where(lanes < 2, block.astype(F32), 0.0))
 
 
-def sum_blocks(ref, count):
-    total = ref[0:count].astype(F32)
+def sum_blocks(ref, count, cols=slice(None)):
+    total = ref[0:count, cols].astype(F32)
     for i in range(1, ref.shape[0] // count):
-        total = total + ref[i * count : (i + 1) * count].astype(F32)
+        total = total + ref[i * count : (i + 1) * count, cols].astype(F32)
     return total
 
 
@@ -184,8 +184,7 @@
     probs = softmax(nt(stacked, kv_ref[:, :LANES]) * DH ** (-0.5) + bias)
     mixed = low(merge_heads(nn(low(probs), kv_ref[:, LANES:]), masks))
     mixed_ref[...] = mixed
-    raw_ref[...] = jnp.zeros_like(raw_ref)
-    raw_ref[pl.ds(pl.multiple_of(meta[6], count), count)] = low(nn(mixed, out_ref[...]))
+    raw_ref[...] = low(nn(mixed, out_ref[...]))
 
 
 def light_forward(
@@ -491,8 +490,7 @@
     q_norm = q_plain * gain_1
     q_gate = sigmoid_dot(q_norm, small[2:3])
     grad_raw = low(q_rows * q_gate)
-    for i in range(grad_raw_ref.shape[0] // routed):
-        grad_raw_ref[i * routed : (i + 1) * routed] = grad_raw
+    grad_raw_ref[...] = grad_raw
     q_logit = row_sum(q_rows * heavy_raw_ref[...]) * q_gate * (1.0 - q_gate)
     q_back = q_logit * small[2:3]
     router_q = jnp.sum(q_norm * q_logit, axis=0, keepdims=True)
@@ -577,7 +575,7 @@
     small = small_ref[...]
     gain_1 = small[0:1]
     place = pl.ds(pl.multiple_of(meta[6], count), count)
-    grad_raw = grad_raw_ref[place]
+    grad_raw = grad_raw_ref[...]
     do = low(nt(grad_raw, out_ref[...]))
     masks = head_rows(LANES, DH)[: HH // PARTS]
     scale = DH ** (-0.5)
@@ -642,7 +640,6 @@
     middle_ref,
     light_ref,
     f_norm_ref,
-    ffn_ref,
     output_ref,
     input_grad_ref,
 ):
@@ -650,11 +647,11 @@
     routed = f_norm_ref.shape[0]
     small = small_ref[...]
     gate = sigmoid_dot(f_norm_ref[...], small[4:5])
-    heavy = exact(pf_t_ref[...], sum_blocks(ffn_ref, routed) * gate)
+    backs = sum_blocks(backs_ref, routed, slice(0, 3 * features))
+    heavy = exact(pf_t_ref[...], backs[:, 2 * features :] * gate)
     output_ref[...] = low(middle_ref[...] + light_ref[...] + heavy)
-    backs = sum_blocks(backs_ref, routed)
     grad = grad_normed_ref[...] + exact(pq_t_ref[...], backs[:, :features])
-    grad = grad + exact(pk_t_ref[...], backs[:, features:])
+    grad = grad + exact(pk_t_ref[...], backs[:, features : 2 * features])
     below = from_below_ref[...].astype(F32)
     above = from_above_ref[...].astype(F32)
     grad = grad + jnp.concatenate([below, above], axis=0)
@@ -674,6 +671,106 @@
     for i in range(1, ref.shape[0]):
         total = total + ref[i, :, cols].astype(F32)
     return total
+
+
+def join_blocks(out_ref, at, first_ref, second_ref, width):
+    rows = out_ref.shape[1]
+    total = first_ref[: out_ref.shape[0] * rows, :width].astype(F32)
+    total = total + second_ref[: out_ref.shape[0] * rows, :width].astype(F32)
+    for i in range(out_ref.shape[0]):
+        out_ref[i, :, at : at + width] = low(total[i * rows : (i + 1) * rows])
+
+
+def join_light(keep_ref, got_ref, out_ref):
+    join_blocks(out_ref, 0, keep_ref, got_ref, keep_ref.shape[1])
+
+
+def join_back(backs_ref, ffn_ref, keep_ref, got_ref, out_ref, down_ref):
+    blocks, routed, width = out_ref.shape
+    features = ffn_ref.shape[1]
+    in_rows = keep_ref.shape[0] - down_ref.shape[0]
+    rows = in_rows // blocks
+    hidden = width - 3 * features
+    total = keep_ref[...].astype(F32) + got_ref[...].astype(F32)
+    down_ref[...] = total[in_rows:, :features]
+    for i in range(blocks):
+        out_ref[i, :, : 2 * features] = backs_ref[i * routed : (i + 1) * routed]
+        out_ref[i, :, 2 * features : 3 * features] = ffn_ref[i * routed : (i + 1) * routed]
+        out_ref[i, :rows, 3 * features :] = low(total[i * rows : (i + 1) * rows, :hidden])
+        out_ref[i, rows:, 3 * features :] = jnp.zeros((routed - rows, hidden), BF)
+
+
+def join_attention(keep_ref, got_ref, head_keep_ref, head_got_ref, out_ref, rest_ref):
+    wide = keep_ref.shape[1]
+    join_blocks(out_ref, 0, keep_ref, got_ref, wide)
+    join_blocks(out_ref, wide, head_keep_ref, head_got_ref, out_ref.shape[2] - wide)
+    start = out_ref.shape[0] * out_ref.shape[1]
+    count, features = rest_ref.shape
+    rest = head_keep_ref[start : start + count, :features].astype(F32)
+    rest_ref[...] = low(rest + head_got_ref[start : start + count, :features].astype(F32))
+
+
+def in_order(pair, own_ref, other_ref, out_ref):
+    out_ref[pair[0]] = own_ref[...]
+    out_ref[1 - pair[0]] = other_ref[...]
+
+
+def pack_late(t_ref, in_ref, out_ref):
+    features = t_ref.shape[1]
+    rows = in_ref.shape[0]
+    hidden = in_ref.shape[1] // 2 // out_ref.shape[0]
+    for i in range(out_ref.shape[0]):
+        out_ref[i, :, :features] = t_ref[...]
+        for half in range(2):
+            at = half * in_ref.shape[1] // 2 + i * hidden
+            to = features + half * hidden
+            out_ref[i, :rows, to : to + hidden] = in_ref[:, at : at + hidden]
+            out_ref[i, rows:, to : to + hidden] = jnp.zeros((out_ref.shape[1] - rows, hidden), BF)
+
+
+def light_results(total_ref, light_in_ref, light_down_ref):
+    rows, features = total_ref.shape[1], light_down_ref.shape[1]
+    wide = light_in_ref.shape[1]
+    more = light_down_ref.shape[0] - rows
+    width = features * more // rows
+    light_in_ref[...] = sum_leading(total_ref, slice(0, wide))
+    light_down_ref[:rows] = sum_leading(total_ref, slice(wide, wide + features))
+    rest = sum_leading(total_ref, slice(wide + features, wide + features + width))
+    for i in range(rows // more):
+        light_down_ref[rows:, i * width : (i + 1) * width] = rest[i * more : (i + 1) * more]
+
+
+def hidden_results(total_ref, heavy_in_ref):
+    blocks = total_ref.shape[0]
+    rows = heavy_in_ref.shape[0]
+    hidden = heavy_in_ref.shape[1] // 2 // blocks
+    first = total_ref.shape[2] - 2 * hidden
+    for i in range(blocks):
+        for half in range(2):
+            at = half * heavy_in_ref.shape[1] // 2 + i * hidden
+            cols = slice(first + half * hidden, first + (half + 1) * hidden)
+            heavy_in_ref[:, at : at + hidden] = total_ref[i, :, cols].astype(F32)[:rows]
+
+
+def attention_results(total_ref, light_qkv_ref, light_out_ref, heavy_ref, small_ref):
+    blocks = total_ref.shape[0]
+    wide = light_qkv_ref.shape[1]
+    features = light_out_ref.shape[1]
+    light_qkv_ref[...] = sum_leading(total_ref, slice(0, wide))
+    light_out_ref[...] = sum_leading(total_ref, slice(wide, wide + features))
+    first = wide + features
+    each = blocks // PARTS
+    width = features // PARTS
+    for kind in range(3):
+        cols = slice(first + kind * LANES, first + (kind + 1) * LANES)
+        pieces = []
+        for part in range(PARTS):
+            total = total_ref[part * each, :, cols].astype(F32)
+            for i in range(1, each):
+                total = total + total_ref[part * each + i, :, cols].astype(F32)
+            pieces.append(total[:, :width])
+        heavy_ref[:, kind * features : (kind + 1) * features] = jnp.concatenate(pieces, axis=1)
+    small_ref[...] = sum_leading(total_ref, slice(first + 3 * LANES, first + 3 * LANES + SMALL))
 
 
 def pack_blocks(*refs):
@@ -684,8 +781,18 @@
         at += ref.shape[1]
 
 
-def call(kernel, args, memory, outs, scratch, flops, name, far=0):
+def after(kernel, count, extra):
+    def body(*refs):
+        kernel(*refs[:count], *refs[count + extra :])
+
+    return body if extra else kernel
+
+
+def call(kernel, args, memory, outs, scratch, flops, name, far=0, needs=()):
     spaces = {"v": pltpu.VMEM, "s": pltpu.SMEM, "h": pl.ANY}
+    kernel = after(kernel, len(args), len(needs))
+    args = tuple(args) + tuple(needs)
+    memory = memory + "h" * len(needs)
     return pl.pallas_call(
         kernel,
         out_shape=[jax.ShapeDtypeStruct(shape, kind) for shape, kind in outs],
@@ -740,30 +847,25 @@
     return jnp.concatenate([down[:rows], jnp.concatenate(pieces, axis=0)], axis=1)
 
 
-def halves_summed(keep, got, height, width):
+def halves_summed(keep, got, needs=()):
+    height, width = keep.shape
     count = height // 2
     steps = width // 128
-    block = 128 * max(i for i in range(1, 7) if steps % i == 0)
+    block = 128 * max(i for i in range(1, 9) if steps % i == 0)
     rows_in = pl.BlockSpec((height, block), lambda i: (0, i))
     rows_out = pl.BlockSpec((count, block), lambda i: (0, i))
     return pl.pallas_call(
-        pair_sum,
+        after(pair_sum, 2, len(needs)),
         grid=(width // block,),
         out_shape=[jax.ShapeDtypeStruct((count, width), BF)] * 2,
-        in_specs=[rows_in] * 2,
+        in_specs=[rows_in] * 2 + [pl.BlockSpec(memory_space=pl.ANY)] * len(needs),
         out_specs=[rows_out] * 2,
         compiler_params=pltpu.CompilerParams(vmem_limit_bytes=VMEM_LIMIT),
         cost_estimate=pl.CostEstimate(
             flops=height * width, bytes_accessed=6 * height * width, transcendentals=0
         ),
         name="pair_sum",
-    )(keep, got)
-
-
-def batch_summed(send, keep):
-    height, width = keep.shape
-    send, keep = halves_summed(keep, swapped(send, 1), height, width)
-    return low(keep.astype(F32) + swapped(send, 2).astype(F32))
+    )(keep, got, *needs)
 
 
 def canonical(piece, core, pair):
@@ -772,15 +874,6 @@
     other = swapped(piece, 1)
     piece = jnp.where(core == 0, jnp.stack([piece, other], 1), jnp.stack([other, piece], 1))
     return piece.reshape((4,) + piece.shape[2:])
-
-
-def unpack_rows(packed, features):
-    rows = packed.shape[0]
-    width = packed.shape[1] - features
-    count = features // width
-    rest = packed[:, features:].reshape(count, rows // count, width)
-    rest = jnp.concatenate([rest[i] for i in range(count)], axis=1)
-    return jnp.concatenate([packed[:, :features], rest], axis=0)
 
 
 def pad_cols(block, width):
@@ -875,9 +968,6 @@
     head_cols = jnp.concatenate([head_cols, every(small)], axis=2)
     sent = jnp.concatenate([every(jnp.concatenate([xq, xk], axis=1)), tall(head_cols)], axis=2)
     travel = exchange(sent, "seq")
-    in_cols = heavy_in.reshape(rows, 2, seq_n, hidden).transpose(2, 0, 1, 3)
-    in_cols = in_cols.reshape(seq_n, rows, 2 * hidden)
-    late = exchange(jnp.concatenate([every(t), tall(in_cols)], axis=2), "seq")
     if query_parts == 2:
         other = lax.ppermute(heavy_out, "seq", [(i, i ^ 1) for i in range(seq_n)])
         out_rows = jnp.where(
@@ -897,13 +987,6 @@
     h_out = piece[:, in_rows:, :features].reshape(batch_n, query_parts, rows, features)
     h_out = h_out.transpose(1, 0, 2, 3).reshape(head_width, features)
     h_out = jnp.pad(h_out, ((0, LANES - head_width), (0, 0)))
-    pack_width = max(2 * hidden, features)
-    piece = late[:, :rows, features:].reshape(in_rows, 2 * hidden)
-    piece = [pad_cols(piece, pack_width), pad_cols(heavy_down, pack_width)]
-    piece = canonical(jnp.concatenate(piece, axis=0), core, pair)
-    h_in = low(nn(order_h, piece[:, :in_rows, : 2 * hidden].reshape(features, 2 * hidden)))
-    h_down = piece[:, in_rows:, :features].reshape(hidden, features)
-    t_all = late[:, :, :features].reshape(keys, features)
     below = shifted(x[tokens - WIN :], "seq", 1)
     above = shifted(x[:WIN], "seq", -1)
 
@@ -936,7 +1019,7 @@
         (meta, xq_part, xk_all, wx, h_out),
         "svvvv",
         [
-            ((keys, features), BF),
+            ((count, features), BF),
             ((count, LANES), BF),
             ((keys, 2 * LANES), BF),
             ((count, LANES), BF),
@@ -946,8 +1029,33 @@
         2_000_000_000,
         "heavy_forward",
     )
-    raw = presum(exchange(raw.reshape(seq_n, routed, features), "seq"))
-
+    part_of, query_of = lambda i: i // query_parts, lambda i: i % query_parts
+    owner = lambda i, step: query_of(i) * PARTS + (part_of(i) + step) % PARTS
+    steps = range(PARTS)
+    raw = raw.reshape(PARTS, routed, features)
+    raw = [lax.dynamic_index_in_dim(raw, (part + step) % PARTS, 0, False) for step in steps]
+    raw = [
+        lax.ppermute(block, "seq", [(i, owner(i, step)) for i in range(seq_n)])
+        for step, block in zip(steps, raw)
+    ]
+    raw = jnp.concatenate(raw, axis=0)
+
+    late = call(
+        pack_late,
+        (t, heavy_in),
+        "vv",
+        [((seq_n, routed, features + 2 * hidden), BF)],
+        [],
+        1_000_000,
+        "pack_late",
+        needs=[travel],
+    )[0]
+    late = exchange(late, "seq")
+    pack_width = max(2 * hidden, features)
+    piece = late[:, :rows, features:].reshape(in_rows, 2 * hidden)
+    piece = [pad_cols(piece, pack_width), pad_cols(heavy_down, pack_width)]
+    late_piece = jnp.concatenate(piece, axis=0)
+    late_other = swapped(late_piece, 2)
     weight = lambda columns: pltpu.VMEM((features, columns), BF)
     q, kv, mixed, heavy_raw, middle, normed2, f_norm, f_sent = call(
         functools.partial(light_forward, layout),
@@ -968,6 +1076,23 @@
         "light_forward",
     )
     f_sent = exchange(f_sent.reshape(seq_n, routed, features + SMALL), "seq")
+    piece = call(
+        in_order,
+        (pair.reshape(1).astype(jnp.int32), late_piece, late_other),
+        "svv",
+        [((2,) + late_piece.shape, BF)],
+        [],
+        1_000_000,
+        "in_order",
+        needs=[middle],
+    )[0]
+    other = swapped(piece, 1)
+    piece = jnp.where(core == 0, jnp.stack([piece, other], 1), jnp.stack([other, piece], 1))
+    piece = piece.reshape((batch_n,) + late_piece.shape)
+    h_in = low(nn(order_h, piece[:, :in_rows, : 2 * hidden].reshape(features, 2 * hidden)))
+    h_down = piece[:, in_rows:, :features].reshape(hidden, features)
+    t_all = late[:, :, :features].reshape(keys, features)
+
     light_hidden = light_in.shape[1] // 2
     down_width = layout["light_down"][1] - layout["light_down"][0]
     half = features // 2
@@ -993,6 +1118,9 @@
         8_000_000_000,
         "light_ffn",
     )
+    light_got = swapped(light_send, 1)
+    light_send, light_keep = halves_summed(light_keep, light_got)
+    light_got = swapped(light_send, 2)
     down_rows = hidden // batch_n
     back, ffn_part, ffn_send, ffn_keep = call(
         functools.partial(heavy_ffn, batch_n),
@@ -1007,18 +1135,24 @@
         [],
         4_000_000_000,
         "heavy_ffn",
+        needs=[light_keep],
     )
     back = presum(exchange(back.reshape(seq_n, routed, features + SMALL), "seq"))
 
-    ffn_total = batch_summed(ffn_send, ffn_keep)
-    light_total = batch_summed(light_send, light_keep)
-    ffn_rows = ffn_total[:in_rows, : 2 * hidden].reshape(seq_n, rows, 2 * hidden)
-    light_rows = light_total.reshape(seq_n, rows, ffn_width)
-    ffn_rows = exchange(jnp.concatenate([light_rows, ffn_rows], axis=2), "seq").astype(F32)
-    grad_h_down = ffn_total[in_rows:, :features].astype(F32)
-    grad_h_in = ffn_rows[:, :, ffn_width:].reshape(seq_n, rows, 2, hidden).transpose(1, 2, 0, 3)
-    grad_h_in = grad_h_in.reshape(rows, 2 * hidden * seq_n)
-    shard_f = jnp.sum(ffn_rows[:, :, :ffn_width], axis=0)
+    ffn_got = swapped(ffn_send, 1)
+    ffn_send, ffn_keep = halves_summed(ffn_keep, ffn_got)
+    ffn_got = swapped(ffn_send, 2)
+    light_rows = call(
+        join_light,
+        (light_keep, light_got),
+        "vv",
+        [((seq_n, rows, ffn_width), BF)],
+        [],
+        10_000_000,
+        "join_light",
+        needs=[ffn_keep],
+    )[0]
+    light_sums = exchange(light_rows, "seq")
 
     (
         grad_middle,
@@ -1027,8 +1161,8 @@
         halo_above,
         grad_raw,
         small_grad,
-        light_send,
-        light_keep,
+        attn_send,
+        attn_keep,
     ) = call(
         functools.partial(light_backward, layout),
         (
@@ -1059,7 +1193,7 @@
             ((tokens, features), F32),
             ((WIN, features), BF),
             ((WIN, features), BF),
-            ((keys, features), BF),
+            ((routed, features), BF),
             ((8, features), F32),
             ((half, wide + features), BF),
             ((half, wide + features), BF),
@@ -1076,14 +1210,20 @@
         16_000_000_000,
         "light_backward",
         2,
-    )
-
-    light_total = batch_summed(light_send, light_keep)
-
-    both = jnp.concatenate([grad_raw, ffn_part], axis=1).reshape(seq_n, routed, 2 * features)
-    both = exchange(both, "seq")
-    grad_raw = both[:, :, :features].reshape(keys, features)
-    ffn_part = presum(both[:, :, features:])
+        [light_rows],
+    )
+
+    attn_got = swapped(attn_send, 1)
+    attn_send, attn_keep = halves_summed(attn_keep, attn_got)
+    attn_got = swapped(attn_send, 2)
+
+    blocks = [
+        lax.ppermute(grad_raw, "seq", [(owner(i, step), i) for i in range(seq_n)])
+        for step in steps
+    ]
+    blocks = jnp.stack(blocks)
+    blocks = [lax.dynamic_index_in_dim(blocks, (m - part) % PARTS, 0, False) for m in steps]
+    grad_raw = jnp.concatenate(blocks, axis=0)
     head_rows_n = head_width // batch_n
     backs, head_send, head_keep = call(
         functools.partial(heavy_backward, batch_n),
@@ -1111,31 +1251,62 @@
         [],
         4_000_000_000,
         "heavy_backward",
-    )
-    backs = presum(exchange(backs.reshape(seq_n, routed, 2 * features), "seq"))
-
-    head_total = batch_summed(head_send, head_keep)
-    out_grads = head_total[in_rows:, :features].reshape(query_parts, rows, features)
-    out_grads = lax.dynamic_update_slice(
-        jnp.zeros((seq_n, rows, features), BF), out_grads, (part * query_parts, 0, 0)
-    )
-    light_width = wide + features
-    total = jnp.concatenate(
-        [
-            light_total.reshape(seq_n, rows, light_width),
-            head_total[:in_rows].reshape(seq_n, rows, head_all),
-            out_grads,
-        ],
-        axis=2,
-    )
-    total = exchange(total, "seq").astype(F32)
-    grad_light = jnp.sum(total[:, :, :light_width], axis=0)
-    head_grads = total[:, :, light_width:]
-    grad_heavy_out = jnp.sum(head_grads[:, :, head_all:], axis=0)
-    grad_small = jnp.sum(head_grads[:, :, 3 * LANES : head_all], axis=0)
-    grad_heads = head_grads[:, :, : 3 * LANES].reshape(PARTS, query_parts, rows, 3, LANES)
-    grad_heads = jnp.sum(grad_heads, axis=1)[:, :, :, :head_width]
-    grad_heads = grad_heads.transpose(1, 2, 0, 3).reshape(rows, wide)
+        needs=[attn_keep, light_sums],
+    )
+    backs, grad_h_down = call(
+        join_back,
+        (backs, ffn_part, ffn_keep, ffn_got),
+        "vvvv",
+        [((seq_n, routed, 3 * features + 2 * hidden), BF), (heavy_down.shape, F32)],
+        [],
+        10_000_000,
+        "join_back",
+    )
+    backs = exchange(backs, "seq")
+    back_rows = presum(backs[:, :, : 3 * features]) if seq_n > 16 else backs.reshape(keys, -1)
+
+    head_got = swapped(head_send, 1)
+    head_send, head_keep = halves_summed(head_keep, head_got)
+    total, out_grads = call(
+        join_attention,
+        (attn_keep, attn_got, head_keep, swapped(head_send, 2)),
+        "vvvv",
+        [((seq_n, rows, wide + features + head_all), BF), ((out_count, features), BF)],
+        [],
+        10_000_000,
+        "join_attention",
+    )
+    total = exchange(total, "seq")
+    out_grads = out_grads.reshape(query_parts, rows, features)
+    if query_parts == 2:
+        out_send = jnp.where(seq % 2 == 0, out_grads[1], out_grads[0])
+        out_keep = jnp.where(seq % 2 == 0, out_grads[0], out_grads[1])
+        other = lax.ppermute(out_send, "seq", [(i, i ^ 1) for i in range(seq_n)])
+        grad_heavy_out = out_keep.astype(F32) + other.astype(F32)
+    else:
+        out_grads = lax.all_to_all(out_grads, "seq", 0, 0, tiled=True, axis_index_groups=groups)
+        grad_heavy_out = jnp.sum(out_grads.astype(F32), axis=0)
+    grad_light_in, grad_light_down = call(
+        light_results,
+        (light_sums,),
+        "v",
+        [(light_in.shape, F32), (light_down.shape, F32)],
+        [],
+        10_000_000,
+        "light_results",
+    )
+    grad_h_in = call(
+        hidden_results, (backs,), "v", [(heavy_in.shape, F32)], [], 10_000_000, "hidden_results"
+    )[0]
+    grad_light_qkv, grad_light_out, grad_heads, grad_small = call(
+        attention_results,
+        (total,),
+        "v",
+        [(light_qkv.shape, F32), (light_out.shape, F32), (heavy_qkv.shape, F32), ((rows, SMALL), F32)],
+        [],
+        10_000_000,
+        "attention_results",
+    )
 
     from_above = shifted(halo_below, "seq", -1)
     from_below = shifted(halo_above, "seq", 1)
@@ -1148,16 +1319,15 @@
             grad_normed,
             from_below,
             from_above,
-            backs,
+            back_rows,
             picks_t[0],
             picks_t[1],
             picks_t[2],
             middle,
             ffn,
             f_norm,
-            ffn_part,
         ),
-        "v" * 14,
+        "v" * 13,
         [((tokens, features), BF), ((tokens, features), F32)],
         [],
         1_000_000_000,
@@ -1168,12 +1338,12 @@
         input_grad[None],
         grad_small[:, :2],
         grad_small[:, 2:5],
-        grad_light[:, :wide],
-        grad_light[:, wide:],
+        grad_light_qkv,
+        grad_light_out,
         grad_heads,
         grad_heavy_out,
-        shard_f[:, : light_in.shape[1]],
-        unpack_rows(shard_f[:, light_in.shape[1] :], features),
+        grad_light_in,
+        grad_light_down,
         grad_h_in,
         grad_h_down,
     )

time: 404 us -> 425 us (1.052); the launches traced: 397 us -> 424 us
  Pallas kernels: 84.1 us -> 114 us
  other arithmetic: 34.8 us -> 17.3 us
  starting transfers between devices: 83.1 us -> 93 us
  waiting for transfers between devices: 143 us -> 152 us
    ppermute x0 -> x9, waiting for transfers between devices: none -> 44 us  [the longest x4 19.6 us: local(): lax.ppermute(grad_raw, 'seq', [(owner(i, step), i) for i in range(seq_n)])]
    pallas_call x8 -> x16, Pallas kernels: 67.5 us -> 99.5 us  [call(): pl.pallas_call(kernel, out_shape=[jax.ShapeDtypeStruct(shape, kind) for s...]
    all_to_all x9 -> x7, waiting for transfers between devices: 56.9 us -> 25.5 us  [exchange(): return lax.all_to_all(blocks, axis, 0, 0, tiled=True)]
    ppermute x0 -> x9, starting transfers between devices: none -> 23.4 us  [the longest x4 11.6 us: local(): lax.ppermute(block, 'seq', [(i, owner(i, step)) for i in range(seq_n)])]
    all_to_all x9 -> x7, starting transfers between devices: 62.6 us -> 44 us  [exchange(): return lax.all_to_all(blocks, axis, 0, 0, tiled=True)]
    ppermute x4, waiting for transfers between devices: 35.4 us -> 23 us  [shifted(): return lax.ppermute(block, axis, route)]
    concatenate x5 -> x3, other arithmetic: 6.26 us -> 1.45 us  [the longest x1 0.69 us: local(): grad_raw = jnp.concatenate(blocks, axis=0)]
    ppermute x1, waiting for transfers between devices: 0.01 us -> 4.41 us  [local(): other = lax.ppermute(heavy_out, 'seq', [(i, i ^ 1) for i in range(seq_n)])]
  transfers between devices with their start and end apart: 27 -> 34, of which waited for: 10 -> 13; matrix products, arithmetic and copies ran while one was open for 14% -> 8% of each run, Pallas kernels for 19% -> 19%
where the time goes in v2:
time: 425 us; the launch traced here: 424 us
  waiting for transfers between devices  152 us (36%)
  Pallas kernels  114 us (27%)
  starting transfers between devices  93 us (22%)
  local copies, waits for them, and re-layouts  27.3 us (6%)
  other arithmetic  17.3 us (4%)
  between operations  15 us (4%)
  matrix products  5.05 us (1%)
    pallas_call x16, Pallas kernels, call(): pl.pallas_call(kernel, out_shape=[jax.ShapeDtypeStruct(shape, kind) for s...  99.5 us
    ppermute x12, waiting for transfers between devices, swapped(): lax.ppermute(block, 'batch', [(i, i ^ distance) for i in range(lax.axis_s...  55.1 us
    all_to_all x7, starting transfers between devices, exchange(): return lax.all_to_all(blocks, axis, 0, 0, tiled=True)  44 us
    all_to_all x7, waiting for transfers between devices, exchange(): return lax.all_to_all(blocks, axis, 0, 0, tiled=True)  25.5 us
    ppermute x4, waiting for transfers between devices, shifted(): return lax.ppermute(block, axis, route)  23 us
    ppermute x4, waiting for transfers between devices, local(): lax.ppermute(grad_raw, 'seq', [(owner(i, step), i) for i in range(seq_n)])  19.6 us
    ppermute x4, waiting for transfers between devices, local(): lax.ppermute(block, 'seq', [(i, owner(i, step)) for i in range(seq_n)])  19.1 us
    ppermute x4, starting transfers between devices, shifted(): return lax.ppermute(block, axis, route)  15.2 us
  transfers between devices with their start and end apart: 34, of which 13 were waited for; matrix products, arithmetic and copies ran while one was open for 8% of the time, Pallas kernels for 19%

profile of v2, /device:TPU:10, one launch (start us, length us, event | category | flops | bytes accessed | tf_op | source)
XLA Modules:
  0.0 423.7 jit_solution(6863642004819431294)
XLA Ops:
  15.3 6.4 %all-to-all-start = ((bf16[8,32,2432]{2,1,0:T(8,128)(2,1)}), bf16[8,32,2432]{2,1,0:T(8,128)(2,1)S(1)}, u32[]{:S(2)}, u32[]{:S(2)}) async-start(bf16[8,32,2432]{2,1,0:T(8,128)(2,1)} %pad_maximum_fusion), calls=%async_computation | async-start | bytes 2490368 | tf_op jit(solution)/shard_map/all_to_all | solution.py:825
  22.9 4.3 %collective-permute-start.3 = (bf16[128,768]{1,0:T(8,128)(2,1)}, bf16[128,768]{1,0:T(8,128)(2,1)}, u32[]{:S(2)}, u32[]{:S(2)}) collective-permute-start(bf16[128,768]{1,0:T(8,128)(2,1)} %get-tuple-element.148), channel_id=1, source_target_pairs={{0,4},{4,8},{8,12},{12,16},{16,20},{20,24},{24,28},{1,5},{5,9},{9,... | collective-permute-start | bytes 589832 | tf_op jit(solution)/shard_map/ppermute | solution.py:817
  28.2 3.2 stack.88.meta.refs_0_
  31.5 4.4 %collective-permute-done = bf16[24,768]{1,0:T(8,128)(2,1)S(1)} collective-permute-done((bf16[24,768]{1,0:T(8,128)(2,1)S(1)}, bf16[24,768]{1,0:T(8,128)(2,1)S(1)}, u32[]{:S(2)}, u32[]{:S(2)}) %collective-permute-start) | collective-permute-done | bytes 36896 | tf_op jit(solution)/shard_map/ppermute | solution.py:972
  35.9 25.4 %all-to-all-done.refs_2_ = bf16[8,32,2432]{2,1,0:T(8,128)(2,1)S(1)} async-done(((bf16[8,32,2432]{2,1,0:T(8,128)(2,1)}), bf16[8,32,2432]{2,1,0:T(8,128)(2,1)S(1)}, u32[]{:S(2)}, u32[]{:S(2)}) %all-to-all-start) | async-done | bytes 1245216 | tf_op jit(solution)/shard_map/all_to_all | solution.py:825
  64.3 8.4 %collective-permute-done.1 = bf16[240,896]{1,0:T(8,128)(2,1)S(1)} collective-permute-done((bf16[240,896]{1,0:T(8,128)(2,1)S(1)}, bf16[240,896]{1,0:T(8,128)(2,1)S(1)}, u32[]{:S(2)}, u32[]{:S(2)}) %collective-permute-start.1) | collective-permute-done | bytes 430112 | tf_op jit(solution)/shard_map/ppermute | solution.py:821
  76.2 2.2 pack_late.1
  78.3 7.5 %all-to-all-start.2 = ((bf16[8,32,1792]{2,1,0:T(8,128)(2,1)}), bf16[8,32,1792]{2,1,0:T(8,128)(2,1)S(1)}, u32[]{:S(2)}, u32[]{:S(2)}) async-start(bf16[8,32,1792]{2,1,0:T(8,128)(2,1)} %pack_late.1), calls=%async_computation.2 | async-start | bytes 1835008 | tf_op jit(solution)/shard_map/all_to_all | solution.py:825
  90.4 2.5 fusion.1.wx_ref.refs_9_
  92.9 3.5 heavy_forward.1
  97.3 3.4 collective-permute-start.5
  100.7 4.3 %collective-permute-start.6 = (bf16[32,768]{1,0:T(8,128)(2,1)S(1)}, bf16[32,768]{1,0:T(8,128)(2,1)S(1)}, u32[]{:S(2)}, u32[]{:S(2)}) collective-permute-start(bf16[32,768]{1,0:T(8,128)(2,1)S(1)} %get-tuple-element.156), channel_id=1, source_target_pairs={{0,4},{4,20},{8,8},{12,24},{16,12},{20,28},{24,0},{28,16},{1,5},{5... | collective-permute-start | bytes 147464 | tf_op jit(solution)/shard_map/ppermute | solution.py:1038
  105.1 3.9 collective-permute-start.8
  109.7 19.1 %collective-permute-done.5 = bf16[32,768]{1,0:T(8,128)(2,1)S(1)} collective-permute-done((bf16[32,768]{1,0:T(8,128)(2,1)S(1)}, bf16[32,768]{1,0:T(8,128)(2,1)S(1)}, u32[]{:S(2)}, u32[]{:S(2)}) %collective-permute-start.5) | collective-permute-done | bytes 49184 | tf_op jit(solution)/shard_map/ppermute | solution.py:1038
  128.8 4.8 %collective-permute-start.4 = (bf16[128,768]{1,0:T(8,128)(2,1)S(1)}, bf16[128,768]{1,0:T(8,128)(2,1)S(1)}, u32[]{:S(2)}, u32[]{:S(2)}) collective-permute-start(bf16[128,768]{1,0:T(8,128)(2,1)S(1)} %get-tuple-element.147), channel_id=1, source_target_pairs={{4,0},{8,4},{12,8},{16,12},{20,16},{24,20},{28,24},{5,1},{9,5},{13... | collective-permute-start | bytes 589832 | tf_op jit(solution)/shard_map/ppermute | solution.py:817
  136.0 2.3 collective-permute-done.4.above_ref.refs_3_
  139.0 10.7 %light_forward.1 = (bf16[256,768]{1,0:T(8,128)(2,1)}, bf16[512,1536]{1,0:T(8,128)(2,1)}, bf16[256,768]{1,0:T(8,128)(2,1)}, f32[32,768]{1,0:T(8,128)}, f32[256,76...) custom-call(s32[7]{0:T(128)} %stack.88.meta.refs_0_, ...), custom_call_target="tpu_custom_call" | custom-call | flops 8000000000 | bytes 20000000 | tf_op jit(solution)/shard_map/light_forward/pallas_call | solution.py:796
  149.8 23.6 %light_ffn.1 = (f32[256,768]{1,0:T(8,128)}, f32[256,768]{1,0:T(8,128)}, bf16[384,3072]{1,0:T(8,128)(2,1)}, bf16[384,3072]{1,0:T(8,128)(2,1)}) custom-call(bf16[256,768]{1,0:T(8,128)(2,1)} %get-tuple-element.72.normed2_ref, bf16[256,768]{1,0:T(8,128)(2,1)} %bitcast.120, bf16[768,768]{1,0:T(8,128)(2,1)} %convert_convert_fusion.order_ref.refs_4_.refs_9_.refs_11_, ...), custom_call_target="tpu_custom_call" | custom-call | flops 8000000000 | bytes 20000000 | tf_op jit(solution)/shard_map/light_ffn/pallas_call | solution.py:796
  174.3 2.5 in_order.1
  177.3 6.1 %all-to-all-start.1 = ((bf16[8,32,896]{2,1,0:T(8,128)(2,1)}), bf16[8,32,896]{2,1,0:T(8,128)(2,1)}, u32[]{:S(2)}, u32[]{:S(2)}) async-start(bf16[8,32,896]{2,1,0:T(8,128)(2,1)} %bitcast.117), calls=%async_computation.1 | async-start | bytes 917504 | tf_op jit(solution)/shard_map/all_to_all | solution.py:825
  186.9 2.6 convolution_convert_fusion.refs_2_
  189.4 4.6 %pair_sum.4 = (bf16[192,3072]{1,0:T(8,128)(2,1)}, bf16[192,3072]{1,0:T(8,128)(2,1)}) custom-call(bf16[384,3072]{1,0:T(8,128)(2,1)} %get-tuple-element.75.keep_ref, bf16[384,3072]{1,0:T(8,128)(2,1)} %collective-permute-done.11.got_ref), custom_call_target="tpu_custom_call" | custom-call | flops 1179648 | bytes 7077888 | tf_op jit(solution)/shard_map/pair_sum/pallas_call | solution.py:857
  194.0 7.0 %heavy_ffn.1 = (bf16[256,896]{1,0:T(8,128)(2,1)}, bf16[256,768]{1,0:T(8,128)(2,1)}, bf16[640,1024]{1,0:T(8,128)(2,1)}, bf16[640,1024]{1,0:T(8,128)(2,1)}) custom-call(bf16[256,896]{1,0:T(8,128)(2,1)} %bitcast.40.refs_0_, bf16[256,768]{1,0:T(8,128)(2,1)} %bitcast.122, bf16[768,1024]{1,0:T(8,128)(2,1)} %convolution_convert_fusion.refs_2_, ...), custom_call_target="tpu_custom_call" | custom-call | flops 4000000000 | bytes 20000000 | tf_op jit(solution)/shard_map/heavy_ffn/pallas_call | solution.py:796
  202.5 6.5 %all-to-all-start.3 = ((bf16[8,32,896]{2,1,0:T(8,128)(2,1)}), bf16[8,32,896]{2,1,0:T(8,128)(2,1)S(1)}, u32[]{:S(2)}, u32[]{:S(2)}) async-start(bf16[8,32,896]{2,1,0:T(8,128)(2,1)} %bitcast.119), calls=%async_computation.3 | async-start | bytes 917504 | tf_op jit(solution)/shard_map/all_to_all | solution.py:825
  211.4 2.9 pair_sum.5
  214.4 15.2 %collective-permute-done.12.refs_1_ = bf16[192,3072]{1,0:T(8,128)(2,1)S(1)} collective-permute-done((bf16[192,3072]{1,0:T(8,128)(2,1)}, bf16[192,3072]{1,0:T(8,128)(2,1)S(1)}, u32[]{:S(2)}, u32[]{:S(2)}) %collective-permute-start.12) | collective-permute-done | bytes 1179680 | tf_op jit(solution)/shard_map/ppermute | solution.py:821
  230.6 2.9 join_light.1.refs_20_
  234.3 19.9 %light_backward.1 = (f32[256,768]{1,0:T(8,128)}, f32[256,768]{1,0:T(8,128)}, bf16[128,768]{1,0:T(8,128)(2,1)}, bf16[128,768]{1,0:T(8,128)(2,1)}, bf16[32,768]{1,...) custom-call(s32[7]{0:T(128)} %stack.88.meta.refs_0_, ...), custom_call_target="tpu_custom_call" | custom-call | flops 16000000000 | bytes 20000000 | tf_op jit(solution)/shard_map/light_backward/pallas_call | solution.py:796
  254.3 6.5 %all-to-all-start.4 = ((bf16[8,24,3072]{2,1,0:T(8,128)(2,1)}), bf16[8,24,3072]{2,1,0:T(8,128)(2,1)S(1)}, u32[]{:S(2)}, u32[]{:S(2)}) async-start(bf16[8,24,3072]{2,1,0:T(8,128)(2,1)} %join_light.1.refs_20_), calls=%async_computation.4 | async-start | bytes 2359296 | tf_op jit(solution)/shard_map/all_to_all | solution.py:825
  261.1 4.3 %collective-permute-start.16 = (bf16[32,768]{1,0:T(8,128)(2,1)}, bf16[32,768]{1,0:T(8,128)(2,1)}, u32[]{:S(2)}, u32[]{:S(2)}) collective-permute-start(bf16[32,768]{1,0:T(8,128)(2,1)} %get-tuple-element.87), channel_id=1, source_target_pairs={{0,0},{16,4},{4,8},{20,12},{8,16},{24,20},{12,24},{28,28},{1,1},{1... | collective-permute-start | bytes 147464 | tf_op jit(solution)/shard_map/ppermute | solution.py:1221
  265.4 2.5 collective-permute-start.17
  267.9 4.4 %collective-permute-start.19 = (bf16[32,768]{1,0:T(8,128)(2,1)}, bf16[32,768]{1,0:T(8,128)(2,1)}, u32[]{:S(2)}, u32[]{:S(2)}) collective-permute-start(bf16[32,768]{1,0:T(8,128)(2,1)} %get-tuple-element.87), channel_id=1, source_target_pairs={{12,0},{28,4},{0,8},{16,12},{4,16},{20,20},{8,24},{24,28},{13,1},{... | collective-permute-start | bytes 147464 | tf_op jit(solution)/shard_map/ppermute | solution.py:1221
  273.0 19.6 %collective-permute-done.16 = bf16[32,768]{1,0:T(8,128)(2,1)} collective-permute-done((bf16[32,768]{1,0:T(8,128)(2,1)}, bf16[32,768]{1,0:T(8,128)(2,1)}, u32[]{:S(2)}, u32[]{:S(2)}) %collective-permute-start.16) | collective-permute-done | bytes 49184 | tf_op jit(solution)/shard_map/ppermute | solution.py:1221
  297.1 4.6 %pair_sum.6 = (bf16[192,3072]{1,0:T(8,128)(2,1)}, bf16[192,3072]{1,0:T(8,128)(2,1)}) custom-call(bf16[384,3072]{1,0:T(8,128)(2,1)} %get-tuple-element.92.keep_ref, bf16[384,3072]{1,0:T(8,128)(2,1)} %copy-done.8), custom_call_target="tpu_custom_call" | custom-call | flops 1179648 | bytes 7077888 | tf_op jit(solution)/shard_map/pair_sum/pallas_call | solution.py:857
  302.8 6.6 %heavy_backward.1 = (bf16[256,1536]{1,0:T(8,128)(2,1)}, bf16[480,896]{1,0:T(8,128)(2,1)}, bf16[480,896]{1,0:T(8,128)(2,1)}) custom-call(s32[7]{0:T(128)} %stack.88.meta.refs_0_, bf16[128,768]{1,0:T(8,128)(2,1)} %constant_dynamic-slice_fusion.xq_ref.refs_1_, bf16[256,768]{1,0:T(8,128)(2,1)} %bitcast.124, bf16[128,768]{1,0:T(8,128)(2,1)} %pad_maximum_fusion.3.refs_3_, ...), custom_call_target="tpu_custom_call" | custom-call | flops 4000000000 | bytes 20000000 | tf_op jit(solution)/shard_map/heavy_backward/pallas_call | solution.py:796
  309.4 3.0 join_back.1
  312.4 4.8 %all-to-all-start.5 = ((bf16[8,32,3328]{2,1,0:T(8,128)(2,1)}), bf16[8,32,3328]{2,1,0:T(8,128)(2,1)S(1)}, u32[]{:S(2)}, u32[]{:S(2)}) async-start(bf16[8,32,3328]{2,1,0:T(8,128)(2,1)} %get-tuple-element.98), calls=%async_computation.5 | async-start | bytes 3407872 | tf_op jit(solution)/shard_map/all_to_all | solution.py:825
  320.7 2.4 pair_sum.7
  324.6 21.5 %collective-permute-done.22.got_ref = bf16[192,3072]{1,0:T(8,128)(2,1)S(1)} collective-permute-done((bf16[192,3072]{1,0:T(8,128)(2,1)}, bf16[192,3072]{1,0:T(8,128)(2,1)S(1)}, u32[]{:S(2)}, u32[]{:S(2)}) %collective-permute-start.22) | collective-permute-done | bytes 1179680 | tf_op jit(solution)/shard_map/ppermute | solution.py:821
  346.1 8.8 %collective-permute-done.24.head_got_ref = bf16[240,896]{1,0:T(8,128)(2,1)S(1)} collective-permute-done((bf16[240,896]{1,0:T(8,128)(2,1)}, bf16[240,896]{1,0:T(8,128)(2,1)S(1)}, u32[]{:S(2)}, u32[]{:S(2)}) %collective-permute-start.24) | collective-permute-done | bytes 430112 | tf_op jit(solution)/shard_map/ppermute | solution.py:821
  355.7 3.3 join_attention.1
  359.1 6.1 %all-to-all-start.6 = ((bf16[8,24,3968]{2,1,0:T(8,128)(2,1)}), bf16[8,24,3968]{2,1,0:T(8,128)(2,1)S(1)}, u32[]{:S(2)}, u32[]{:S(2)}) async-start(bf16[8,24,3968]{2,1,0:T(8,128)(2,1)} %get-tuple-element.107), calls=%async_computation.6 | async-start | bytes 3047424 | tf_op jit(solution)/shard_map/all_to_all | solution.py:825
  366.6 4.3 %collective-permute-start.14 = (bf16[128,768]{1,0:T(8,128)(2,1)}, bf16[128,768]{1,0:T(8,128)(2,1)S(1)}, u32[]{:S(2)}, u32[]{:S(2)}) collective-permute-start(bf16[128,768]{1,0:T(8,128)(2,1)} %get-tuple-element.85), channel_id=1, source_target_pairs={{0,4},{4,8},{8,12},{12,16},{16,20},{20,24},{24,28},{1,5},{5,9},{9,... | collective-permute-start | bytes 589832 | tf_op jit(solution)/shard_map/ppermute | solution.py:817
  374.8 5.3 %collective-permute-done.25 = bf16[24,768]{1,0:T(8,128)(2,1)S(1)} collective-permute-done((bf16[24,768]{1,0:T(8,128)(2,1)S(1)}, bf16[24,768]{1,0:T(8,128)(2,1)S(1)}, u32[]{:S(2)}, u32[]{:S(2)}) %collective-permute-start.25) | collective-permute-done | bytes 36896 | tf_op jit(solution)/shard_map/ppermute | solution.py:1284
  380.8 2.4 hidden_results.1
  383.2 18.9 %collective-permute-done.14.from_below_ref = bf16[128,768]{1,0:T(8,128)(2,1)S(1)} collective-permute-done((bf16[128,768]{1,0:T(8,128)(2,1)}, bf16[128,768]{1,0:T(8,128)(2,1)S(1)}, u32[]{:S(2)}, u32[]{:S(2)}) %collective-permute-start.14) | collective-permute-done | bytes 196640 | tf_op jit(solution)/shard_map/ppermute | solution.py:817
  404.5 5.8 %finish.1 = (bf16[256,768]{1,0:T(8,128)(2,1)}, f32[256,768]{1,0:T(8,128)}) custom-call(bf16[256,768]{1,0:T(8,128)(2,1)} %bitcast.104, f32[8,768]{1,0:T(8,128)} %get-tuple-element.64.small_ref.refs_16_.refs_7_, f32[256,768]{1,0:T(8,128)} %get-tuple-element.83.grad_middle_ref, f32[256,768]{1,0:T(8,128)} %get-tuple-element.84.grad_normed_ref, ...), custom_call_target="tpu_custom_call" | custom-call | flops 1000000000 | bytes 20000000 | tf_op jit(solution)/shard_map/finish/pallas_call | solution.py:796
  411.5 2.3 attention_results.1
  (201 shorter events, 61.1 us)
Async XLA Ops:
  7.2 131.1 %all-gather.2.cloned.1.call-start = ((), (), s32[]{:S(2)}) async-start(), calls=%async_computation.7 | async-start | bytes 9732096 | tf_op jit(solution)/shard_map/all_gather | solution.py:945
  15.3 11.9 %copy-start.39 = (s32[1,4]{1,0:T(1,128)S(1)}, s32[1,4]{1,0:T(1,128)}, u32[]{:S(2)}) copy-start(s32[1,4]{1,0:T(1,128)} %param.23) | copy-start | bytes 52
  15.3 12.2 %copy-start.23 = (s32[2,2,8,24]{3,2,1,0:T(8,128)S(1)}, s32[2,2,8,24]{3,2,1,0:T(8,128)}, u32[]{:S(2)}) copy-start(s32[2,2,8,24]{3,2,1,0:T(8,128)} %constant.142.clone) | copy-start | bytes 9220
  15.3 12.2 %copy-start.24 = (s32[2,2,8,24]{3,2,1,0:T(8,128)S(1)}, s32[2,2,8,24]{3,2,1,0:T(8,128)}, u32[]{:S(2)}) copy-start(s32[2,2,8,24]{3,2,1,0:T(8,128)} %constant.143.clone) | copy-start | bytes 9220
  15.3 46.0 %all-to-all-start = ((bf16[8,32,2432]{2,1,0:T(8,128)(2,1)}), bf16[8,32,2432]{2,1,0:T(8,128)(2,1)S(1)}, u32[]{:S(2)}, u32[]{:S(2)}) async-start(bf16[8,32,2432]{2,1,0:T(8,128)(2,1)} %pad_maximum_fusion), calls=%async_computation | async-start | bytes 2490368 | tf_op jit(solution)/shard_map/all_to_all | solution.py:825
  21.6 14.2 %collective-permute-start = (bf16[24,768]{1,0:T(8,128)(2,1)S(1)}, bf16[24,768]{1,0:T(8,128)(2,1)S(1)}, u32[]{:S(2)}, u32[]{:S(2)}) collective-permute-start(bf16[24,768]{1,0:T(8,128)(2,1)S(1)} %copy-done.22), channel_id=1, source_target_pairs={{0,4},{4,0},{8,12},{12,8},{16,20},{20,16},{24,28},{28,24},{1,5},{5... | collective-permute-start | bytes 110600 | tf_op jit(solution)/shard_map/ppermute | solution.py:972
  22.9 113.1 %collective-permute-start.3 = (bf16[128,768]{1,0:T(8,128)(2,1)}, bf16[128,768]{1,0:T(8,128)(2,1)}, u32[]{:S(2)}, u32[]{:S(2)}) collective-permute-start(bf16[128,768]{1,0:T(8,128)(2,1)} %get-tuple-element.148), channel_id=1, source_target_pairs={{0,4},{4,8},{8,12},{12,16},{16,20},{20,24},{24,28},{1,5},{5,9},{9,... | collective-permute-start | bytes 589832 | tf_op jit(solution)/shard_map/ppermute | solution.py:817
  61.3 12.5 %copy-start.1 = (bf16[8,32,2432]{2,1,0:T(8,128)(2,1)}, bf16[8,32,2432]{2,1,0:T(8,128)(2,1)S(1)}, u32[]{:S(2)}) copy-start(bf16[8,32,2432]{2,1,0:T(8,128)(2,1)S(1)} %all-to-all-done.refs_2_) | copy-start | bytes 3735556
  61.4 12.5 %copy-start.16 = (bf16[1,256,768]{2,1,0:T(8,128)(2,1)S(1)}, bf16[1,256,768]{2,1,0:T(8,128)(2,1)}, u32[]{:S(2)}) copy-start(bf16[1,256,768]{2,1,0:T(8,128)(2,1)} %param.22) | copy-start | bytes 1179652
  61.5 11.2 %collective-permute-start.1 = (bf16[240,896]{1,0:T(8,128)(2,1)S(1)}, bf16[240,896]{1,0:T(8,128)(2,1)S(1)}, u32[]{:S(2)}, u32[]{:S(2)}) collective-permute-start(bf16[240,896]{1,0:T(8,128)(2,1)S(1)} %get-tuple-element.146), channel_id=1, source_target_pairs={{0,2},{1,3},{2,0},{3,1},{4,6},{5,7},{6,4},{7,5},{8,10},{9,11},{10,... | collective-permute-start | bytes 1290248 | tf_op jit(solution)/shard_map/ppermute | solution.py:821
  63.6 9.1 %copy-start.30 = (s32[32]{0:T(128)}, s32[32]{0:T(128)S(1)}, u32[]{:S(2)}) copy-start(s32[32]{0:T(128)S(1)} %get-tuple-element.162) | copy-start | bytes 388
  63.6 45.4 %copy-start.28 = (s32[32]{0:T(128)}, s32[32]{0:T(128)S(1)}, u32[]{:S(2)}) copy-start(s32[32]{0:T(128)S(1)} %get-tuple-element.161) | copy-start | bytes 388
  73.8 13.7 %collective-permute-start.2 = (bf16[2,240,896]{2,1,0:T(8,128)(2,1)}, bf16[2,240,896]{2,1,0:T(8,128)(2,1)}, u32[]{:S(2)}, u32[]{:S(2)}) collective-permute-start(bf16[2,240,896]{2,1,0:T(8,128)(2,1)} %maximum_select_fusion.3), channel_id=1, source_target_pairs={{0,1},{1,0},{2,3},{3,2},{4,5},{5,4},{6,7},{7,6},{8,9},{9,8},{10,11... | collective-permute-start | bytes 2580488 | tf_op jit(solution)/shard_map/ppermute | solution.py:821
  76.2 9.7 %copy-start.2 = (bf16[8,32,2432]{2,1,0:T(8,128)(2,1)S(1)}, bf16[8,32,2432]{2,1,0:T(8,128)(2,1)}, u32[]{:S(2)}) copy-start(bf16[8,32,2432]{2,1,0:T(8,128)(2,1)} %copy-done.1) | copy-start | bytes 3735556
  78.3 56.0 %all-to-all-start.2 = ((bf16[8,32,1792]{2,1,0:T(8,128)(2,1)}), bf16[8,32,1792]{2,1,0:T(8,128)(2,1)S(1)}, u32[]{:S(2)}, u32[]{:S(2)}) async-start(bf16[8,32,1792]{2,1,0:T(8,128)(2,1)} %pack_late.1), calls=%async_computation.2 | async-start | bytes 1835008 | tf_op jit(solution)/shard_map/all_to_all | solution.py:825
  96.4 38.0 %copy-start.20 = (bf16[128,768]{1,0:T(8,128)(2,1)S(1)}, bf16[128,768]{1,0:T(8,128)(2,1)}, u32[]{:S(2)}) copy-start(bf16[128,768]{1,0:T(8,128)(2,1)} %param.34) | copy-start | bytes 589828
  97.3 31.5 %collective-permute-start.5 = (bf16[32,768]{1,0:T(8,128)(2,1)S(1)}, bf16[32,768]{1,0:T(8,128)(2,1)S(1)}, u32[]{:S(2)}, u32[]{:S(2)}) collective-permute-start(bf16[32,768]{1,0:T(8,128)(2,1)S(1)} %get-tuple-element.153), channel_id=1, source_target_pairs={{0,0},{4,16},{8,4},{12,20},{16,8},{20,24},{24,12},{28,28},{1,1},{5... | collective-permute-start | bytes 147464 | tf_op jit(solution)/shard_map/ppermute | solution.py:1038
  100.7 32.9 %collective-permute-start.6 = (bf16[32,768]{1,0:T(8,128)(2,1)S(1)}, bf16[32,768]{1,0:T(8,128)(2,1)S(1)}, u32[]{:S(2)}, u32[]{:S(2)}) collective-permute-start(bf16[32,768]{1,0:T(8,128)(2,1)S(1)} %get-tuple-element.156), channel_id=1, source_target_pairs={{0,4},{4,20},{8,8},{12,24},{16,12},{20,28},{24,0},{28,16},{1,5},{5... | collective-permute-start | bytes 147464 | tf_op jit(solution)/shard_map/ppermute | solution.py:1038
  105.0 28.6 %collective-permute-start.7 = (bf16[32,768]{1,0:T(8,128)(2,1)S(1)}, bf16[32,768]{1,0:T(8,128)(2,1)S(1)}, u32[]{:S(2)}, u32[]{:S(2)}) collective-permute-start(bf16[32,768]{1,0:T(8,128)(2,1)S(1)} %get-tuple-element.155), channel_id=1, source_target_pairs={{0,8},{4,24},{8,12},{12,28},{16,0},{20,16},{24,4},{28,20},{1,9},{5... | collective-permute-start | bytes 147464 | tf_op jit(solution)/shard_map/ppermute | solution.py:1038
  105.1 28.6 %collective-permute-start.8 = (bf16[32,768]{1,0:T(8,128)(2,1)S(1)}, bf16[32,768]{1,0:T(8,128)(2,1)S(1)}, u32[]{:S(2)}, u32[]{:S(2)}) collective-permute-start(bf16[32,768]{1,0:T(8,128)(2,1)S(1)} %get-tuple-element.154), channel_id=1, source_target_pairs={{0,12},{4,28},{8,0},{12,16},{16,4},{20,20},{24,8},{28,24},{1,13},{... | collective-permute-start | bytes 147464 | tf_op jit(solution)/shard_map/ppermute | solution.py:1038
  128.8 9.5 %collective-permute-start.4 = (bf16[128,768]{1,0:T(8,128)(2,1)S(1)}, bf16[128,768]{1,0:T(8,128)(2,1)S(1)}, u32[]{:S(2)}, u32[]{:S(2)}) collective-permute-start(bf16[128,768]{1,0:T(8,128)(2,1)S(1)} %get-tuple-element.147), channel_id=1, source_target_pairs={{4,0},{8,4},{12,8},{16,12},{20,16},{24,20},{28,24},{5,1},{9,5},{13... | collective-permute-start | bytes 589832 | tf_op jit(solution)/shard_map/ppermute | solution.py:817
  134.5 15.3 %copy-start.7 = (bf16[320,1024]{1,0:T(8,128)(2,1)}, bf16[320,1024]{1,0:T(8,128)(2,1)S(1)}, u32[]{:S(2)}) copy-start(bf16[320,1024]{1,0:T(8,128)(2,1)S(1)} %fusion.11.refs_1_) | copy-start | bytes 1966084
  134.5 39.0 %collective-permute-start.9 = (bf16[320,1024]{1,0:T(8,128)(2,1)S(1)}, bf16[320,1024]{1,0:T(8,128)(2,1)S(1)}, u32[]{:S(2)}, u32[]{:S(2)}) collective-permute-start(bf16[320,1024]{1,0:T(8,128)(2,1)S(1)} %fusion.11.refs_1_), channel_id=1, source_target_pairs={{0,2},{1,3},{2,0},{3,1},{4,6},{5,7},{6,4},{7,5},{8,10},{9,11},{10,... | collective-permute-start | bytes 1966088 | tf_op jit(solution)/shard_map/ppermute | solution.py:821
  173.3 16.1 %collective-permute-start.11 = (bf16[384,3072]{1,0:T(8,128)(2,1)}, bf16[384,3072]{1,0:T(8,128)(2,1)}, u32[]{:S(2)}, u32[]{:S(2)}) collective-permute-start(bf16[384,3072]{1,0:T(8,128)(2,1)} %get-tuple-element.76), channel_id=1, source_target_pairs={{0,1},{1,0},{2,3},{3,2},{4,5},{5,4},{6,7},{7,6},{8,9},{9,8},{10,11... | collective-permute-start | bytes 7077896 | tf_op jit(solution)/shard_map/ppermute | solution.py:821
  176.7 8.3 %collective-permute-start.10 = (bf16[2,320,1024]{2,1,0:T(8,128)(2,1)}, bf16[2,320,1024]{2,1,0:T(8,128)(2,1)S(1)}, u32[]{:S(2)}, u32[]{:S(2)}) collective-permute-start(bf16[2,320,1024]{2,1,0:T(8,128)(2,1)} %in_order.1), channel_id=1, source_target_pairs={{0,1},{1,0},{2,3},{3,2},{4,5},{5,4},{6,7},{7,6},{8,9},{9,8},{10,11... | collective-permute-start | bytes 3932168 | tf_op jit(solution)/shard_map/ppermute | solution.py:821
  177.3 16.7 %all-to-all-start.1 = ((bf16[8,32,896]{2,1,0:T(8,128)(2,1)}), bf16[8,32,896]{2,1,0:T(8,128)(2,1)}, u32[]{:S(2)}, u32[]{:S(2)}) async-start(bf16[8,32,896]{2,1,0:T(8,128)(2,1)} %bitcast.117), calls=%async_computation.1 | async-start | bytes 917504 | tf_op jit(solution)/shard_map/all_to_all | solution.py:825
  194.0 15.1 %copy-start.31 = (s32[32]{0:T(128)S(1)}, s32[32]{0:T(128)}, u32[]{:S(2)}) copy-start(s32[32]{0:T(128)} %copy-done.30) | copy-start | bytes 388
  194.0 15.7 %copy-start.29 = (s32[32]{0:T(128)S(1)}, s32[32]{0:T(128)}, u32[]{:S(2)}) copy-start(s32[32]{0:T(128)} %copy-done.28) | copy-start | bytes 388
  201.0 9.4 %collective-permute-start.13 = (bf16[640,1024]{1,0:T(8,128)(2,1)}, bf16[640,1024]{1,0:T(8,128)(2,1)S(1)}, u32[]{:S(2)}, u32[]{:S(2)}) collective-permute-start(bf16[640,1024]{1,0:T(8,128)(2,1)} %get-tuple-element.81), channel_id=1, source_target_pairs={{0,1},{1,0},{2,3},{3,2},{4,5},{5,4},{6,7},{7,6},{8,9},{9,8},{10,11... | collective-permute-start | bytes 3932168 | tf_op jit(solution)/shard_map/ppermute | solution.py:821
  201.0 28.6 %collective-permute-start.12 = (bf16[192,3072]{1,0:T(8,128)(2,1)}, bf16[192,3072]{1,0:T(8,128)(2,1)S(1)}, u32[]{:S(2)}, u32[]{:S(2)}) collective-permute-start(bf16[192,3072]{1,0:T(8,128)(2,1)} %get-tuple-element.79), channel_id=1, source_target_pairs={{0,2},{1,3},{2,0},{3,1},{4,6},{5,7},{6,4},{7,5},{8,10},{9,11},{10,... | collective-permute-start | bytes 3538952 | tf_op jit(solution)/shard_map/ppermute | solution.py:821
  202.5 31.0 %all-to-all-start.3 = ((bf16[8,32,896]{2,1,0:T(8,128)(2,1)}), bf16[8,32,896]{2,1,0:T(8,128)(2,1)S(1)}, u32[]{:S(2)}, u32[]{:S(2)}) async-start(bf16[8,32,896]{2,1,0:T(8,128)(2,1)} %bitcast.119), calls=%async_computation.3 | async-start | bytes 917504 | tf_op jit(solution)/shard_map/all_to_all | solution.py:825
  254.3 41.5 %collective-permute-start.20 = (bf16[384,3072]{1,0:T(8,128)(2,1)}, bf16[384,3072]{1,0:T(8,128)(2,1)S(1)}, u32[]{:S(2)}, u32[]{:S(2)}) collective-permute-start(bf16[384,3072]{1,0:T(8,128)(2,1)} %get-tuple-element.93), channel_id=1, source_target_pairs={{0,1},{1,0},{2,3},{3,2},{4,5},{5,4},{6,7},{7,6},{8,9},{9,8},{10,11... | collective-permute-start | bytes 7077896 | tf_op jit(solution)/shard_map/ppermute | solution.py:821
  254.3 47.4 %all-to-all-start.4 = ((bf16[8,24,3072]{2,1,0:T(8,128)(2,1)}), bf16[8,24,3072]{2,1,0:T(8,128)(2,1)S(1)}, u32[]{:S(2)}, u32[]{:S(2)}) async-start(bf16[8,24,3072]{2,1,0:T(8,128)(2,1)} %join_light.1.refs_20_), calls=%async_computation.4 | async-start | bytes 2359296 | tf_op jit(solution)/shard_map/all_to_all | solution.py:825
  261.1 31.5 %collective-permute-start.16 = (bf16[32,768]{1,0:T(8,128)(2,1)}, bf16[32,768]{1,0:T(8,128)(2,1)}, u32[]{:S(2)}, u32[]{:S(2)}) collective-permute-start(bf16[32,768]{1,0:T(8,128)(2,1)} %get-tuple-element.87), channel_id=1, source_target_pairs={{0,0},{16,4},{4,8},{20,12},{8,16},{24,20},{12,24},{28,28},{1,1},{1... | collective-permute-start | bytes 147464 | tf_op jit(solution)/shard_map/ppermute | solution.py:1221
  265.4 28.7 %collective-permute-start.17 = (bf16[32,768]{1,0:T(8,128)(2,1)}, bf16[32,768]{1,0:T(8,128)(2,1)}, u32[]{:S(2)}, u32[]{:S(2)}) collective-permute-start(bf16[32,768]{1,0:T(8,128)(2,1)} %get-tuple-element.87), channel_id=1, source_target_pairs={{4,0},{20,4},{8,8},{24,12},{12,16},{28,20},{0,24},{16,28},{5,1},{2... | collective-permute-start | bytes 147464 | tf_op jit(solution)/shard_map/ppermute | solution.py:1221
  267.8 26.2 %collective-permute-start.18 = (bf16[32,768]{1,0:T(8,128)(2,1)}, bf16[32,768]{1,0:T(8,128)(2,1)}, u32[]{:S(2)}, u32[]{:S(2)}) collective-permute-start(bf16[32,768]{1,0:T(8,128)(2,1)} %get-tuple-element.87), channel_id=1, source_target_pairs={{8,0},{24,4},{12,8},{28,12},{0,16},{16,20},{4,24},{20,28},{9,1},{2... | collective-permute-start | bytes 147464 | tf_op jit(solution)/shard_map/ppermute | solution.py:1221
  267.9 26.2 %collective-permute-start.19 = (bf16[32,768]{1,0:T(8,128)(2,1)}, bf16[32,768]{1,0:T(8,128)(2,1)}, u32[]{:S(2)}, u32[]{:S(2)}) collective-permute-start(bf16[32,768]{1,0:T(8,128)(2,1)} %get-tuple-element.87), channel_id=1, source_target_pairs={{12,0},{28,4},{0,8},{16,12},{4,16},{20,20},{8,24},{24,28},{13,1},{... | collective-permute-start | bytes 147464 | tf_op jit(solution)/shard_map/ppermute | solution.py:1221
  292.6 16.8 %collective-permute-start.21 = (bf16[320,1024]{1,0:T(8,128)(2,1)}, bf16[320,1024]{1,0:T(8,128)(2,1)}, u32[]{:S(2)}, u32[]{:S(2)}) collective-permute-start(bf16[320,1024]{1,0:T(8,128)(2,1)} %get-tuple-element.97), channel_id=1, source_target_pairs={{0,2},{1,3},{2,0},{3,1},{4,6},{5,7},{6,4},{7,5},{8,10},{9,11},{10,... | collective-permute-start | bytes 1966088 | tf_op jit(solution)/shard_map/ppermute | solution.py:821
  312.4 46.7 %all-to-all-start.5 = ((bf16[8,32,3328]{2,1,0:T(8,128)(2,1)}), bf16[8,32,3328]{2,1,0:T(8,128)(2,1)S(1)}, u32[]{:S(2)}, u32[]{:S(2)}) async-start(bf16[8,32,3328]{2,1,0:T(8,128)(2,1)} %get-tuple-element.98), calls=%async_computation.5 | async-start | bytes 3407872 | tf_op jit(solution)/shard_map/all_to_all | solution.py:825
  317.1 2.6 collective-permute-start.23
  317.2 29.0 %collective-permute-start.22 = (bf16[192,3072]{1,0:T(8,128)(2,1)}, bf16[192,3072]{1,0:T(8,128)(2,1)S(1)}, u32[]{:S(2)}, u32[]{:S(2)}) collective-permute-start(bf16[192,3072]{1,0:T(8,128)(2,1)} %get-tuple-element.102), channel_id=1, source_target_pairs={{0,2},{1,3},{2,0},{3,1},{4,6},{5,7},{6,4},{7,5},{8,10},{9,11},{10,... | collective-permute-start | bytes 3538952 | tf_op jit(solution)/shard_map/ppermute | solution.py:821
  323.1 31.8 %collective-permute-start.24 = (bf16[240,896]{1,0:T(8,128)(2,1)}, bf16[240,896]{1,0:T(8,128)(2,1)S(1)}, u32[]{:S(2)}, u32[]{:S(2)}) collective-permute-start(bf16[240,896]{1,0:T(8,128)(2,1)} %get-tuple-element.106), channel_id=1, source_target_pairs={{0,2},{1,3},{2,0},{3,1},{4,6},{5,7},{6,4},{7,5},{8,10},{9,11},{10,... | collective-permute-start | bytes 1290248 | tf_op jit(solution)/shard_map/ppermute | solution.py:821
  346.1 8.8 %copy-start.10 = (bf16[192,3072]{1,0:T(8,128)(2,1)}, bf16[192,3072]{1,0:T(8,128)(2,1)S(1)}, u32[]{:S(2)}) copy-start(bf16[192,3072]{1,0:T(8,128)(2,1)S(1)} %collective-permute-done.22.got_ref) | copy-start | bytes 3538948
  359.1 11.7 %copy-start.37 = (bf16[128,768]{1,0:T(8,128)(2,1)S(1)}, bf16[128,768]{1,0:T(8,128)(2,1)}, u32[]{:S(2)}) copy-start(bf16[128,768]{1,0:T(8,128)(2,1)} %get-tuple-element.86) | copy-start | bytes 589828
  359.1 51.3 %all-to-all-start.6 = ((bf16[8,24,3968]{2,1,0:T(8,128)(2,1)}), bf16[8,24,3968]{2,1,0:T(8,128)(2,1)S(1)}, u32[]{:S(2)}, u32[]{:S(2)}) async-start(bf16[8,24,3968]{2,1,0:T(8,128)(2,1)} %get-tuple-element.107), calls=%async_computation.6 | async-start | bytes 3047424 | tf_op jit(solution)/shard_map/all_to_all | solution.py:825
  365.3 14.9 %collective-permute-start.25 = (bf16[24,768]{1,0:T(8,128)(2,1)S(1)}, bf16[24,768]{1,0:T(8,128)(2,1)S(1)}, u32[]{:S(2)}, u32[]{:S(2)}) collective-permute-start(bf16[24,768]{1,0:T(8,128)(2,1)S(1)} %broadcast_select_fusion), channel_id=1, source_target_pairs={{0,4},{4,0},{8,12},{12,8},{16,20},{20,16},{24,28},{28,24},{1,5},{5... | collective-permute-start | bytes 110600 | tf_op jit(solution)/shard_map/ppermute | solution.py:1284
  366.6 35.5 %collective-permute-start.14 = (bf16[128,768]{1,0:T(8,128)(2,1)}, bf16[128,768]{1,0:T(8,128)(2,1)S(1)}, u32[]{:S(2)}, u32[]{:S(2)}) collective-permute-start(bf16[128,768]{1,0:T(8,128)(2,1)} %get-tuple-element.85), channel_id=1, source_target_pairs={{0,4},{4,8},{8,12},{12,16},{16,20},{20,24},{24,28},{1,5},{5,9},{9,... | collective-permute-start | bytes 589832 | tf_op jit(solution)/shard_map/ppermute | solution.py:817
  370.8 33.0 %collective-permute-start.15 = (bf16[128,768]{1,0:T(8,128)(2,1)S(1)}, bf16[128,768]{1,0:T(8,128)(2,1)S(1)}, u32[]{:S(2)}, u32[]{:S(2)}) collective-permute-start(bf16[128,768]{1,0:T(8,128)(2,1)S(1)} %copy-done.37), channel_id=1, source_target_pairs={{4,0},{8,4},{12,8},{16,12},{20,16},{24,20},{28,24},{5,1},{9,5},{13... | collective-permute-start | bytes 589832 | tf_op jit(solution)/shard_map/ppermute | solution.py:817
  (28 other events, 82.1 us)
Sparse Core Ops, SparseCore 0:
  11.5 115.2 all-gather.1

commit v3 on v2

--- a/solution.py
+++ b/solution.py
@@ -184,7 +184,8 @@
     probs = softmax(nt(stacked, kv_ref[:, :LANES]) * DH ** (-0.5) + bias)
     mixed = low(merge_heads(nn(low(probs), kv_ref[:, LANES:]), masks))
     mixed_ref[...] = mixed
-    raw_ref[...] = low(nn(mixed, out_ref[...]))
+    raw_ref[...] = jnp.zeros_like(raw_ref)
+    raw_ref[pl.ds(pl.multiple_of(meta[6], count), count)] = low(nn(mixed, out_ref[...]))
 
 
 def light_forward(
@@ -193,36 +194,21 @@
     below_ref,
     x_ref,
     above_ref,
-    xq_ref,
-    raw_ref,
-    pq_t_ref,
-    pf_ref,
     small_ref,
     full_ref,
     q_ref,
     kv_ref,
     mixed_ref,
-    heavy_raw_ref,
-    middle_ref,
-    normed2_ref,
-    f_norm_ref,
-    f_sent_ref,
+    base_ref,
     w_qkv,
     w_lo,
     sems,
 ):
     tokens, features = x_ref.shape
-    routed = xq_ref.shape[0]
     copies = load(full_ref, [(layout["light_qkv"], w_qkv), (layout["light_out"], w_lo)], sems)
-    small = small_ref[...]
-    gain_1, gain_2 = small[0:1], small[1:2]
+    gain_1 = small_ref[0:1]
     xe = jnp.concatenate([below_ref[...], x_ref[...], above_ref[...]], axis=0).astype(F32)
     ne = low(xe * rms_inverse(xe) * gain_1)
-    xq = xq_ref[...].astype(F32)
-    q_gate = sigmoid_dot(xq * rms_inverse(xq) * gain_1, small[2:3])
-    heavy_raw = sum_blocks(raw_ref, routed)
-    heavy_raw_ref[...] = heavy_raw
-    base = x_ref[...].astype(F32) + exact(pq_t_ref[...], heavy_raw * q_gate)
     copies[0].wait()
     q_ref[...] = low(nn(ne[WIN : WIN + tokens], w_qkv[:, :features]))
     kv_ref[...] = low(nn(ne, w_qkv[:, features:]))
@@ -239,7 +225,30 @@
         values = kv_ref[key_rows, features + part * width : features + (part + 1) * width]
         mixed_ref[rows, cols] = low(merge_heads(nn(low(probs), values), masks))
     copies[1].wait()
-    middle = base + nn(mixed_ref[...], w_lo[...])
+    base_ref[...] = x_ref[...].astype(F32) + nn(mixed_ref[...], w_lo[...])
+
+
+def second_norm(
+    base_ref,
+    xq_ref,
+    raw_ref,
+    pq_t_ref,
+    pf_ref,
+    small_ref,
+    heavy_raw_ref,
+    middle_ref,
+    normed2_ref,
+    f_norm_ref,
+    f_sent_ref,
+):
+    routed = xq_ref.shape[0]
+    small = small_ref[...]
+    gain_1, gain_2 = small[0:1], small[1:2]
+    xq = xq_ref[...].astype(F32)
+    q_gate = sigmoid_dot(xq * rms_inverse(xq) * gain_1, small[2:3])
+    heavy_raw = sum_blocks(raw_ref, routed)
+    heavy_raw_ref[...] = heavy_raw
+    middle = base_ref[...] + exact(pq_t_ref[...], heavy_raw * q_gate)
     middle_ref[...] = middle
     normed2 = middle * rms_inverse(middle) * gain_2
     normed2_ref[...] = low(normed2)
@@ -363,11 +372,9 @@
     in_ref,
     down_ref,
     order_ref,
-    order_units_ref,
     back_ref,
     ffn_ref,
-    send_ref,
-    keep_ref,
+    grads_ref,
 ):
     features = in_ref.shape[0]
     hidden_n = down_ref.shape[0]
@@ -385,8 +392,7 @@
     back_ref[:, :features] = low(nt(grad_pair, w_in))
     back_ref[:, features:] = two_lanes(row_sum(t * ffn))
     grad_in = low(tn(low(nn(f_in, order_ref[...])), grad_pair))
-    grad_down = low(tn(low(nn(hidden, order_units_ref[...])), grad_ffn))
-    put_blocks(send_ref, keep_ref, batch_n, grad_in, grad_down)
+    put_blocks(grads_ref, grads_ref, batch_n, grad_in, low(tn(hidden, grad_ffn)))
 
 
 def put_blocks(send_ref, keep_ref, batch_n, upper, lower):
@@ -396,7 +402,7 @@
     width = send_ref.shape[1]
     for i in range(batch_n):
         ref = send_ref if i < batch_n // 2 else keep_ref
-        start = i % (batch_n // 2) * total
+        start = i * total if send_ref is keep_ref else i % (batch_n // 2) * total
         places = [(start, upper_rows, upper), (start + upper_rows, lower_rows, lower)]
         for first, count, values in places:
             ref[first : first + count, : values.shape[1]] = values[i * count : (i + 1) * count]
@@ -406,21 +412,12 @@
                 )
 
 
-def light_backward(
+def norm_backward(
     layout,
-    meta,
-    below_ref,
-    x_ref,
-    above_ref,
     xq_ref,
     pq_ref,
-    pq_t_ref,
     pf_t_ref,
     g_ref,
-    order_ref,
-    q_ref,
-    kv_ref,
-    mixed_ref,
     heavy_raw_ref,
     middle_ref,
     f_norm_ref,
@@ -429,45 +426,18 @@
     back_ref,
     full_ref,
     grad_middle_ref,
-    grad_normed_ref,
-    halo_below_ref,
-    halo_above_ref,
+    do_ref,
     grad_raw_ref,
+    q_back_ref,
     small_grad_ref,
-    send_ref,
-    keep_ref,
-    w_qkv,
     w_lo,
-    dq_ref,
-    dkv_ref,
-    stage,
     sems,
-    out_sems,
 ):
-    tokens, features = x_ref.shape
+    features = g_ref.shape[1]
     routed = xq_ref.shape[0]
-    half = features // 2
-    copies = load(full_ref, [(layout["light_out"], w_lo), (layout["light_qkv"], w_qkv)], sems)
+    copies = load(full_ref, [(layout["light_out"], w_lo)], sems)
     small = small_ref[...]
     gain_1, gain_2 = small[0:1], small[1:2]
-    started = []
-
-    def put(at, grad):
-        width = grad.shape[1]
-        slot = len(started) % stage.shape[0]
-        if len(started) >= stage.shape[0]:
-            for copy in started[-stage.shape[0]]:
-                copy.wait()
-        stage[slot, :, :width] = low(grad)
-        both = []
-        for i, ref in enumerate((send_ref, keep_ref)):
-            source = stage.at[slot, i * half : (i + 1) * half, :width]
-            both.append(
-                pltpu.make_async_copy(source, ref.at[:, at : at + width], out_sems.at[slot, i])
-            )
-            both[-1].start()
-        started.append(both)
-
     sums = sum_blocks(back_ref, routed)
     f_norm = f_norm_ref[...]
     f_gate = sigmoid_dot(f_norm, small[4:5])
@@ -482,24 +452,70 @@
     gain_2_grad = jnp.sum(grad_n2 * (middle * inverse_2), axis=0, keepdims=True)
     grad_middle = g_ref[...].astype(F32) + rms_back(grad_n2, middle, inverse_2, gain_2)
     grad_middle_ref[...] = grad_middle
-    middle_low = low(grad_middle)
-
     q_rows = exact(pq_ref[...], grad_middle)
     xq = xq_ref[...].astype(F32)
     q_plain = xq * rms_inverse(xq)
     q_norm = q_plain * gain_1
     q_gate = sigmoid_dot(q_norm, small[2:3])
     grad_raw = low(q_rows * q_gate)
-    grad_raw_ref[...] = grad_raw
+    for i in range(grad_raw_ref.shape[0] // routed):
+        grad_raw_ref[i * routed : (i + 1) * routed] = grad_raw
     q_logit = row_sum(q_rows * heavy_raw_ref[...]) * q_gate * (1.0 - q_gate)
     q_back = q_logit * small[2:3]
+    q_back_ref[...] = q_back
     router_q = jnp.sum(q_norm * q_logit, axis=0, keepdims=True)
     gain_1_grad = jnp.sum(q_back * q_plain, axis=0, keepdims=True)
-
+    rest = jnp.zeros((4, features), F32)
+    small_grad_ref[...] = jnp.concatenate(
+        [gain_1_grad, gain_2_grad, router_q, router_f, rest], axis=0
+    )
     copies[0].wait()
-    order = order_ref[...]
-    put(3 * features, tn(low(nn(mixed_ref[...], order)), middle_low))
-    do = low(nt(middle_low, w_lo[...]))
+    do_ref[...] = low(nt(low(grad_middle), w_lo[...]))
+
+
+def light_backward(
+    layout,
+    meta,
+    below_ref,
+    x_ref,
+    above_ref,
+    pq_t_ref,
+    q_ref,
+    kv_ref,
+    mixed_ref,
+    grad_middle_ref,
+    do_ref,
+    q_back_ref,
+    small_ref,
+    small_part_ref,
+    full_ref,
+    grad_normed_ref,
+    halo_below_ref,
+    halo_above_ref,
+    small_grad_ref,
+    grads_ref,
+    w_qkv,
+    dq_ref,
+    dkv_ref,
+    stage,
+    sems,
+    out_sems,
+):
+    tokens, features = x_ref.shape
+    copies = load(full_ref, [(layout["light_qkv"], w_qkv)], sems)
+    gain_1 = small_ref[0:1]
+    started = []
+
+    def put(at, grad):
+        slot = len(started) % stage.shape[0]
+        if len(started) >= stage.shape[0]:
+            started[-stage.shape[0]].wait()
+        stage[slot] = low(grad)
+        place = grads_ref.at[:, at : at + grad.shape[1]]
+        started.append(pltpu.make_async_copy(stage.at[slot], place, out_sems.at[slot]))
+        started[-1].start()
+
+    put(3 * features, tn(mixed_ref[...], low(grad_middle_ref[...])))
     width = features // 2
     masks = head_rows(width, DL)
     scale = DL ** (-0.5)
@@ -511,7 +527,7 @@
         key_rows = slice(block * WIN, (block + 3) * WIN)
         bias = jnp.concatenate([light_bias(meta, block, tokens)] * len(masks), axis=0)
         stacked = stack_heads(q_ref[rows, cols], masks)
-        do_stacked = stack_heads(do[rows, cols], masks)
+        do_stacked = stack_heads(do_ref[rows, cols], masks)
         key = kv_ref[key_rows, cols]
         probs = softmax(nt(stacked, key) * scale + bias)
         grad_probs = nt(do_stacked, kv_ref[key_rows, value_cols])
@@ -520,10 +536,10 @@
         dkv_ref[key_rows, cols] += tn(ds, stacked) * scale
         dkv_ref[key_rows, value_cols] += tn(low(probs), do_stacked)
 
-    copies[1].wait()
+    copies[0].wait()
     xe = jnp.concatenate([below_ref[...], x_ref[...], above_ref[...]], axis=0).astype(F32)
     plain = xe * rms_inverse(xe)
-    left = low(nn(low(plain * gain_1), order))
+    left = low(plain * gain_1)
     dk = low(dkv_ref[:, :features])
     dv = low(dkv_ref[:, features:])
     inner = slice(WIN, WIN + tokens)
@@ -534,19 +550,16 @@
     own = back[inner] + nt(dq_ref[...], w_qkv[:, :features])
     halo_below_ref[...] = low(back[:WIN])
     halo_above_ref[...] = low(back[WIN + tokens :])
-    gain_1_grad = gain_1_grad + jnp.sum(own * plain[inner], axis=0, keepdims=True)
+    part = small_part_ref[...]
+    gain_1_grad = part[0:1] + jnp.sum(own * plain[inner], axis=0, keepdims=True)
     gain_1_grad = gain_1_grad + jnp.sum(back[:WIN] * plain[:WIN], axis=0, keepdims=True)
     gain_1_grad = gain_1_grad + jnp.sum(
         back[WIN + tokens :] * plain[WIN + tokens :], axis=0, keepdims=True
     )
-    grad_normed_ref[...] = own + exact(pq_t_ref[...], q_back)
-    rest = jnp.zeros((4, features), F32)
-    small_grad_ref[...] = jnp.concatenate(
-        [gain_1_grad, gain_2_grad, router_q, router_f, rest], axis=0
-    )
-    for both in started[-stage.shape[0] :]:
-        for copy in both:
-            copy.wait()
+    grad_normed_ref[...] = own + exact(pq_t_ref[...], q_back_ref[...])
+    small_grad_ref[...] = jnp.concatenate([gain_1_grad, part[1:]], axis=0)
+    for copy in started[-stage.shape[0] :]:
+        copy.wait()
 
 
 def heavy_backward(
@@ -575,7 +588,7 @@
     small = small_ref[...]
     gain_1 = small[0:1]
     place = pl.ds(pl.multiple_of(meta[6], count), count)
-    grad_raw = grad_raw_ref[...]
+    grad_raw = grad_raw_ref[place]
     do = low(nt(grad_raw, out_ref[...]))
     masks = head_rows(LANES, DH)[: HH // PARTS]
     scale = DH ** (-0.5)
@@ -685,13 +698,13 @@
     join_blocks(out_ref, 0, keep_ref, got_ref, keep_ref.shape[1])
 
 
-def join_back(backs_ref, ffn_ref, keep_ref, got_ref, out_ref, down_ref):
+def join_back(backs_ref, ffn_ref, grads_ref, out_ref, down_ref):
     blocks, routed, width = out_ref.shape
     features = ffn_ref.shape[1]
-    in_rows = keep_ref.shape[0] - down_ref.shape[0]
+    in_rows = grads_ref.shape[0] - down_ref.shape[0]
     rows = in_rows // blocks
     hidden = width - 3 * features
-    total = keep_ref[...].astype(F32) + got_ref[...].astype(F32)
+    total = grads_ref[...].astype(F32)
     down_ref[...] = total[in_rows:, :features]
     for i in range(blocks):
         out_ref[i, :, : 2 * features] = backs_ref[i * routed : (i + 1) * routed]
@@ -700,19 +713,24 @@
         out_ref[i, rows:, 3 * features :] = jnp.zeros((routed - rows, hidden), BF)
 
 
-def join_attention(keep_ref, got_ref, head_keep_ref, head_got_ref, out_ref, rest_ref):
-    wide = keep_ref.shape[1]
-    join_blocks(out_ref, 0, keep_ref, got_ref, wide)
-    join_blocks(out_ref, wide, head_keep_ref, head_got_ref, out_ref.shape[2] - wide)
+def join_heads(keep_ref, got_ref, out_ref, rest_ref):
+    join_blocks(out_ref, 0, keep_ref, got_ref, out_ref.shape[2])
     start = out_ref.shape[0] * out_ref.shape[1]
     count, features = rest_ref.shape
-    rest = head_keep_ref[start : start + count, :features].astype(F32)
-    rest_ref[...] = low(rest + head_got_ref[start : start + count, :features].astype(F32))
-
-
-def in_order(pair, own_ref, other_ref, out_ref):
-    out_ref[pair[0]] = own_ref[...]
-    out_ref[1 - pair[0]] = other_ref[...]
+    rest = keep_ref[start : start + count, :features].astype(F32)
+    rest_ref[...] = low(rest + got_ref[start : start + count, :features].astype(F32))
+
+
+def pack_units(late_ref, down_ref, out_ref):
+    blocks, routed, width = late_ref.shape
+    features = down_ref.shape[1]
+    in_rows = out_ref.shape[0] - down_ref.shape[0]
+    rows = in_rows // blocks
+    hidden = width - features
+    pieces = [late_ref[i, :, features:].astype(F32)[:rows] for i in range(blocks)]
+    out_ref[...] = jnp.zeros_like(out_ref)
+    out_ref[:in_rows, :hidden] = low(jnp.concatenate(pieces, axis=0))
+    out_ref[in_rows:, :features] = down_ref[...]
 
 
 def pack_late(t_ref, in_ref, out_ref):
@@ -752,13 +770,10 @@
             heavy_in_ref[:, at : at + hidden] = total_ref[i, :, cols].astype(F32)[:rows]
 
 
-def attention_results(total_ref, light_qkv_ref, light_out_ref, heavy_ref, small_ref):
+def head_results(total_ref, heavy_ref, small_ref):
+    features = heavy_ref.shape[1] // 3
     blocks = total_ref.shape[0]
-    wide = light_qkv_ref.shape[1]
-    features = light_out_ref.shape[1]
-    light_qkv_ref[...] = sum_leading(total_ref, slice(0, wide))
-    light_out_ref[...] = sum_leading(total_ref, slice(wide, wide + features))
-    first = wide + features
+    first = 0
     each = blocks // PARTS
     width = features // PARTS
     for kind in range(3):
@@ -801,7 +816,7 @@
         + [pl.BlockSpec(memory_space=pl.ANY)] * far,
         scratch_shapes=scratch,
         compiler_params=pltpu.CompilerParams(vmem_limit_bytes=VMEM_LIMIT),
-        cost_estimate=pl.CostEstimate(flops=flops, bytes_accessed=20_000_000, transcendentals=0),
+        cost_estimate=pl.CostEstimate(flops=flops, bytes_accessed=flops // 400, transcendentals=0),
         name=name,
     )(*args)
 
@@ -862,7 +877,7 @@
         out_specs=[rows_out] * 2,
         compiler_params=pltpu.CompilerParams(vmem_limit_bytes=VMEM_LIMIT),
         cost_estimate=pl.CostEstimate(
-            flops=height * width, bytes_accessed=6 * height * width, transcendentals=0
+            flops=height * width, bytes_accessed=height * width // 8, transcendentals=0
         ),
         name="pair_sum",
     )(keep, got, *needs)
@@ -966,8 +981,8 @@
     head_cols = head_cols.transpose(2, 0, 1, 3).reshape(PARTS, rows, 3 * LANES)
     head_cols = jnp.repeat(head_cols, query_parts, axis=0)
     head_cols = jnp.concatenate([head_cols, every(small)], axis=2)
-    sent = jnp.concatenate([every(jnp.concatenate([xq, xk], axis=1)), tall(head_cols)], axis=2)
-    travel = exchange(sent, "seq")
+    travelling = every(jnp.concatenate([xq, xk], axis=1))
+    travel = exchange(jnp.concatenate([travelling, tall(head_cols)], axis=2), "seq")
     if query_parts == 2:
         other = lax.ppermute(heavy_out, "seq", [(i, i ^ 1) for i in range(seq_n)])
         out_rows = jnp.where(
@@ -995,8 +1010,6 @@
         return jnp.where(pair == 0, jnp.flip(array, 1), array).reshape(-1)
 
     order = order_matrix(relative(index.transpose(2, 1, 0, 3)))
-    units = np.arange(hidden).reshape(2, 2, -1)
-    order_units = order_matrix(relative(units.transpose(1, 0, 2)))
     out_index = np.arange(head_width).reshape(query_parts, 2, 2, rows)
     out_index = relative(out_index.transpose(2, 1, 0, 3))
     rest = jnp.arange(head_width, LANES, dtype=out_index.dtype)
@@ -1019,7 +1032,7 @@
         (meta, xq_part, xk_all, wx, h_out),
         "svvvv",
         [
-            ((count, features), BF),
+            ((keys, features), BF),
             ((count, LANES), BF),
             ((keys, 2 * LANES), BF),
             ((count, LANES), BF),
@@ -1029,16 +1042,7 @@
         2_000_000_000,
         "heavy_forward",
     )
-    part_of, query_of = lambda i: i // query_parts, lambda i: i % query_parts
-    owner = lambda i, step: query_of(i) * PARTS + (part_of(i) + step) % PARTS
-    steps = range(PARTS)
-    raw = raw.reshape(PARTS, routed, features)
-    raw = [lax.dynamic_index_in_dim(raw, (part + step) % PARTS, 0, False) for step in steps]
-    raw = [
-        lax.ppermute(block, "seq", [(i, owner(i, step)) for i in range(seq_n)])
-        for step, block in zip(steps, raw)
-    ]
-    raw = jnp.concatenate(raw, axis=0)
+    raw = presum(exchange(raw.reshape(seq_n, routed, features), "seq"))
 
     late = call(
         pack_late,
@@ -1052,47 +1056,53 @@
     )[0]
     late = exchange(late, "seq")
     pack_width = max(2 * hidden, features)
-    piece = late[:, :rows, features:].reshape(in_rows, 2 * hidden)
-    piece = [pad_cols(piece, pack_width), pad_cols(heavy_down, pack_width)]
-    late_piece = jnp.concatenate(piece, axis=0)
-    late_other = swapped(late_piece, 2)
+    piece = call(
+        pack_units,
+        (late, heavy_down),
+        "vv",
+        [((in_rows + heavy_down.shape[0], pack_width), BF)],
+        [],
+        1_000_000,
+        "pack_units",
+        needs=[full],
+    )[0]
+    piece = lax.all_gather(piece, "batch", axis=0, tiled=True)
+    piece = piece.reshape(batch_n, -1, pack_width)
+    h_in = low(nn(order_h, piece[:, :in_rows, : 2 * hidden].reshape(features, 2 * hidden)))
+    h_down = piece[:, in_rows:, :features].reshape(hidden, features)
+    t_all = late[:, :, :features].reshape(keys, features)
+
     weight = lambda columns: pltpu.VMEM((features, columns), BF)
-    q, kv, mixed, heavy_raw, middle, normed2, f_norm, f_sent = call(
+    q, kv, mixed, base = call(
         functools.partial(light_forward, layout),
-        (meta, below, x, above, xq, raw, picks_t[0], picks[2], small_rows, full),
-        "svvvvvvvvh",
+        (meta, below, x, above, small_rows, full),
+        "svvvvh",
         [
             ((tokens, features), BF),
             ((tokens + 2 * WIN, 2 * features), BF),
             ((tokens, features), BF),
+            ((tokens, features), F32),
+        ],
+        [weight(wide), weight(features), pltpu.SemaphoreType.DMA((2,))],
+        8_000_000_000,
+        "light_forward",
+    )
+    heavy_raw, middle, normed2, f_norm, f_sent = call(
+        second_norm,
+        (base, xq, raw, picks_t[0], picks[2], small_rows),
+        "vvvvvv",
+        [
             ((routed, features), F32),
             ((tokens, features), F32),
             ((tokens, features), BF),
             ((routed, features), F32),
             ((keys, features + SMALL), BF),
         ],
-        [weight(wide), weight(features), pltpu.SemaphoreType.DMA((2,))],
-        8_000_000_000,
-        "light_forward",
+        [],
+        1_000_000,
+        "second_norm",
     )
     f_sent = exchange(f_sent.reshape(seq_n, routed, features + SMALL), "seq")
-    piece = call(
-        in_order,
-        (pair.reshape(1).astype(jnp.int32), late_piece, late_other),
-        "svv",
-        [((2,) + late_piece.shape, BF)],
-        [],
-        1_000_000,
-        "in_order",
-        needs=[middle],
-    )[0]
-    other = swapped(piece, 1)
-    piece = jnp.where(core == 0, jnp.stack([piece, other], 1), jnp.stack([other, piece], 1))
-    piece = piece.reshape((batch_n,) + late_piece.shape)
-    h_in = low(nn(order_h, piece[:, :in_rows, : 2 * hidden].reshape(features, 2 * hidden)))
-    h_down = piece[:, in_rows:, :features].reshape(hidden, features)
-    t_all = late[:, :, :features].reshape(keys, features)
-
     light_hidden = light_in.shape[1] // 2
     down_width = layout["light_down"][1] - layout["light_down"][0]
     half = features // 2
@@ -1115,70 +1125,37 @@
             weight(down_width),
             pltpu.SemaphoreType.DMA((2,)),
         ],
-        8_000_000_000,
+        1_000_000,
         "light_ffn",
     )
-    light_got = swapped(light_send, 1)
-    light_send, light_keep = halves_summed(light_keep, light_got)
-    light_got = swapped(light_send, 2)
     down_rows = hidden // batch_n
-    back, ffn_part, ffn_send, ffn_keep = call(
+    back, ffn_part, ffn_grads = call(
         functools.partial(heavy_ffn, batch_n),
-        (f_sent.reshape(keys, features + SMALL), t_all, h_in, h_down, order, order_units),
-        "vvvvvv",
+        (f_sent.reshape(keys, features + SMALL), t_all, h_in, h_down, order_h),
+        "vvvvv",
         [
             ((keys, features + SMALL), BF),
             ((keys, features), BF),
-            ((batch_n // 2 * (in_rows + down_rows), pack_width), BF),
-            ((batch_n // 2 * (in_rows + down_rows), pack_width), BF),
+            ((batch_n * (in_rows + down_rows), pack_width), BF),
         ],
         [],
         4_000_000_000,
         "heavy_ffn",
-        needs=[light_keep],
     )
     back = presum(exchange(back.reshape(seq_n, routed, features + SMALL), "seq"))
 
-    ffn_got = swapped(ffn_send, 1)
-    ffn_send, ffn_keep = halves_summed(ffn_keep, ffn_got)
-    ffn_got = swapped(ffn_send, 2)
-    light_rows = call(
-        join_light,
-        (light_keep, light_got),
-        "vv",
-        [((seq_n, rows, ffn_width), BF)],
-        [],
-        10_000_000,
-        "join_light",
-        needs=[ffn_keep],
-    )[0]
-    light_sums = exchange(light_rows, "seq")
-
-    (
-        grad_middle,
-        grad_normed,
-        halo_below,
-        halo_above,
-        grad_raw,
-        small_grad,
-        attn_send,
-        attn_keep,
-    ) = call(
-        functools.partial(light_backward, layout),
+    ffn_grads = lax.psum_scatter(ffn_grads, "batch", scatter_dimension=0, tiled=True)
+    light_got = swapped(light_send, 1)
+    light_send, light_keep = halves_summed(light_keep, light_got)
+    light_got = swapped(light_send, 2)
+
+    grad_middle, do, grad_raw, q_back, small_grad = call(
+        functools.partial(norm_backward, layout),
         (
-            meta,
-            below,
-            x,
-            above,
             xq,
             picks[0],
-            picks_t[0],
             picks_t[2],
             g,
-            order,
-            q,
-            kv,
-            mixed,
             heavy_raw,
             middle,
             f_norm,
@@ -1187,43 +1164,71 @@
             back,
             full,
         ),
-        "s" + "v" * 18 + "h",
+        "v" * 10 + "h",
         [
             ((tokens, features), F32),
+            ((tokens, features), BF),
+            ((keys, features), BF),
+            ((routed, features), F32),
+            ((8, features), F32),
+        ],
+        [weight(features), pltpu.SemaphoreType.DMA((1,))],
+        1_000_000,
+        "norm_backward",
+    )
+    grad_normed, halo_below, halo_above, small_grad, attn_grads = call(
+        functools.partial(light_backward, layout),
+        (
+            meta,
+            below,
+            x,
+            above,
+            picks_t[0],
+            q,
+            kv,
+            mixed,
+            grad_middle,
+            do,
+            q_back,
+            small_rows,
+            small_grad,
+            full,
+        ),
+        "s" + "v" * 12 + "h",
+        [
             ((tokens, features), F32),
             ((WIN, features), BF),
             ((WIN, features), BF),
-            ((routed, features), BF),
             ((8, features), F32),
-            ((half, wide + features), BF),
-            ((half, wide + features), BF),
+            ((features, wide + features), BF),
         ],
         [
             weight(wide),
-            weight(features),
             pltpu.VMEM((tokens, features), BF),
             pltpu.VMEM((tokens + 2 * WIN, 2 * features), F32),
             pltpu.VMEM((3, features, features), BF),
-            pltpu.SemaphoreType.DMA((2,)),
-            pltpu.SemaphoreType.DMA((3, 2)),
+            pltpu.SemaphoreType.DMA((1,)),
+            pltpu.SemaphoreType.DMA((3,)),
         ],
-        16_000_000_000,
+        1_000_000,
         "light_backward",
-        2,
-        [light_rows],
-    )
-
-    attn_got = swapped(attn_send, 1)
-    attn_send, attn_keep = halves_summed(attn_keep, attn_got)
-    attn_got = swapped(attn_send, 2)
-
-    blocks = [
-        lax.ppermute(grad_raw, "seq", [(owner(i, step), i) for i in range(seq_n)])
-        for step in steps
-    ]
-    blocks = jnp.stack(blocks)
-    blocks = [lax.dynamic_index_in_dim(blocks, (m - part) % PARTS, 0, False) for m in steps]
-    grad_raw = jnp.concatenate(blocks, axis=0)
+        1,
+        [light_keep],
+    )
+
+    attn_sums = lax.psum_scatter(attn_grads, BOTH, scatter_dimension=0, tiled=True)
+    light_rows = call(
+        join_light,
+        (light_keep, light_got),
+        "vv",
+        [((seq_n, rows, ffn_width), BF)],
+        [],
+        1_000_000,
+        "join_light",
+    )[0]
+    light_sums = exchange(light_rows, "seq")
+
+    grad_raw = exchange(grad_raw.reshape(seq_n, routed, features), "seq").reshape(keys, features)
     head_rows_n = head_width // batch_n
     backs, head_send, head_keep = call(
         functools.partial(heavy_backward, batch_n),
@@ -1249,17 +1254,16 @@
             ((batch_n // 2 * (in_rows + head_rows_n), head_all), BF),
         ],
         [],
-        4_000_000_000,
+        1_000_000,
         "heavy_backward",
-        needs=[attn_keep, light_sums],
     )
     backs, grad_h_down = call(
         join_back,
-        (backs, ffn_part, ffn_keep, ffn_got),
-        "vvvv",
+        (backs, ffn_part, ffn_grads),
+        "vvv",
         [((seq_n, routed, 3 * features + 2 * hidden), BF), (heavy_down.shape, F32)],
         [],
-        10_000_000,
+        1_000_000,
         "join_back",
     )
     backs = exchange(backs, "seq")
@@ -1268,13 +1272,13 @@
     head_got = swapped(head_send, 1)
     head_send, head_keep = halves_summed(head_keep, head_got)
     total, out_grads = call(
-        join_attention,
-        (attn_keep, attn_got, head_keep, swapped(head_send, 2)),
-        "vvvv",
-        [((seq_n, rows, wide + features + head_all), BF), ((out_count, features), BF)],
+        join_heads,
+        (head_keep, swapped(head_send, 2)),
+        "vv",
+        [((seq_n, rows, head_all), BF), ((out_count, features), BF)],
         [],
-        10_000_000,
-        "join_attention",
+        1_000_000,
+        "join_heads",
     )
     total = exchange(total, "seq")
     out_grads = out_grads.reshape(query_parts, rows, features)
@@ -1292,21 +1296,28 @@
         "v",
         [(light_in.shape, F32), (light_down.shape, F32)],
         [],
-        10_000_000,
+        1_000_000,
         "light_results",
     )
     grad_h_in = call(
-        hidden_results, (backs,), "v", [(heavy_in.shape, F32)], [], 10_000_000, "hidden_results"
+        hidden_results,
+        (backs,),
+        "v",
+        [(heavy_in.shape, F32)],
+        [],
+        1_000_000,
+        "hidden_results",
     )[0]
-    grad_light_qkv, grad_light_out, grad_heads, grad_small = call(
-        attention_results,
+    grad_heads, grad_small = call(
+        head_results,
         (total,),
         "v",
-        [(light_qkv.shape, F32), (light_out.shape, F32), (heavy_qkv.shape, F32), ((rows, SMALL), F32)],
+        [(heavy_qkv.shape, F32), ((rows, SMALL), F32)],
         [],
-        10_000_000,
-        "attention_results",
-    )
+        1_000_000,
+        "head_results",
+    )
+    attn_sums = attn_sums.astype(F32)
 
     from_above = shifted(halo_below, "seq", -1)
     from_below = shifted(halo_above, "seq", 1)
@@ -1330,7 +1341,7 @@
         "v" * 13,
         [((tokens, features), BF), ((tokens, features), F32)],
         [],
-        1_000_000_000,
+        1_000_000,
         "finish",
     )
     return (
@@ -1338,8 +1349,8 @@
         input_grad[None],
         grad_small[:, :2],
         grad_small[:, 2:5],
-        grad_light_qkv,
-        grad_light_out,
+        attn_sums[:, :wide],
+        attn_sums[:, wide:],
         grad_heads,
         grad_heavy_out,
         grad_light_in,

time: 425 us -> 418 us (0.984); the launches traced: 424 us -> 409 us
  blocking collectives: 0 us -> 49.1 us
  waiting for transfers between devices: 152 us -> 121 us
  Pallas kernels: 114 us -> 95.7 us
  starting transfers between devices: 93 us -> 75.6 us
  local copies, waits for them, and re-layouts: 27.3 us -> 33.6 us
    all_to_all x0 -> x1, blocking collectives: none -> 49.1 us  [exchange(): return lax.all_to_all(blocks, axis, 0, 0, tiled=True)]
    reduce_scatter x0 -> x2, waiting for transfers between devices: none -> 41.5 us  [the longest x1 41.5 us: local(): lax.psum_scatter(attn_grads, BOTH, scatter_dimension=0, tiled=True)]
    ppermute x8 -> x0, waiting for transfers between devices: 38.8 us -> none  [the longest x4 19.6 us: local(): lax.ppermute(grad_raw, 'seq', [(owner(i, step), i) for i in range(seq_n)])]
    ppermute x12 -> x6, waiting for transfers between devices: 55.1 us -> 16.4 us  [swapped(): lax.ppermute(block, 'batch', [(i, i ^ distance) for i in range(lax.axis_s...]
    all_to_all x7 -> x8, waiting for transfers between devices: 25.5 us -> 48.5 us  [exchange(): return lax.all_to_all(blocks, axis, 0, 0, tiled=True)]
    ppermute x4, waiting for transfers between devices: 23 us -> 0.01 us  [shifted(): return lax.ppermute(block, axis, route)]
    ppermute x8 -> x0, starting transfers between devices: 22.8 us -> none  [the longest x4 11.6 us: local(): lax.ppermute(block, 'seq', [(i, owner(i, step)) for i in range(seq_n)])]
    all_to_all x7 -> x8, starting transfers between devices: 44 us -> 55.8 us  [exchange(): return lax.all_to_all(blocks, axis, 0, 0, tiled=True)]
  transfers between devices with their start and end apart: 34 -> 24, of which waited for: 13 -> 12; matrix products, arithmetic and copies ran while one was open for 8% -> 10% of each run, Pallas kernels for 19% -> 19%
where the time goes in v3:
time: 418 us; the launch traced here: 409 us
  waiting for transfers between devices  121 us (29%)
  Pallas kernels  95.7 us (23%)
  starting transfers between devices  75.6 us (18%)
  blocking collectives  49.1 us (12%)
  local copies, waits for them, and re-layouts  33.6 us (8%)
  other arithmetic  14.6 us (3%)
  between operations  14.5 us (3%)
  matrix products  5.02 us (1%)
    pallas_call x18, Pallas kernels, call(): pl.pallas_call(kernel, out_shape=[jax.ShapeDtypeStruct(shape, kind) for s...  88.6 us
    all_to_all x8, starting transfers between devices, exchange(): return lax.all_to_all(blocks, axis, 0, 0, tiled=True)  55.8 us
    all_to_all x1, blocking collectives, exchange(): return lax.all_to_all(blocks, axis, 0, 0, tiled=True)  49.1 us
    all_to_all x8, waiting for transfers between devices, exchange(): return lax.all_to_all(blocks, axis, 0, 0, tiled=True)  48.5 us
    reduce_scatter x1, waiting for transfers between devices, local(): lax.psum_scatter(attn_grads, BOTH, scatter_dimension=0, tiled=True)  41.5 us
    ppermute x6, waiting for transfers between devices, swapped(): lax.ppermute(block, 'batch', [(i, i ^ distance) for i in range(lax.axis_s...  16.4 us
    unnamed x69, local copies, waits for them, and re-layouts  14.2 us
    ppermute x4, starting transfers between devices, shifted(): return lax.ppermute(block, axis, route)  12.9 us
  transfers between devices with their start and end apart: 24, of which 12 were waited for; matrix products, arithmetic and copies ran while one was open for 10% of the time, Pallas kernels for 19%

profile of v3, /device:TPU:10, one launch (start us, length us, event | category | flops | bytes accessed | tf_op | source)
XLA Modules:
  0.0 409.2 jit_solution(2055955345567332777)
XLA Ops:
  9.3 1.8 pack.1
  15.3 6.4 %all-to-all-start = ((bf16[8,32,2432]{2,1,0:T(8,128)(2,1)}), bf16[8,32,2432]{2,1,0:T(8,128)(2,1)S(1)}, u32[]{:S(2)}, u32[]{:S(2)}) async-start(bf16[8,32,2432]{2,1,0:T(8,128)(2,1)} %pad_maximum_fusion), calls=%async_computation | async-start | bytes 2490368 | tf_op jit(solution)/shard_map/all_to_all | solution.py:840
  22.7 38.2 %all-to-all-done.refs_2_ = bf16[8,32,2432]{2,1,0:T(8,128)(2,1)S(1)} async-done(((bf16[8,32,2432]{2,1,0:T(8,128)(2,1)}), bf16[8,32,2432]{2,1,0:T(8,128)(2,1)S(1)}, u32[]{:S(2)}, u32[]{:S(2)}) %all-to-all-start) | async-done | bytes 1245216 | tf_op jit(solution)/shard_map/all_to_all | solution.py:840
  61.9 2.0 pack_late.1
  64.0 49.1 %all_to_all.45.refs_0_ = bf16[8,32,1792]{2,1,0:T(8,128)(2,1)} all-to-all(bf16[8,32,1792]{2,1,0:T(8,128)(2,1)} %pack_late.1), channel_id=1, replica_groups=mesh['seq'=8,'batch'=4] {'seq'}, dimensions={0} | all-to-all | bytes 1835008 | tf_op jit(solution)/shard_map/all_to_all | solution.py:840
  113.1 5.1 %all-gather.3.cloned.1.call-done.full_ref.refs_2_.refs_13_ = bf16[768,6144]{1,0:T(8,128)(2,1)} async-done(((bf16[24,6144]{1,0:T(8,128)(2,1)}), bf16[768,6144]{1,0:T(8,128)(2,1)}) %all-gather.3.cloned.1.call-update) | async-done | bytes 9437200 | tf_op jit(solution)/shard_map/all_gather | solution.py:960
  118.2 2.1 pack_units.1
  121.2 3.2 collective-permute-done
  124.5 1.6 collective-permute-start.1
  126.9 2.6 collective-permute-start.4
  129.6 4.1 collective-permute-start.3
  135.1 3.2 stack.59.meta.refs_0_
  144.8 2.5 convolution_convert_fusion.1.wx_ref
  148.1 3.6 heavy_forward.1
  151.8 10.6 %all-to-all-start.1 = ((bf16[8,32,768]{2,1,0:T(8,128)(2,1)}), bf16[8,32,768]{2,1,0:T(8,128)(2,1)S(1)}, u32[]{:S(2)}, u32[]{:S(2)}) async-start(bf16[8,32,768]{2,1,0:T(8,128)(2,1)} %bitcast.103), calls=%async_computation.1 | async-start | bytes 786432 | tf_op jit(solution)/shard_map/all_to_all | solution.py:840
  163.1 10.0 %light_forward.1 = (bf16[256,768]{1,0:T(8,128)(2,1)}, bf16[512,1536]{1,0:T(8,128)(2,1)}, bf16[256,768]{1,0:T(8,128)(2,1)}, f32[256,768]{1,0:T(8,128)}) custom-call(s32[7]{0:T(128)} %stack.59.meta.refs_0_, bf16[128,768]{1,0:T(8,128)(2,1)} %collective-permute-done.3.below_ref.refs_1_, bf16[256,768]{1,0:T(8,128)(2,1)} %bitcast.77, bf16[128,768]{1,0:T(8,128)(2,1)} %copy-done.17, ...), custom_call_target="tpu_custom_call" | custom-call | flops 8000000000 | bytes 20000000 | tf_op jit(solution)/shard_map/light_forward/pallas_call | solution.py:811
  173.9 4.0 second_norm.1
  177.9 6.0 %all-to-all-start.2 = ((bf16[8,32,896]{2,1,0:T(8,128)(2,1)}), bf16[8,32,896]{2,1,0:T(8,128)(2,1)S(1)}, u32[]{:S(2)}, u32[]{:S(2)}) async-start(bf16[8,32,896]{2,1,0:T(8,128)(2,1)} %bitcast.100), calls=%async_computation.2 | async-start | bytes 917504 | tf_op jit(solution)/shard_map/all_to_all | solution.py:840
  185.5 1.8 slice.150
  187.3 2.1 slice.152
  190.9 2.5 convolution_convert_fusion.in_ref
  195.2 6.5 %heavy_ffn.1 = (bf16[256,896]{1,0:T(8,128)(2,1)}, bf16[256,768]{1,0:T(8,128)(2,1)}, bf16[1280,1024]{1,0:T(8,128)(2,1)}) custom-call(bf16[256,896]{1,0:T(8,128)(2,1)} %bitcast.101, bf16[256,768]{1,0:T(8,128)(2,1)} %bitcast.104, bf16[768,1024]{1,0:T(8,128)(2,1)} %convolution_convert_fusion.in_ref, bf16[512,768]{1,0:T(8,128)(2,1)} %bitcast.99, ...), custom_call_target="tpu_custom_call" | custom-call | flops 4000000000 | bytes 10000000 | tf_op jit(solution)/shard_map/heavy_ffn/pallas_call | solution.py:811
  204.0 11.9 %light_ffn.1 = (f32[256,768]{1,0:T(8,128)}, f32[256,768]{1,0:T(8,128)}, bf16[384,3072]{1,0:T(8,128)(2,1)}, bf16[384,3072]{1,0:T(8,128)(2,1)}) custom-call(bf16[256,768]{1,0:T(8,128)(2,1)} %get-tuple-element.66.normed2_ref, bf16[256,768]{1,0:T(8,128)(2,1)} %bitcast.80, bf16[768,768]{1,0:T(8,128)(2,1)} %convert_convert_fusion.order_ref, ...), custom_call_target="tpu_custom_call" | custom-call | flops 1000000 | bytes 2500 | tf_op jit(solution)/shard_map/light_ffn/pallas_call | solution.py:811
  215.9 6.9 %all-to-all-start.4 = ((bf16[8,32,896]{2,1,0:T(8,128)(2,1)}), bf16[8,32,896]{2,1,0:T(8,128)(2,1)S(1)}, u32[]{:S(2)}, u32[]{:S(2)}) async-start(bf16[8,32,896]{2,1,0:T(8,128)(2,1)} %bitcast.43), calls=%async_computation.4 | async-start | bytes 917504 | tf_op jit(solution)/shard_map/all_to_all | solution.py:840
  224.2 4.6 %pair_sum.2 = (bf16[192,3072]{1,0:T(8,128)(2,1)}, bf16[192,3072]{1,0:T(8,128)(2,1)}) custom-call(bf16[384,3072]{1,0:T(8,128)(2,1)} %get-tuple-element.77.keep_ref, bf16[384,3072]{1,0:T(8,128)(2,1)} %copy-done.6), custom_call_target="tpu_custom_call" | custom-call | flops 1179648 | bytes 147456 | tf_op jit(solution)/shard_map/pair_sum/pallas_call | solution.py:872
  228.8 2.5 collective-permute-start.11
  234.6 5.3 %norm_backward.1 = (f32[256,768]{1,0:T(8,128)}, bf16[256,768]{1,0:T(8,128)(2,1)}, bf16[256,768]{1,0:T(8,128)(2,1)}, f32[32,768]{1,0:T(8,128)}, f32[8,768]{1,0:T(8,128)}) custom-call(bf16[32,768]{1,0:T(8,128)(2,1)} %copy-done.13, f32[32,256]{1,0:T(8,128)} %fusion.11.pq_ref, f32[256,32]{1,0:T(8,128)} %fusion.8.pf_t_ref, bf16[256,768]{1,0:T(8,128)(2,1)} %bitcast.81, ...), custom_call_target="tpu_custom_call" | custom-call | flops 1000000 | bytes 2500 | tf_op jit(solution)/shard_map/norm_backward/pallas_call | solution.py:811
  239.9 6.6 %all-to-all-start.5 = ((bf16[8,32,768]{2,1,0:T(8,128)(2,1)}), bf16[8,32,768]{2,1,0:T(8,128)(2,1)S(1)}, u32[]{:S(2)}, u32[]{:S(2)}) async-start(bf16[8,32,768]{2,1,0:T(8,128)(2,1)} %bitcast.102), calls=%async_computation.5 | async-start | bytes 786432 | tf_op jit(solution)/shard_map/all_to_all | solution.py:840
  246.5 14.9 %light_backward.1 = (f32[256,768]{1,0:T(8,128)}, bf16[128,768]{1,0:T(8,128)(2,1)}, bf16[128,768]{1,0:T(8,128)(2,1)}, f32[8,768]{1,0:T(8,128)}, bf16[768,3072]{1,0:T(8,128)(2,1)}) custom-call(s32[7]{0:T(128)} %stack.59.meta.refs_0_, bf16[128,768]{1,0:T(8,128)(2,1)} %collective-permute-done.3.below_ref.refs_1_, bf16[256,768]{1,0:T(8,128)(2,1)} %bitcast.78, ...), custom_call_target="tpu_custom_call" | custom-call | flops 1000000 | bytes 2500 | tf_op jit(solution)/shard_map/light_backward/pallas_call | solution.py:811
  264.1 2.9 join_light.1
  267.1 6.3 %all-to-all-start.8 = ((bf16[8,24,3072]{2,1,0:T(8,128)(2,1)}), bf16[8,24,3072]{2,1,0:T(8,128)(2,1)S(1)}, u32[]{:S(2)}, u32[]{:S(2)}) async-start(bf16[8,24,3072]{2,1,0:T(8,128)(2,1)} %join_light.1), calls=%async_computation.10 | async-start | bytes 2359296 | tf_op jit(solution)/shard_map/all_to_all | solution.py:840
  274.3 6.8 %heavy_backward.1 = (bf16[256,1536]{1,0:T(8,128)(2,1)}, bf16[480,896]{1,0:T(8,128)(2,1)}, bf16[480,896]{1,0:T(8,128)(2,1)}) custom-call(s32[7]{0:T(128)} %stack.59.meta.refs_0_, bf16[128,768]{1,0:T(8,128)(2,1)} %constant_dynamic-slice_fusion.xq_ref, bf16[256,768]{1,0:T(8,128)(2,1)} %bitcast.89, bf16[256,768]{1,0:T(8,128)(2,1)} %bitcast.90, ...), custom_call_target="tpu_custom_call" | custom-call | flops 1000000 | bytes 2500 | tf_op jit(solution)/shard_map/heavy_backward/pallas_call | solution.py:811
  281.0 2.6 collective-permute-done.8.got_ref
  284.5 2.5 pair_sum.3
  287.9 11.3 %collective-permute-done.9.got_ref = bf16[240,896]{1,0:T(8,128)(2,1)S(1)} collective-permute-done((bf16[240,896]{1,0:T(8,128)(2,1)}, bf16[240,896]{1,0:T(8,128)(2,1)S(1)}, u32[]{:S(2)}, u32[]{:S(2)}) %collective-permute-start.9) | collective-permute-done | bytes 430112 | tf_op jit(solution)/shard_map/ppermute | solution.py:836
  299.9 2.0 join_heads.1
  301.9 6.0 %all-to-all-start.7 = ((bf16[8,24,896]{2,1,0:T(8,128)(2,1)}), bf16[8,24,896]{2,1,0:T(8,128)(2,1)S(1)}, u32[]{:S(2)}, u32[]{:S(2)}) async-start(bf16[8,24,896]{2,1,0:T(8,128)(2,1)} %get-tuple-element.99), calls=%async_computation.8 | async-start | bytes 688128 | tf_op jit(solution)/shard_map/all_to_all | solution.py:840
  307.9 2.8 join_back.1
  310.7 8.2 %all-to-all-done.7.total_ref = bf16[8,24,896]{2,1,0:T(8,128)(2,1)S(1)} async-done(((bf16[8,24,896]{2,1,0:T(8,128)(2,1)}), bf16[8,24,896]{2,1,0:T(8,128)(2,1)S(1)}, u32[]{:S(2)}, u32[]{:S(2)}) %all-to-all-start.7) | async-done | bytes 344096 | tf_op jit(solution)/shard_map/all_to_all | solution.py:840
  319.7 7.0 %all-to-all-start.6 = ((bf16[8,32,3328]{2,1,0:T(8,128)(2,1)}), bf16[8,32,3328]{2,1,0:T(8,128)(2,1)S(1)}, u32[]{:S(2)}, u32[]{:S(2)}) async-start(bf16[8,32,3328]{2,1,0:T(8,128)(2,1)} %get-tuple-element.91), calls=%async_computation.7 | async-start | bytes 3407872 | tf_op jit(solution)/shard_map/all_to_all | solution.py:840
  327.9 4.3 %collective-permute-start.6 = (bf16[128,768]{1,0:T(8,128)(2,1)}, bf16[128,768]{1,0:T(8,128)(2,1)S(1)}, u32[]{:S(2)}, u32[]{:S(2)}) collective-permute-start(bf16[128,768]{1,0:T(8,128)(2,1)} %get-tuple-element.81), channel_id=1, source_target_pairs={{0,4},{4,8},{8,12},{12,16},{16,20},{20,24},{24,28},{1,5},{5,9},{9,... | collective-permute-start | bytes 589832 | tf_op jit(solution)/shard_map/ppermute | solution.py:832
  332.2 1.9 collective-permute-start.7
  334.1 2.1 light_results.1
  336.2 6.3 %collective-permute-done.10 = bf16[24,768]{1,0:T(8,128)(2,1)S(1)} collective-permute-done((bf16[24,768]{1,0:T(8,128)(2,1)S(1)}, bf16[24,768]{1,0:T(8,128)(2,1)S(1)}, u32[]{:S(2)}, u32[]{:S(2)}) %collective-permute-start.10) | collective-permute-done | bytes 36896 | tf_op jit(solution)/shard_map/ppermute | solution.py:1288
  343.1 1.8 head_results.1
  347.7 41.5 %reduce-scatter.5.cloned.1.call-done = bf16[24,3072]{1,0:T(8,128)(2,1)} async-done(((bf16[768,3072]{1,0:T(8,128)(2,1)}), bf16[24,3072]{1,0:T(8,128)(2,1)}) %reduce-scatter.5.cloned.1.call-update) | async-done | bytes 147472 | tf_op jit(solution)/shard_map/reduce_scatter | solution.py:1219
  393.4 2.4 hidden_results.1
  396.5 5.8 %finish.1 = (bf16[256,768]{1,0:T(8,128)(2,1)}, f32[256,768]{1,0:T(8,128)}) custom-call(bf16[256,768]{1,0:T(8,128)(2,1)} %bitcast.79, f32[8,768]{1,0:T(8,128)} %get-tuple-element.60.small_ref.refs_11_, f32[256,768]{1,0:T(8,128)} %get-tuple-element.70.refs_8_.grad_middle_ref, f32[256,768]{1,0:T(8,128)} %get-tuple-element.80.grad_normed_ref, ...), custom_call_target="tpu_custom_call" | custom-call | flops 1000000 | bytes 2500 | tf_op jit(solution)/shard_map/finish/pallas_call | solution.py:811
  (157 shorter events, 48.5 us)
Async XLA Ops:
  7.2 111.1 %all-gather.3.cloned.1.call-start = ((), (), s32[]{:S(2)}) async-start(), calls=%async_computation.11 | async-start | bytes 9732096 | tf_op jit(solution)/shard_map/all_gather | solution.py:960
  9.3 4.1 %copy-start.23 = (s32[3,1,32]{2,1,0:T(1,128)S(1)}, s32[3,1,32]{2,1,0:T(1,128)}, u32[]{:S(2)}) copy-start(s32[3,1,32]{2,1,0:T(1,128)} %param.22) | copy-start | bytes 1156
  9.3 4.2 %copy-start.3 = (bf16[1,256,768]{2,1,0:T(8,128)(2,1)S(1)}, bf16[1,256,768]{2,1,0:T(8,128)(2,1)}, u32[]{:S(2)}) copy-start(bf16[1,256,768]{2,1,0:T(8,128)(2,1)} %param.19) | copy-start | bytes 1179652
  14.1 1.2 copy-start.13
  15.3 6.4 %copy-start.5 = (bf16[1,256,768]{2,1,0:T(8,128)(2,1)S(1)}, bf16[1,256,768]{2,1,0:T(8,128)(2,1)}, u32[]{:S(2)}) copy-start(bf16[1,256,768]{2,1,0:T(8,128)(2,1)} %param.20) | copy-start | bytes 1179652
  15.3 45.6 %all-to-all-start = ((bf16[8,32,2432]{2,1,0:T(8,128)(2,1)}), bf16[8,32,2432]{2,1,0:T(8,128)(2,1)S(1)}, u32[]{:S(2)}, u32[]{:S(2)}) async-start(bf16[8,32,2432]{2,1,0:T(8,128)(2,1)} %pad_maximum_fusion), calls=%async_computation | async-start | bytes 2490368 | tf_op jit(solution)/shard_map/all_to_all | solution.py:840
  21.7 165.6 %all-gather.5.cloned.1.call-start = ((), (), s32[]{:S(2)}) async-start(), calls=%async_computation.12 | async-start | bytes 3276800 | tf_op jit(solution)/shard_map/all_gather | solution.py:1069
  60.9 1.0 copy-start.1
  113.1 7.2 %copy-start.20 = (bf16[24,768]{1,0:T(8,128)(2,1)S(1)}, bf16[24,768]{1,0:T(8,128)(2,1)}, u32[]{:S(2)}) copy-start(bf16[24,768]{1,0:T(8,128)(2,1)} %param.28) | copy-start | bytes 110596
  113.1 11.3 %copy-start.2 = (bf16[8,32,2432]{2,1,0:T(8,128)(2,1)S(1)}, bf16[8,32,2432]{2,1,0:T(8,128)(2,1)}, u32[]{:S(2)}) copy-start(bf16[8,32,2432]{2,1,0:T(8,128)(2,1)} %copy-done.1) | copy-start | bytes 3735556
  120.3 4.0 collective-permute-start
  124.5 15.9 %collective-permute-start.1 = (bf16[240,896]{1,0:T(8,128)(2,1)S(1)}, bf16[240,896]{1,0:T(8,128)(2,1)S(1)}, u32[]{:S(2)}, u32[]{:S(2)}) collective-permute-start(bf16[240,896]{1,0:T(8,128)(2,1)S(1)} %get-tuple-element.138), channel_id=1, source_target_pairs={{0,2},{1,3},{2,0},{3,1},{4,6},{5,7},{6,4},{7,5},{8,10},{9,11},{10,... | collective-permute-start | bytes 1290248 | tf_op jit(solution)/shard_map/ppermute | solution.py:836
  126.9 35.5 %collective-permute-start.4 = (bf16[128,768]{1,0:T(8,128)(2,1)}, bf16[128,768]{1,0:T(8,128)(2,1)S(1)}, u32[]{:S(2)}, u32[]{:S(2)}) collective-permute-start(bf16[128,768]{1,0:T(8,128)(2,1)} %get-tuple-element.139), channel_id=1, source_target_pairs={{4,0},{8,4},{12,8},{16,12},{20,16},{24,20},{28,24},{5,1},{9,5},{13... | collective-permute-start | bytes 589832 | tf_op jit(solution)/shard_map/ppermute | solution.py:832
  129.6 32.9 %collective-permute-start.3 = (bf16[128,768]{1,0:T(8,128)(2,1)}, bf16[128,768]{1,0:T(8,128)(2,1)}, u32[]{:S(2)}, u32[]{:S(2)}) collective-permute-start(bf16[128,768]{1,0:T(8,128)(2,1)} %get-tuple-element.140), channel_id=1, source_target_pairs={{0,4},{4,8},{8,12},{12,16},{16,20},{20,24},{24,28},{1,5},{5,9},{9,... | collective-permute-start | bytes 589832 | tf_op jit(solution)/shard_map/ppermute | solution.py:832
  139.6 1.8 copy-start.24
  139.6 1.8 copy-start.26
  140.7 3.1 collective-permute-start.2
  151.8 21.3 %all-to-all-start.1 = ((bf16[8,32,768]{2,1,0:T(8,128)(2,1)}), bf16[8,32,768]{2,1,0:T(8,128)(2,1)S(1)}, u32[]{:S(2)}, u32[]{:S(2)}) async-start(bf16[8,32,768]{2,1,0:T(8,128)(2,1)} %bitcast.103), calls=%async_computation.1 | async-start | bytes 786432 | tf_op jit(solution)/shard_map/all_to_all | solution.py:840
  173.1 0.8 copy-start.9
  177.9 16.6 %all-to-all-start.2 = ((bf16[8,32,896]{2,1,0:T(8,128)(2,1)}), bf16[8,32,896]{2,1,0:T(8,128)(2,1)S(1)}, u32[]{:S(2)}, u32[]{:S(2)}) async-start(bf16[8,32,896]{2,1,0:T(8,128)(2,1)} %bitcast.100), calls=%async_computation.2 | async-start | bytes 917504 | tf_op jit(solution)/shard_map/all_to_all | solution.py:840
  183.9 124.0 %reduce-scatter.3.cloned.1.call-start = ((), (), s32[]{:S(2)}) async-start(), calls=%async_computation.13 | async-start | bytes 3276800 | tf_op jit(solution)/shard_map/reduce_scatter | solution.py:1147
  215.8 7.0 %collective-permute-start.5 = (bf16[384,3072]{1,0:T(8,128)(2,1)}, bf16[384,3072]{1,0:T(8,128)(2,1)S(1)}, u32[]{:S(2)}, u32[]{:S(2)}) collective-permute-start(bf16[384,3072]{1,0:T(8,128)(2,1)} %get-tuple-element.78), channel_id=1, source_target_pairs={{0,1},{1,0},{2,3},{3,2},{4,5},{5,4},{6,7},{7,6},{8,9},{9,8},{10,11... | collective-permute-start | bytes 7077896 | tf_op jit(solution)/shard_map/ppermute | solution.py:836
  215.9 17.9 %all-to-all-start.4 = ((bf16[8,32,896]{2,1,0:T(8,128)(2,1)}), bf16[8,32,896]{2,1,0:T(8,128)(2,1)S(1)}, u32[]{:S(2)}, u32[]{:S(2)}) async-start(bf16[8,32,896]{2,1,0:T(8,128)(2,1)} %bitcast.43), calls=%async_computation.4 | async-start | bytes 917504 | tf_op jit(solution)/shard_map/all_to_all | solution.py:840
  222.9 1.4 copy-start.6
  224.2 7.1 %copy-start.27 = (s32[32]{0:T(128)S(1)}, s32[32]{0:T(128)}, u32[]{:S(2)}) copy-start(s32[32]{0:T(128)} %copy-done.26) | copy-start | bytes 388
  224.2 7.8 %copy-start.25 = (s32[32]{0:T(128)S(1)}, s32[32]{0:T(128)}, u32[]{:S(2)}) copy-start(s32[32]{0:T(128)} %copy-done.24) | copy-start | bytes 388
  228.8 34.2 %collective-permute-start.11 = (bf16[192,3072]{1,0:T(8,128)(2,1)}, bf16[192,3072]{1,0:T(8,128)(2,1)S(1)}, u32[]{:S(2)}, u32[]{:S(2)}) collective-permute-start(bf16[192,3072]{1,0:T(8,128)(2,1)} %get-tuple-element.104), channel_id=1, source_target_pairs={{0,2},{1,3},{2,0},{3,1},{4,6},{5,7},{6,4},{7,5},{8,10},{9,11},{10,... | collective-permute-start | bytes 3538952 | tf_op jit(solution)/shard_map/ppermute | solution.py:836
  239.9 27.1 %all-to-all-start.5 = ((bf16[8,32,768]{2,1,0:T(8,128)(2,1)}), bf16[8,32,768]{2,1,0:T(8,128)(2,1)S(1)}, u32[]{:S(2)}, u32[]{:S(2)}) async-start(bf16[8,32,768]{2,1,0:T(8,128)(2,1)} %bitcast.102), calls=%async_computation.5 | async-start | bytes 786432 | tf_op jit(solution)/shard_map/all_to_all | solution.py:840
  246.5 142.6 %reduce-scatter.5.cloned.1.call-start = ((), (), s32[]{:S(2)}) async-start(), calls=%async_computation.14 | async-start | bytes 4866048 | tf_op jit(solution)/shard_map/reduce_scatter | solution.py:1219
  263.1 1.0 copy-start.11
  267.0 6.3 %copy-start.29 = (s32[2,2,2,24]{3,2,1,0:T(2,128)S(1)}, s32[2,2,2,24]{3,2,1,0:T(2,128)}, u32[]{:S(2)}) copy-start(s32[2,2,2,24]{3,2,1,0:T(2,128)} %constant.76.clone) | copy-start | bytes 2308
  267.0 6.3 %copy-start.30 = (s32[2,2,2,24]{3,2,1,0:T(2,128)S(1)}, s32[2,2,2,24]{3,2,1,0:T(2,128)}, u32[]{:S(2)}) copy-start(s32[2,2,2,24]{3,2,1,0:T(2,128)} %constant.75.clone) | copy-start | bytes 2308
  267.0 7.2 %copy-start.8 = (bf16[8,32,768]{2,1,0:T(8,128)(2,1)}, bf16[8,32,768]{2,1,0:T(8,128)(2,1)S(1)}, u32[]{:S(2)}) copy-start(bf16[8,32,768]{2,1,0:T(8,128)(2,1)S(1)} %all-to-all-done.5) | copy-start | bytes 1179652
  267.1 34.9 %all-to-all-start.8 = ((bf16[8,24,3072]{2,1,0:T(8,128)(2,1)}), bf16[8,24,3072]{2,1,0:T(8,128)(2,1)S(1)}, u32[]{:S(2)}, u32[]{:S(2)}) async-start(bf16[8,24,3072]{2,1,0:T(8,128)(2,1)} %join_light.1), calls=%async_computation.10 | async-start | bytes 2359296 | tf_op jit(solution)/shard_map/all_to_all | solution.py:840
  281.0 2.6 collective-permute-start.8
  283.6 0.9 copy-start.12
  287.0 12.2 %collective-permute-start.9 = (bf16[240,896]{1,0:T(8,128)(2,1)}, bf16[240,896]{1,0:T(8,128)(2,1)S(1)}, u32[]{:S(2)}, u32[]{:S(2)}) collective-permute-start(bf16[240,896]{1,0:T(8,128)(2,1)} %get-tuple-element.98), channel_id=1, source_target_pairs={{0,2},{1,3},{2,0},{3,1},{4,6},{5,7},{6,4},{7,5},{8,10},{9,11},{10,... | collective-permute-start | bytes 1290248 | tf_op jit(solution)/shard_map/ppermute | solution.py:836
  301.9 17.0 %copy-start.4 = (bf16[8,24,3072]{2,1,0:T(8,128)(2,1)}, bf16[8,24,3072]{2,1,0:T(8,128)(2,1)S(1)}, u32[]{:S(2)}) copy-start(bf16[8,24,3072]{2,1,0:T(8,128)(2,1)S(1)} %all-to-all-done.8.total_ref) | copy-start | bytes 3538948
  301.9 17.0 %all-to-all-start.7 = ((bf16[8,24,896]{2,1,0:T(8,128)(2,1)}), bf16[8,24,896]{2,1,0:T(8,128)(2,1)S(1)}, u32[]{:S(2)}, u32[]{:S(2)}) async-start(bf16[8,24,896]{2,1,0:T(8,128)(2,1)} %get-tuple-element.99), calls=%async_computation.8 | async-start | bytes 688128 | tf_op jit(solution)/shard_map/all_to_all | solution.py:840
  318.9 7.7 %copy-start.16 = (bf16[48,768]{1,0:T(8,128)(2,1)S(1)}, bf16[48,768]{1,0:T(8,128)(2,1)}, u32[]{:S(2)}) copy-start(bf16[48,768]{1,0:T(8,128)(2,1)} %get-tuple-element.103) | copy-start | bytes 221188
  318.9 8.3 %copy-start.31 = (s32[32]{0:T(128)S(1)}, s32[32]{0:T(128)}, u32[]{:S(2)}) copy-start(s32[32]{0:T(128)} %get-tuple-element.144) | copy-start | bytes 388
  318.9 13.3 %copy-start.32 = (bf16[128,768]{1,0:T(8,128)(2,1)S(1)}, bf16[128,768]{1,0:T(8,128)(2,1)}, u32[]{:S(2)}) copy-start(bf16[128,768]{1,0:T(8,128)(2,1)} %get-tuple-element.82) | copy-start | bytes 589828
  319.7 72.5 %all-to-all-start.6 = ((bf16[8,32,3328]{2,1,0:T(8,128)(2,1)}), bf16[8,32,3328]{2,1,0:T(8,128)(2,1)S(1)}, u32[]{:S(2)}, u32[]{:S(2)}) async-start(bf16[8,32,3328]{2,1,0:T(8,128)(2,1)} %get-tuple-element.91), calls=%async_computation.7 | async-start | bytes 3407872 | tf_op jit(solution)/shard_map/all_to_all | solution.py:840
  326.6 15.8 %collective-permute-start.10 = (bf16[24,768]{1,0:T(8,128)(2,1)S(1)}, bf16[24,768]{1,0:T(8,128)(2,1)S(1)}, u32[]{:S(2)}, u32[]{:S(2)}) collective-permute-start(bf16[24,768]{1,0:T(8,128)(2,1)S(1)} %broadcast_select_fusion), channel_id=1, source_target_pairs={{0,4},{4,0},{8,12},{12,8},{16,20},{20,16},{24,28},{28,24},{1,5},{5... | collective-permute-start | bytes 110600 | tf_op jit(solution)/shard_map/ppermute | solution.py:1288
  327.9 67.8 %collective-permute-start.6 = (bf16[128,768]{1,0:T(8,128)(2,1)}, bf16[128,768]{1,0:T(8,128)(2,1)S(1)}, u32[]{:S(2)}, u32[]{:S(2)}) collective-permute-start(bf16[128,768]{1,0:T(8,128)(2,1)} %get-tuple-element.81), channel_id=1, source_target_pairs={{0,4},{4,8},{8,12},{12,16},{16,20},{20,24},{24,28},{1,5},{5,9},{9,... | collective-permute-start | bytes 589832 | tf_op jit(solution)/shard_map/ppermute | solution.py:832
  332.2 63.6 %collective-permute-start.7 = (bf16[128,768]{1,0:T(8,128)(2,1)S(1)}, bf16[128,768]{1,0:T(8,128)(2,1)S(1)}, u32[]{:S(2)}, u32[]{:S(2)}) collective-permute-start(bf16[128,768]{1,0:T(8,128)(2,1)S(1)} %copy-done.32), channel_id=1, source_target_pairs={{4,0},{8,4},{12,8},{16,12},{20,16},{24,20},{28,24},{5,1},{9,5},{13... | collective-permute-start | bytes 589832 | tf_op jit(solution)/shard_map/ppermute | solution.py:832
  392.2 1.2 copy-start
  395.8 0.8 copy-start.19
  (9 other events, 6.5 us)
Sparse Core Ops, SparseCore 0:
  11.5 106.6 all-gather.2
  120.5 30.6 all-gather.4
  201.8 42.3 reduce-scatter.2
  261.6 127.5 reduce-scatter.4

commit v4 on v2

--- a/solution.py
+++ b/solution.py
@@ -142,10 +142,10 @@
     return row_sum(jnp.where(lanes < 2, block.astype(F32), 0.0))
 
 
-def sum_blocks(ref, count, cols=slice(None)):
-    total = ref[0:count, cols].astype(F32)
+def sum_blocks(ref, count):
+    total = ref[0:count].astype(F32)
     for i in range(1, ref.shape[0] // count):
-        total = total + ref[i * count : (i + 1) * count, cols].astype(F32)
+        total = total + ref[i * count : (i + 1) * count].astype(F32)
     return total
 
 
@@ -184,7 +184,8 @@
     probs = softmax(nt(stacked, kv_ref[:, :LANES]) * DH ** (-0.5) + bias)
     mixed = low(merge_heads(nn(low(probs), kv_ref[:, LANES:]), masks))
     mixed_ref[...] = mixed
-    raw_ref[...] = low(nn(mixed, out_ref[...]))
+    raw_ref[...] = jnp.zeros_like(raw_ref)
+    raw_ref[pl.ds(pl.multiple_of(meta[6], count), count)] = low(nn(mixed, out_ref[...]))
 
 
 def light_forward(
@@ -490,7 +491,8 @@
     q_norm = q_plain * gain_1
     q_gate = sigmoid_dot(q_norm, small[2:3])
     grad_raw = low(q_rows * q_gate)
-    grad_raw_ref[...] = grad_raw
+    for i in range(grad_raw_ref.shape[0] // routed):
+        grad_raw_ref[i * routed : (i + 1) * routed] = grad_raw
     q_logit = row_sum(q_rows * heavy_raw_ref[...]) * q_gate * (1.0 - q_gate)
     q_back = q_logit * small[2:3]
     router_q = jnp.sum(q_norm * q_logit, axis=0, keepdims=True)
@@ -575,7 +577,7 @@
     small = small_ref[...]
     gain_1 = small[0:1]
     place = pl.ds(pl.multiple_of(meta[6], count), count)
-    grad_raw = grad_raw_ref[...]
+    grad_raw = grad_raw_ref[place]
     do = low(nt(grad_raw, out_ref[...]))
     masks = head_rows(LANES, DH)[: HH // PARTS]
     scale = DH ** (-0.5)
@@ -647,7 +649,7 @@
     routed = f_norm_ref.shape[0]
     small = small_ref[...]
     gate = sigmoid_dot(f_norm_ref[...], small[4:5])
-    backs = sum_blocks(backs_ref, routed, slice(0, 3 * features))
+    backs = sum_blocks(backs_ref, routed)
     heavy = exact(pf_t_ref[...], backs[:, 2 * features :] * gate)
     output_ref[...] = low(middle_ref[...] + light_ref[...] + heavy)
     grad = grad_normed_ref[...] + exact(pq_t_ref[...], backs[:, :features])
@@ -681,23 +683,14 @@
         out_ref[i, :, at : at + width] = low(total[i * rows : (i + 1) * rows])
 
 
-def join_light(keep_ref, got_ref, out_ref):
-    join_blocks(out_ref, 0, keep_ref, got_ref, keep_ref.shape[1])
-
-
-def join_back(backs_ref, ffn_ref, keep_ref, got_ref, out_ref, down_ref):
-    blocks, routed, width = out_ref.shape
-    features = ffn_ref.shape[1]
-    in_rows = keep_ref.shape[0] - down_ref.shape[0]
-    rows = in_rows // blocks
-    hidden = width - 3 * features
-    total = keep_ref[...].astype(F32) + got_ref[...].astype(F32)
-    down_ref[...] = total[in_rows:, :features]
-    for i in range(blocks):
-        out_ref[i, :, : 2 * features] = backs_ref[i * routed : (i + 1) * routed]
-        out_ref[i, :, 2 * features : 3 * features] = ffn_ref[i * routed : (i + 1) * routed]
-        out_ref[i, :rows, 3 * features :] = low(total[i * rows : (i + 1) * rows, :hidden])
-        out_ref[i, rows:, 3 * features :] = jnp.zeros((routed - rows, hidden), BF)
+def join_ffn(light_keep_ref, light_got_ref, ffn_keep_ref, ffn_got_ref, out_ref, down_ref):
+    wide = light_keep_ref.shape[1]
+    join_blocks(out_ref, 0, light_keep_ref, light_got_ref, wide)
+    join_blocks(out_ref, wide, ffn_keep_ref, ffn_got_ref, out_ref.shape[2] - wide)
+    start = out_ref.shape[0] * out_ref.shape[1]
+    count, features = down_ref.shape
+    down = ffn_keep_ref[start : start + count, :features].astype(F32)
+    down_ref[...] = down + ffn_got_ref[start : start + count, :features].astype(F32)
 
 
 def join_attention(keep_ref, got_ref, head_keep_ref, head_got_ref, out_ref, rest_ref):
@@ -710,25 +703,8 @@
     rest_ref[...] = low(rest + head_got_ref[start : start + count, :features].astype(F32))
 
 
-def in_order(pair, own_ref, other_ref, out_ref):
-    out_ref[pair[0]] = own_ref[...]
-    out_ref[1 - pair[0]] = other_ref[...]
-
-
-def pack_late(t_ref, in_ref, out_ref):
-    features = t_ref.shape[1]
-    rows = in_ref.shape[0]
-    hidden = in_ref.shape[1] // 2 // out_ref.shape[0]
-    for i in range(out_ref.shape[0]):
-        out_ref[i, :, :features] = t_ref[...]
-        for half in range(2):
-            at = half * in_ref.shape[1] // 2 + i * hidden
-            to = features + half * hidden
-            out_ref[i, :rows, to : to + hidden] = in_ref[:, at : at + hidden]
-            out_ref[i, rows:, to : to + hidden] = jnp.zeros((out_ref.shape[1] - rows, hidden), BF)
-
-
-def light_results(total_ref, light_in_ref, light_down_ref):
+def ffn_results(total_ref, light_in_ref, light_down_ref, heavy_in_ref):
+    blocks = total_ref.shape[0]
     rows, features = total_ref.shape[1], light_down_ref.shape[1]
     wide = light_in_ref.shape[1]
     more = light_down_ref.shape[0] - rows
@@ -738,18 +714,13 @@
     rest = sum_leading(total_ref, slice(wide + features, wide + features + width))
     for i in range(rows // more):
         light_down_ref[rows:, i * width : (i + 1) * width] = rest[i * more : (i + 1) * more]
-
-
-def hidden_results(total_ref, heavy_in_ref):
-    blocks = total_ref.shape[0]
-    rows = heavy_in_ref.shape[0]
+    first = wide + features + width
     hidden = heavy_in_ref.shape[1] // 2 // blocks
-    first = total_ref.shape[2] - 2 * hidden
     for i in range(blocks):
         for half in range(2):
             at = half * heavy_in_ref.shape[1] // 2 + i * hidden
             cols = slice(first + half * hidden, first + (half + 1) * hidden)
-            heavy_in_ref[:, at : at + hidden] = total_ref[i, :, cols].astype(F32)[:rows]
+            heavy_in_ref[:, at : at + hidden] = total_ref[i, :, cols].astype(F32)
 
 
 def attention_results(total_ref, light_qkv_ref, light_out_ref, heavy_ref, small_ref):
@@ -968,6 +939,9 @@
     head_cols = jnp.concatenate([head_cols, every(small)], axis=2)
     sent = jnp.concatenate([every(jnp.concatenate([xq, xk], axis=1)), tall(head_cols)], axis=2)
     travel = exchange(sent, "seq")
+    in_cols = heavy_in.reshape(rows, 2, seq_n, hidden).transpose(2, 0, 1, 3)
+    in_cols = in_cols.reshape(seq_n, rows, 2 * hidden)
+    late = exchange(jnp.concatenate([every(t), tall(in_cols)], axis=2), "seq")
     if query_parts == 2:
         other = lax.ppermute(heavy_out, "seq", [(i, i ^ 1) for i in range(seq_n)])
         out_rows = jnp.where(
@@ -987,6 +961,13 @@
     h_out = piece[:, in_rows:, :features].reshape(batch_n, query_parts, rows, features)
     h_out = h_out.transpose(1, 0, 2, 3).reshape(head_width, features)
     h_out = jnp.pad(h_out, ((0, LANES - head_width), (0, 0)))
+    pack_width = max(2 * hidden, features)
+    piece = late[:, :rows, features:].reshape(in_rows, 2 * hidden)
+    piece = [pad_cols(piece, pack_width), pad_cols(heavy_down, pack_width)]
+    piece = canonical(jnp.concatenate(piece, axis=0), core, pair)
+    h_in = low(nn(order_h, piece[:, :in_rows, : 2 * hidden].reshape(features, 2 * hidden)))
+    h_down = piece[:, in_rows:, :features].reshape(hidden, features)
+    t_all = late[:, :, :features].reshape(keys, features)
     below = shifted(x[tokens - WIN :], "seq", 1)
     above = shifted(x[:WIN], "seq", -1)
 
@@ -1019,7 +1000,7 @@
         (meta, xq_part, xk_all, wx, h_out),
         "svvvv",
         [
-            ((count, features), BF),
+            ((keys, features), BF),
             ((count, LANES), BF),
             ((keys, 2 * LANES), BF),
             ((count, LANES), BF),
@@ -1029,33 +1010,8 @@
         2_000_000_000,
         "heavy_forward",
     )
-    part_of, query_of = lambda i: i // query_parts, lambda i: i % query_parts
-    owner = lambda i, step: query_of(i) * PARTS + (part_of(i) + step) % PARTS
-    steps = range(PARTS)
-    raw = raw.reshape(PARTS, routed, features)
-    raw = [lax.dynamic_index_in_dim(raw, (part + step) % PARTS, 0, False) for step in steps]
-    raw = [
-        lax.ppermute(block, "seq", [(i, owner(i, step)) for i in range(seq_n)])
-        for step, block in zip(steps, raw)
-    ]
-    raw = jnp.concatenate(raw, axis=0)
-
-    late = call(
-        pack_late,
-        (t, heavy_in),
-        "vv",
-        [((seq_n, routed, features + 2 * hidden), BF)],
-        [],
-        1_000_000,
-        "pack_late",
-        needs=[travel],
-    )[0]
-    late = exchange(late, "seq")
-    pack_width = max(2 * hidden, features)
-    piece = late[:, :rows, features:].reshape(in_rows, 2 * hidden)
-    piece = [pad_cols(piece, pack_width), pad_cols(heavy_down, pack_width)]
-    late_piece = jnp.concatenate(piece, axis=0)
-    late_other = swapped(late_piece, 2)
+    raw = presum(exchange(raw.reshape(seq_n, routed, features), "seq"))
+
     weight = lambda columns: pltpu.VMEM((features, columns), BF)
     q, kv, mixed, heavy_raw, middle, normed2, f_norm, f_sent = call(
         functools.partial(light_forward, layout),
@@ -1076,23 +1032,6 @@
         "light_forward",
     )
     f_sent = exchange(f_sent.reshape(seq_n, routed, features + SMALL), "seq")
-    piece = call(
-        in_order,
-        (pair.reshape(1).astype(jnp.int32), late_piece, late_other),
-        "svv",
-        [((2,) + late_piece.shape, BF)],
-        [],
-        1_000_000,
-        "in_order",
-        needs=[middle],
-    )[0]
-    other = swapped(piece, 1)
-    piece = jnp.where(core == 0, jnp.stack([piece, other], 1), jnp.stack([other, piece], 1))
-    piece = piece.reshape((batch_n,) + late_piece.shape)
-    h_in = low(nn(order_h, piece[:, :in_rows, : 2 * hidden].reshape(features, 2 * hidden)))
-    h_down = piece[:, in_rows:, :features].reshape(hidden, features)
-    t_all = late[:, :, :features].reshape(keys, features)
-
     light_hidden = light_in.shape[1] // 2
     down_width = layout["light_down"][1] - layout["light_down"][0]
     half = features // 2
@@ -1118,9 +1057,6 @@
         8_000_000_000,
         "light_ffn",
     )
-    light_got = swapped(light_send, 1)
-    light_send, light_keep = halves_summed(light_keep, light_got)
-    light_got = swapped(light_send, 2)
     down_rows = hidden // batch_n
     back, ffn_part, ffn_send, ffn_keep = call(
         functools.partial(heavy_ffn, batch_n),
@@ -1135,24 +1071,15 @@
         [],
         4_000_000_000,
         "heavy_ffn",
-        needs=[light_keep],
     )
     back = presum(exchange(back.reshape(seq_n, routed, features + SMALL), "seq"))
 
+    light_got = swapped(light_send, 1)
     ffn_got = swapped(ffn_send, 1)
+    light_send, light_keep = halves_summed(light_keep, light_got)
+    light_got = swapped(light_send, 2)
     ffn_send, ffn_keep = halves_summed(ffn_keep, ffn_got)
     ffn_got = swapped(ffn_send, 2)
-    light_rows = call(
-        join_light,
-        (light_keep, light_got),
-        "vv",
-        [((seq_n, rows, ffn_width), BF)],
-        [],
-        10_000_000,
-        "join_light",
-        needs=[ffn_keep],
-    )[0]
-    light_sums = exchange(light_rows, "seq")
 
     (
         grad_middle,
@@ -1193,7 +1120,7 @@
             ((tokens, features), F32),
             ((WIN, features), BF),
             ((WIN, features), BF),
-            ((routed, features), BF),
+            ((keys, features), BF),
             ((8, features), F32),
             ((half, wide + features), BF),
             ((half, wide + features), BF),
@@ -1210,20 +1137,12 @@
         16_000_000_000,
         "light_backward",
         2,
-        [light_rows],
     )
 
     attn_got = swapped(attn_send, 1)
     attn_send, attn_keep = halves_summed(attn_keep, attn_got)
     attn_got = swapped(attn_send, 2)
-
-    blocks = [
-        lax.ppermute(grad_raw, "seq", [(owner(i, step), i) for i in range(seq_n)])
-        for step in steps
-    ]
-    blocks = jnp.stack(blocks)
-    blocks = [lax.dynamic_index_in_dim(blocks, (m - part) % PARTS, 0, False) for m in steps]
-    grad_raw = jnp.concatenate(blocks, axis=0)
+    grad_raw = exchange(grad_raw.reshape(seq_n, routed, features), "seq").reshape(keys, features)
     head_rows_n = head_width // batch_n
     backs, head_send, head_keep = call(
         functools.partial(heavy_backward, batch_n),
@@ -1251,19 +1170,10 @@
         [],
         4_000_000_000,
         "heavy_backward",
-        needs=[attn_keep, light_sums],
-    )
-    backs, grad_h_down = call(
-        join_back,
-        (backs, ffn_part, ffn_keep, ffn_got),
-        "vvvv",
-        [((seq_n, routed, 3 * features + 2 * hidden), BF), (heavy_down.shape, F32)],
-        [],
-        10_000_000,
-        "join_back",
-    )
-    backs = exchange(backs, "seq")
-    back_rows = presum(backs[:, :, : 3 * features]) if seq_n > 16 else backs.reshape(keys, -1)
+        needs=[attn_keep],
+    )
+    backs = jnp.concatenate([backs, ffn_part], axis=1)
+    backs = presum(exchange(backs.reshape(seq_n, routed, 3 * features), "seq"))
 
     head_got = swapped(head_send, 1)
     head_send, head_keep = halves_summed(head_keep, head_got)
@@ -1275,9 +1185,21 @@
         [],
         10_000_000,
         "join_attention",
+        needs=[light_keep, ffn_keep, backs],
     )
     total = exchange(total, "seq")
     out_grads = out_grads.reshape(query_parts, rows, features)
+    ffn_rows, grad_h_down = call(
+        join_ffn,
+        (light_keep, light_got, ffn_keep, ffn_got),
+        "vvvv",
+        [((seq_n, rows, ffn_width + 2 * hidden), BF), (heavy_down.shape, F32)],
+        [],
+        10_000_000,
+        "join_ffn",
+        needs=[total],
+    )
+    ffn_rows = exchange(ffn_rows, "seq")
     if query_parts == 2:
         out_send = jnp.where(seq % 2 == 0, out_grads[1], out_grads[0])
         out_keep = jnp.where(seq % 2 == 0, out_grads[0], out_grads[1])
@@ -1286,18 +1208,15 @@
     else:
         out_grads = lax.all_to_all(out_grads, "seq", 0, 0, tiled=True, axis_index_groups=groups)
         grad_heavy_out = jnp.sum(out_grads.astype(F32), axis=0)
-    grad_light_in, grad_light_down = call(
-        light_results,
-        (light_sums,),
+    grad_light_in, grad_light_down, grad_h_in = call(
+        ffn_results,
+        (ffn_rows,),
         "v",
-        [(light_in.shape, F32), (light_down.shape, F32)],
+        [(light_in.shape, F32), (light_down.shape, F32), (heavy_in.shape, F32)],
         [],
         10_000_000,
-        "light_results",
-    )
-    grad_h_in = call(
-        hidden_results, (backs,), "v", [(heavy_in.shape, F32)], [], 10_000_000, "hidden_results"
-    )[0]
+        "ffn_results",
+    )
     grad_light_qkv, grad_light_out, grad_heads, grad_small = call(
         attention_results,
         (total,),
@@ -1319,7 +1238,7 @@
             grad_normed,
             from_below,
             from_above,
-            back_rows,
+            backs,
             picks_t[0],
             picks_t[1],
             picks_t[2],

time: 425 us -> 411 us (0.967); the launches traced: 424 us -> 404 us
  Pallas kernels: 114 us -> 94 us
  starting transfers between devices: 93 us -> 82.8 us
  other arithmetic: 17.3 us -> 25.6 us
    ppermute x8 -> x0, waiting for transfers between devices: 38.8 us -> none  [the longest x4 19.6 us: local(): lax.ppermute(grad_raw, 'seq', [(owner(i, step), i) for i in range(seq_n)])]
    all_to_all x7 -> x9, waiting for transfers between devices: 25.5 us -> 53.9 us  [exchange(): return lax.all_to_all(blocks, axis, 0, 0, tiled=True)]
    ppermute x8 -> x0, starting transfers between devices: 22.8 us -> none  [the longest x4 11.6 us: local(): lax.ppermute(block, 'seq', [(i, owner(i, step)) for i in range(seq_n)])]
    pallas_call x16 -> x12, Pallas kernels: 99.5 us -> 79.5 us  [call(): pl.pallas_call(kernel, out_shape=[jax.ShapeDtypeStruct(shape, kind) for s...]
    all_to_all x7 -> x9, starting transfers between devices: 44 us -> 61.5 us  [exchange(): return lax.all_to_all(blocks, axis, 0, 0, tiled=True)]
    ppermute x12, waiting for transfers between devices: 55.1 us -> 69.3 us  [swapped(): lax.ppermute(block, 'batch', [(i, i ^ distance) for i in range(lax.axis_s...]
    ppermute x4, waiting for transfers between devices: 23 us -> 29.6 us  [shifted(): return lax.ppermute(block, axis, route)]
    ppermute x1, waiting for transfers between devices: 5.29 us -> 0.01 us  [local(): other = lax.ppermute(out_send, 'seq', [(i, i ^ 1) for i in range(seq_n)])]
  transfers between devices with their start and end apart: 34 -> 28, of which waited for: 13 -> 12; matrix products, arithmetic and copies ran while one was open for 8% -> 11% of each run, Pallas kernels for 19% -> 14%
where the time goes in v4:
time: 411 us; the launch traced here: 404 us
  waiting for transfers between devices  153 us (37%)
  Pallas kernels  94 us (23%)
  starting transfers between devices  82.8 us (20%)
  local copies, waits for them, and re-layouts  28.4 us (7%)
  other arithmetic  25.6 us (6%)
  between operations  14.8 us (4%)
  matrix products  5.02 us (1%)
    pallas_call x12, Pallas kernels, call(): pl.pallas_call(kernel, out_shape=[jax.ShapeDtypeStruct(shape, kind) for s...  79.5 us
    ppermute x12, waiting for transfers between devices, swapped(): lax.ppermute(block, 'batch', [(i, i ^ distance) for i in range(lax.axis_s...  69.3 us
    all_to_all x9, starting transfers between devices, exchange(): return lax.all_to_all(blocks, axis, 0, 0, tiled=True)  61.5 us
    all_to_all x9, waiting for transfers between devices, exchange(): return lax.all_to_all(blocks, axis, 0, 0, tiled=True)  53.9 us
    ppermute x4, waiting for transfers between devices, shifted(): return lax.ppermute(block, axis, route)  29.6 us
    unnamed x80, local copies, waits for them, and re-layouts  14.9 us
    pallas_call x4, Pallas kernels, halves_summed(): pl.pallas_call(after(pair_sum, 2, len(needs)), grid=(width // block,), ou...  14.5 us
    ppermute x4, starting transfers between devices, shifted(): return lax.ppermute(block, axis, route)  12.3 us
  transfers between devices with their start and end apart: 28, of which 12 were waited for; matrix products, arithmetic and copies ran while one was open for 11% of the time, Pallas kernels for 14%

profile of v4, /device:TPU:10, one launch (start us, length us, event | category | flops | bytes accessed | tf_op | source)
XLA Modules:
  0.0 403.6 jit_solution(3594282515583092723)
XLA Ops:
  9.4 1.7 pack.1
  14.8 6.4 %all-to-all-start = ((bf16[8,32,2432]{2,1,0:T(8,128)(2,1)}), bf16[8,32,2432]{2,1,0:T(8,128)(2,1)S(1)}, u32[]{:S(2)}, u32[]{:S(2)}) async-start(bf16[8,32,2432]{2,1,0:T(8,128)(2,1)} %pad_maximum_fusion), calls=%async_computation | async-start | bytes 2490368 | tf_op jit(solution)/shard_map/all_to_all | solution.py:796
  22.5 4.4 %collective-permute-start.3 = (bf16[128,768]{1,0:T(8,128)(2,1)}, bf16[128,768]{1,0:T(8,128)(2,1)}, u32[]{:S(2)}, u32[]{:S(2)}) collective-permute-start(bf16[128,768]{1,0:T(8,128)(2,1)} %get-tuple-element.153), channel_id=1, source_target_pairs={{0,4},{4,8},{8,12},{12,16},{16,20},{20,24},{24,28},{1,5},{5,9},{9,... | collective-permute-start | bytes 589832 | tf_op jit(solution)/shard_map/ppermute | solution.py:788
  26.9 1.9 collective-permute-start.4
  31.2 29.1 %all-to-all-done = bf16[8,32,2432]{2,1,0:T(8,128)(2,1)S(1)} async-done(((bf16[8,32,2432]{2,1,0:T(8,128)(2,1)}), bf16[8,32,2432]{2,1,0:T(8,128)(2,1)S(1)}, u32[]{:S(2)}, u32[]{:S(2)}) %all-to-all-start) | async-done | bytes 1245216 | tf_op jit(solution)/shard_map/all_to_all | solution.py:796
  60.3 9.4 %all-to-all-start.3 = ((bf16[8,32,1792]{2,1,0:T(8,128)(2,1)}), bf16[8,32,1792]{2,1,0:T(8,128)(2,1)S(1)}, u32[]{:S(2)}, u32[]{:S(2)}) async-start(bf16[8,32,1792]{2,1,0:T(8,128)(2,1)} %fusion.6), calls=%async_computation.3 | async-start | bytes 1835008 | tf_op jit(solution)/shard_map/all_to_all | solution.py:796
  74.3 6.5 %collective-permute-done.1 = bf16[240,896]{1,0:T(8,128)(2,1)S(1)} collective-permute-done((bf16[240,896]{1,0:T(8,128)(2,1)S(1)}, bf16[240,896]{1,0:T(8,128)(2,1)S(1)}, u32[]{:S(2)}, u32[]{:S(2)}) %collective-permute-start.1) | collective-permute-done | bytes 430112 | tf_op jit(solution)/shard_map/ppermute | solution.py:792
  82.7 3.2 stack.93.meta.refs_0_
  85.9 19.3 %all-to-all-done.3 = bf16[8,32,1792]{2,1,0:T(8,128)(2,1)S(1)} async-done(((bf16[8,32,1792]{2,1,0:T(8,128)(2,1)}), bf16[8,32,1792]{2,1,0:T(8,128)(2,1)S(1)}, u32[]{:S(2)}, u32[]{:S(2)}) %all-to-all-start.3) | async-done | bytes 917536 | tf_op jit(solution)/shard_map/all_to_all | solution.py:796
  105.3 2.0 fusion.27
  110.5 1.8 maximum_select_fusion.1
  113.3 2.5 fusion.2.wx_ref.refs_9_
  115.8 3.8 heavy_forward.1
  119.5 9.1 %all-to-all-start.1 = ((bf16[8,32,768]{2,1,0:T(8,128)(2,1)}), bf16[8,32,768]{2,1,0:T(8,128)(2,1)S(1)}, u32[]{:S(2)}, u32[]{:S(2)}) async-start(bf16[8,32,768]{2,1,0:T(8,128)(2,1)} %bitcast.120), calls=%async_computation.1 | async-start | bytes 786432 | tf_op jit(solution)/shard_map/all_to_all | solution.py:796
  130.2 2.6 maximum_select_fusion.3
  133.5 2.6 all-to-all-done.1
  136.8 10.8 %light_forward.1 = (bf16[256,768]{1,0:T(8,128)(2,1)}, bf16[512,1536]{1,0:T(8,128)(2,1)}, bf16[256,768]{1,0:T(8,128)(2,1)}, f32[32,768]{1,0:T(8,128)}, f32[256,76...) custom-call(s32[7]{0:T(128)} %stack.93.meta.refs_0_, ...), custom_call_target="tpu_custom_call" | custom-call | flops 8000000000 | bytes 20000000 | tf_op jit(solution)/shard_map/light_forward/pallas_call | solution.py:767
  147.5 5.7 %all-to-all-start.2 = ((bf16[8,32,896]{2,1,0:T(8,128)(2,1)}), bf16[8,32,896]{2,1,0:T(8,128)(2,1)S(1)}, u32[]{:S(2)}, u32[]{:S(2)}) async-start(bf16[8,32,896]{2,1,0:T(8,128)(2,1)} %bitcast.110), calls=%async_computation.2 | async-start | bytes 917504 | tf_op jit(solution)/shard_map/all_to_all | solution.py:796
  156.2 2.2 maximum_select_fusion
  159.4 2.5 convolution_convert_fusion.in_ref
  162.9 6.9 %heavy_ffn.1 = (bf16[256,896]{1,0:T(8,128)(2,1)}, bf16[256,768]{1,0:T(8,128)(2,1)}, bf16[640,1024]{1,0:T(8,128)(2,1)}, bf16[640,1024]{1,0:T(8,128)(2,1)}) custom-call(bf16[256,896]{1,0:T(8,128)(2,1)} %bitcast.111, bf16[256,768]{1,0:T(8,128)(2,1)} %bitcast.121, bf16[768,1024]{1,0:T(8,128)(2,1)} %convolution_convert_fusion.in_ref, bf16[512,768]{1,0:T(8,128)(2,1)} %bitcast.109, ...), custom_call_target="tpu_custom_call" | custom-call | flops 4000000000 | bytes 20000000 | tf_op jit(solution)/shard_map/heavy_ffn/pallas_call | solution.py:767
  169.8 6.6 %all-to-all-start.4 = ((bf16[8,32,896]{2,1,0:T(8,128)(2,1)}), bf16[8,32,896]{2,1,0:T(8,128)(2,1)S(1)}, u32[]{:S(2)}, u32[]{:S(2)}) async-start(bf16[8,32,896]{2,1,0:T(8,128)(2,1)} %bitcast.113), calls=%async_computation.4 | async-start | bytes 917504 | tf_op jit(solution)/shard_map/all_to_all | solution.py:796
  177.0 11.9 %light_ffn.1 = (f32[256,768]{1,0:T(8,128)}, f32[256,768]{1,0:T(8,128)}, bf16[384,3072]{1,0:T(8,128)(2,1)}, bf16[384,3072]{1,0:T(8,128)(2,1)}) custom-call(bf16[256,768]{1,0:T(8,128)(2,1)} %get-tuple-element.73.normed2_ref, bf16[256,768]{1,0:T(8,128)(2,1)} %bitcast.115, bf16[768,768]{1,0:T(8,128)(2,1)} %convert_convert_fusion.order_ref.refs_11_, ...), custom_call_target="tpu_custom_call" | custom-call | flops 8000000000 | bytes 20000000 | tf_op jit(solution)/shard_map/light_ffn/pallas_call | solution.py:767
  189.7 20.3 %light_backward.1 = (f32[256,768]{1,0:T(8,128)}, f32[256,768]{1,0:T(8,128)}, bf16[128,768]{1,0:T(8,128)(2,1)}, bf16[128,768]{1,0:T(8,128)(2,1)}, bf16[256,768]{1...) custom-call(s32[7]{0:T(128)} %stack.93.meta.refs_0_, ...), custom_call_target="tpu_custom_call" | custom-call | flops 16000000000 | bytes 20000000 | tf_op jit(solution)/shard_map/light_backward/pallas_call | solution.py:767
  210.2 6.0 %all-to-all-start.5 = ((bf16[8,32,768]{2,1,0:T(8,128)(2,1)}), bf16[8,32,768]{2,1,0:T(8,128)(2,1)S(1)}, u32[]{:S(2)}, u32[]{:S(2)}) async-start(bf16[8,32,768]{2,1,0:T(8,128)(2,1)} %bitcast.117), calls=%async_computation.5 | async-start | bytes 786432 | tf_op jit(solution)/shard_map/all_to_all | solution.py:796
  218.5 4.6 %pair_sum.4 = (bf16[192,3072]{1,0:T(8,128)(2,1)}, bf16[192,3072]{1,0:T(8,128)(2,1)}) custom-call(bf16[384,3072]{1,0:T(8,128)(2,1)} %get-tuple-element.86.keep_ref, bf16[384,3072]{1,0:T(8,128)(2,1)} %copy-done.4), custom_call_target="tpu_custom_call" | custom-call | flops 1179648 | bytes 7077888 | tf_op jit(solution)/shard_map/pair_sum/pallas_call | solution.py:828
  223.1 2.8 all-to-all-done.5
  226.6 6.7 %heavy_backward.1 = (bf16[256,1536]{1,0:T(8,128)(2,1)}, bf16[480,896]{1,0:T(8,128)(2,1)}, bf16[480,896]{1,0:T(8,128)(2,1)}) custom-call(s32[7]{0:T(128)} %stack.93.meta.refs_0_, bf16[128,768]{1,0:T(8,128)(2,1)} %constant_dynamic-slice_fusion.xq_ref.refs_1_, bf16[256,768]{1,0:T(8,128)(2,1)} %bitcast.123, bf16[256,768]{1,0:T(8,128)(2,1)} %bitcast.118, ...), custom_call_target="tpu_custom_call" | custom-call | flops 4000000000 | bytes 20000000 | tf_op jit(solution)/shard_map/heavy_backward/pallas_call | solution.py:767
  233.3 2.2 pad_maximum_fusion.1
  235.5 6.3 %all-to-all-start.6 = ((bf16[8,32,2304]{2,1,0:T(8,128)(2,1)}), bf16[8,32,2304]{2,1,0:T(8,128)(2,1)S(1)}, u32[]{:S(2)}, u32[]{:S(2)}) async-start(bf16[8,32,2304]{2,1,0:T(8,128)(2,1)} %bitcast.55), calls=%async_computation.6 | async-start | bytes 2359296 | tf_op jit(solution)/shard_map/all_to_all | solution.py:796
  242.9 3.3 collective-permute-done.11.got_ref
  247.2 2.5 pair_sum.5
  251.4 3.0 pair_sum.7
  254.3 4.6 %pair_sum.6 = (bf16[192,3072]{1,0:T(8,128)(2,1)}, bf16[192,3072]{1,0:T(8,128)(2,1)}) custom-call(bf16[384,3072]{1,0:T(8,128)(2,1)} %get-tuple-element.99.keep_ref, bf16[384,3072]{1,0:T(8,128)(2,1)} %collective-permute-done.13.got_ref), custom_call_target="tpu_custom_call" | custom-call | flops 1179648 | bytes 7077888 | tf_op jit(solution)/shard_map/pair_sum/pallas_call | solution.py:828
  258.9 12.6 %collective-permute-done.10.refs_1_ = bf16[192,3072]{1,0:T(8,128)(2,1)} collective-permute-done((bf16[192,3072]{1,0:T(8,128)(2,1)}, bf16[192,3072]{1,0:T(8,128)(2,1)}, u32[]{:S(2)}, u32[]{:S(2)}) %collective-permute-start.10) | collective-permute-done | bytes 1179680 | tf_op jit(solution)/shard_map/ppermute | solution.py:792
  271.5 8.2 %collective-permute-done.12.refs_3_ = bf16[240,896]{1,0:T(8,128)(2,1)S(1)} collective-permute-done((bf16[240,896]{1,0:T(8,128)(2,1)}, bf16[240,896]{1,0:T(8,128)(2,1)S(1)}, u32[]{:S(2)}, u32[]{:S(2)}) %collective-permute-start.12) | collective-permute-done | bytes 430112 | tf_op jit(solution)/shard_map/ppermute | solution.py:792
  280.8 3.3 join_attention.1
  284.1 6.0 %all-to-all-start.7 = ((bf16[8,24,3968]{2,1,0:T(8,128)(2,1)}), bf16[8,24,3968]{2,1,0:T(8,128)(2,1)S(1)}, u32[]{:S(2)}, u32[]{:S(2)}) async-start(bf16[8,24,3968]{2,1,0:T(8,128)(2,1)} %get-tuple-element.105), calls=%async_computation.7 | async-start | bytes 3047424 | tf_op jit(solution)/shard_map/all_to_all | solution.py:796
  292.1 38.7 %collective-permute-done.17.refs_3_ = bf16[320,1024]{1,0:T(8,128)(2,1)S(1)} collective-permute-done((bf16[320,1024]{1,0:T(8,128)(2,1)}, bf16[320,1024]{1,0:T(8,128)(2,1)S(1)}, u32[]{:S(2)}, u32[]{:S(2)}) %collective-permute-start.17) | collective-permute-done | bytes 655392 | tf_op jit(solution)/shard_map/ppermute | solution.py:792
  333.2 3.6 join_ffn.1
  336.8 6.1 %all-to-all-start.8 = ((bf16[8,24,4096]{2,1,0:T(8,128)(2,1)}), bf16[8,24,4096]{2,1,0:T(8,128)(2,1)S(1)}, u32[]{:S(2)}, u32[]{:S(2)}) async-start(bf16[8,24,4096]{2,1,0:T(8,128)(2,1)} %get-tuple-element.113), calls=%async_computation.8 | async-start | bytes 3145728 | tf_op jit(solution)/shard_map/all_to_all | solution.py:796
  343.6 3.4 collective-permute-start.7
  347.0 2.6 collective-permute-start.8
  351.2 27.4 %collective-permute-done.7.from_below_ref = bf16[128,768]{1,0:T(8,128)(2,1)S(1)} collective-permute-done((bf16[128,768]{1,0:T(8,128)(2,1)S(1)}, bf16[128,768]{1,0:T(8,128)(2,1)S(1)}, u32[]{:S(2)}, u32[]{:S(2)}) %collective-permute-start.7) | collective-permute-done | bytes 196640 | tf_op jit(solution)/shard_map/ppermute | solution.py:788
  378.6 2.1 collective-permute-done.8.from_above_ref
  381.5 5.7 %finish.1 = (bf16[256,768]{1,0:T(8,128)(2,1)}, f32[256,768]{1,0:T(8,128)}) custom-call(bf16[256,768]{1,0:T(8,128)(2,1)} %bitcast.97, f32[8,768]{1,0:T(8,128)} %get-tuple-element.65.small_ref.refs_7_, f32[256,768]{1,0:T(8,128)} %get-tuple-element.77.grad_middle_ref, f32[256,768]{1,0:T(8,128)} %get-tuple-element.78.grad_normed_ref, ...), custom_call_target="tpu_custom_call" | custom-call | flops 1000000000 | bytes 20000000 | tf_op jit(solution)/shard_map/finish/pallas_call | solution.py:767
  387.8 2.3 attention_results.1
  394.0 2.5 ffn_results.1
  (179 shorter events, 49.2 us)
Async XLA Ops:
  7.2 5.4 %copy-start.33 = (bf16[24,2]{0,1:T(2,128)(2,1)S(1)}, bf16[24,2]{0,1:T(2,128)(2,1)}, u32[]{:S(2)}) copy-start(bf16[24,2]{0,1:T(2,128)(2,1)} %param.25) | copy-start | bytes 292
  7.2 5.4 %copy-start.32 = (bf16[24,3]{0,1:T(4,128)(2,1)S(1)}, bf16[24,3]{0,1:T(4,128)(2,1)}, u32[]{:S(2)}) copy-start(bf16[24,3]{0,1:T(4,128)(2,1)} %param.26) | copy-start | bytes 436
  7.2 128.8 %all-gather.2.cloned.1.call-start = ((), (), s32[]{:S(2)}) async-start(), calls=%async_computation.9 | async-start | bytes 9732096 | tf_op jit(solution)/shard_map/all_gather | solution.py:916
  11.1 1.7 copy-start.29
  11.1 1.9 copy-start.3
  14.8 6.4 %copy-start.24 = (bf16[24,768]{1,0:T(8,128)(2,1)S(1)}, bf16[24,768]{1,0:T(8,128)(2,1)}, u32[]{:S(2)}) copy-start(bf16[24,768]{1,0:T(8,128)(2,1)} %param.30) | copy-start | bytes 110596
  14.8 14.0 %copy-start.16 = (bf16[24,8192]{1,0:T(8,128)(2,1)S(1)}, bf16[24,8192]{1,0:T(8,128)(2,1)}, u32[]{:S(2)}) copy-start(bf16[24,8192]{1,0:T(8,128)(2,1)} %param.33) | copy-start | bytes 1179652
  14.8 45.5 %all-to-all-start = ((bf16[8,32,2432]{2,1,0:T(8,128)(2,1)}), bf16[8,32,2432]{2,1,0:T(8,128)(2,1)S(1)}, u32[]{:S(2)}, u32[]{:S(2)}) async-start(bf16[8,32,2432]{2,1,0:T(8,128)(2,1)} %pad_maximum_fusion), calls=%async_computation | async-start | bytes 2490368 | tf_op jit(solution)/shard_map/all_to_all | solution.py:796
  21.1 49.8 %collective-permute-start = (bf16[24,768]{1,0:T(8,128)(2,1)S(1)}, bf16[24,768]{1,0:T(8,128)(2,1)S(1)}, u32[]{:S(2)}, u32[]{:S(2)}) collective-permute-start(bf16[24,768]{1,0:T(8,128)(2,1)S(1)} %copy-done.24), channel_id=1, source_target_pairs={{0,4},{4,0},{8,12},{12,8},{16,20},{20,16},{24,28},{28,24},{1,5},{5... | collective-permute-start | bytes 110600 | tf_op jit(solution)/shard_map/ppermute | solution.py:946
  22.5 7.1 %copy-start.36 = (s32[1,4]{1,0:T(1,128)S(1)}, s32[1,4]{1,0:T(1,128)}, u32[]{:S(2)}) copy-start(s32[1,4]{1,0:T(1,128)} %param.23) | copy-start | bytes 52
  22.5 7.3 %copy-start.17 = (bf16[1,256,768]{2,1,0:T(8,128)(2,1)S(1)}, bf16[1,256,768]{2,1,0:T(8,128)(2,1)}, u32[]{:S(2)}) copy-start(bf16[1,256,768]{2,1,0:T(8,128)(2,1)} %param.22) | copy-start | bytes 1179652
  22.5 111.0 %collective-permute-start.3 = (bf16[128,768]{1,0:T(8,128)(2,1)}, bf16[128,768]{1,0:T(8,128)(2,1)}, u32[]{:S(2)}, u32[]{:S(2)}) collective-permute-start(bf16[128,768]{1,0:T(8,128)(2,1)} %get-tuple-element.153), channel_id=1, source_target_pairs={{0,4},{4,8},{8,12},{12,16},{16,20},{20,24},{24,28},{1,5},{5,9},{9,... | collective-permute-start | bytes 589832 | tf_op jit(solution)/shard_map/ppermute | solution.py:788
  26.9 106.6 %collective-permute-start.4 = (bf16[128,768]{1,0:T(8,128)(2,1)}, bf16[128,768]{1,0:T(8,128)(2,1)}, u32[]{:S(2)}, u32[]{:S(2)}) collective-permute-start(bf16[128,768]{1,0:T(8,128)(2,1)} %get-tuple-element.152), channel_id=1, source_target_pairs={{4,0},{8,4},{12,8},{16,12},{20,16},{24,20},{28,24},{5,1},{9,5},{13... | collective-permute-start | bytes 589832 | tf_op jit(solution)/shard_map/ppermute | solution.py:788
  60.3 44.9 %all-to-all-start.3 = ((bf16[8,32,1792]{2,1,0:T(8,128)(2,1)}), bf16[8,32,1792]{2,1,0:T(8,128)(2,1)S(1)}, u32[]{:S(2)}, u32[]{:S(2)}) async-start(bf16[8,32,1792]{2,1,0:T(8,128)(2,1)} %fusion.6), calls=%async_computation.3 | async-start | bytes 1835008 | tf_op jit(solution)/shard_map/all_to_all | solution.py:796
  71.9 14.0 %copy-start.25 = (s32[2,2,8,24]{3,2,1,0:T(8,128)S(1)}, s32[2,2,8,24]{3,2,1,0:T(8,128)}, u32[]{:S(2)}) copy-start(s32[2,2,8,24]{3,2,1,0:T(8,128)} %constant.77.clone) | copy-start | bytes 9220
  71.9 14.0 %copy-start.26 = (s32[2,2,8,24]{3,2,1,0:T(8,128)S(1)}, s32[2,2,8,24]{3,2,1,0:T(8,128)}, u32[]{:S(2)}) copy-start(s32[2,2,8,24]{3,2,1,0:T(8,128)} %constant.78.clone) | copy-start | bytes 9220
  71.9 9.0 %collective-permute-start.1 = (bf16[240,896]{1,0:T(8,128)(2,1)S(1)}, bf16[240,896]{1,0:T(8,128)(2,1)S(1)}, u32[]{:S(2)}, u32[]{:S(2)}) collective-permute-start(bf16[240,896]{1,0:T(8,128)(2,1)S(1)} %get-tuple-element.151), channel_id=1, source_target_pairs={{0,2},{1,3},{2,0},{3,1},{4,6},{5,7},{6,4},{7,5},{8,10},{9,11},{10,... | collective-permute-start | bytes 1290248 | tf_op jit(solution)/shard_map/ppermute | solution.py:792
  82.7 27.8 %collective-permute-start.2 = (bf16[2,240,896]{2,1,0:T(8,128)(2,1)}, bf16[2,240,896]{2,1,0:T(8,128)(2,1)}, u32[]{:S(2)}, u32[]{:S(2)}) collective-permute-start(bf16[2,240,896]{2,1,0:T(8,128)(2,1)} %maximum_select_fusion.5), channel_id=1, source_target_pairs={{0,1},{1,0},{2,3},{3,2},{4,5},{5,4},{6,7},{7,6},{8,9},{9,8},{10,11... | collective-permute-start | bytes 2580488 | tf_op jit(solution)/shard_map/ppermute | solution.py:792
  107.3 3.0 copy-start.6
  107.3 3.0 copy-start.7
  107.3 22.9 %collective-permute-start.5 = (bf16[320,1024]{1,0:T(8,128)(2,1)}, bf16[320,1024]{1,0:T(8,128)(2,1)}, u32[]{:S(2)}, u32[]{:S(2)}) collective-permute-start(bf16[320,1024]{1,0:T(8,128)(2,1)} %get-tuple-element.148), channel_id=1, source_target_pairs={{0,2},{1,3},{2,0},{3,1},{4,6},{5,7},{6,4},{7,5},{8,10},{9,11},{10,... | collective-permute-start | bytes 1966088 | tf_op jit(solution)/shard_map/ppermute | solution.py:792
  119.5 16.5 %all-to-all-start.1 = ((bf16[8,32,768]{2,1,0:T(8,128)(2,1)}), bf16[8,32,768]{2,1,0:T(8,128)(2,1)S(1)}, u32[]{:S(2)}, u32[]{:S(2)}) async-start(bf16[8,32,768]{2,1,0:T(8,128)(2,1)} %bitcast.120), calls=%async_computation.1 | async-start | bytes 786432 | tf_op jit(solution)/shard_map/all_to_all | solution.py:796
  132.8 23.4 %collective-permute-start.6 = (bf16[2,320,1024]{2,1,0:T(8,128)(2,1)}, bf16[2,320,1024]{2,1,0:T(8,128)(2,1)}, u32[]{:S(2)}, u32[]{:S(2)}) collective-permute-start(bf16[2,320,1024]{2,1,0:T(8,128)(2,1)} %maximum_select_fusion.3), channel_id=1, source_target_pairs={{0,1},{1,0},{2,3},{3,2},{4,5},{5,4},{6,7},{7,6},{8,9},{9,8},{10,11... | collective-permute-start | bytes 3932168 | tf_op jit(solution)/shard_map/ppermute | solution.py:792
  147.5 14.5 %all-to-all-start.2 = ((bf16[8,32,896]{2,1,0:T(8,128)(2,1)}), bf16[8,32,896]{2,1,0:T(8,128)(2,1)S(1)}, u32[]{:S(2)}, u32[]{:S(2)}) async-start(bf16[8,32,896]{2,1,0:T(8,128)(2,1)} %bitcast.110), calls=%async_computation.2 | async-start | bytes 917504 | tf_op jit(solution)/shard_map/all_to_all | solution.py:796
  169.8 19.1 %all-to-all-start.4 = ((bf16[8,32,896]{2,1,0:T(8,128)(2,1)}), bf16[8,32,896]{2,1,0:T(8,128)(2,1)S(1)}, u32[]{:S(2)}, u32[]{:S(2)}) async-start(bf16[8,32,896]{2,1,0:T(8,128)(2,1)} %bitcast.113), calls=%async_computation.4 | async-start | bytes 917504 | tf_op jit(solution)/shard_map/all_to_all | solution.py:796
  189.7 26.5 %copy-start.30 = (s32[2,2,2,24]{3,2,1,0:T(2,128)S(1)}, s32[2,2,2,24]{3,2,1,0:T(2,128)}, u32[]{:S(2)}) copy-start(s32[2,2,2,24]{3,2,1,0:T(2,128)} %constant.81.clone) | copy-start | bytes 2308
  189.7 26.5 %copy-start.31 = (s32[2,2,2,24]{3,2,1,0:T(2,128)S(1)}, s32[2,2,2,24]{3,2,1,0:T(2,128)}, u32[]{:S(2)}) copy-start(s32[2,2,2,24]{3,2,1,0:T(2,128)} %constant.82.clone) | copy-start | bytes 2308
  210.1 7.0 %collective-permute-start.9 = (bf16[384,3072]{1,0:T(8,128)(2,1)}, bf16[384,3072]{1,0:T(8,128)(2,1)S(1)}, u32[]{:S(2)}, u32[]{:S(2)}) collective-permute-start(bf16[384,3072]{1,0:T(8,128)(2,1)} %get-tuple-element.87), channel_id=1, source_target_pairs={{0,1},{1,0},{2,3},{3,2},{4,5},{5,4},{6,7},{7,6},{8,9},{9,8},{10,11... | collective-permute-start | bytes 7077896 | tf_op jit(solution)/shard_map/ppermute | solution.py:792
  210.2 15.7 %all-to-all-start.5 = ((bf16[8,32,768]{2,1,0:T(8,128)(2,1)}), bf16[8,32,768]{2,1,0:T(8,128)(2,1)S(1)}, u32[]{:S(2)}, u32[]{:S(2)}) async-start(bf16[8,32,768]{2,1,0:T(8,128)(2,1)} %bitcast.117), calls=%async_computation.5 | async-start | bytes 786432 | tf_op jit(solution)/shard_map/all_to_all | solution.py:796
  217.1 37.3 %collective-permute-start.13 = (bf16[384,3072]{1,0:T(8,128)(2,1)}, bf16[384,3072]{1,0:T(8,128)(2,1)}, u32[]{:S(2)}, u32[]{:S(2)}) collective-permute-start(bf16[384,3072]{1,0:T(8,128)(2,1)} %get-tuple-element.100), channel_id=1, source_target_pairs={{0,1},{1,0},{2,3},{3,2},{4,5},{5,4},{6,7},{7,6},{8,9},{9,8},{10,11... | collective-permute-start | bytes 7077896 | tf_op jit(solution)/shard_map/ppermute | solution.py:792
  217.1 1.4 copy-start.4
  226.6 6.7 %copy-start.15 = (bf16[256,768]{1,0:T(8,128)(2,1)S(1)}, bf16[256,768]{1,0:T(8,128)(2,1)}, u32[]{:S(2)}) copy-start(bf16[256,768]{1,0:T(8,128)(2,1)} %get-tuple-element.90) | copy-start | bytes 1179652
  235.5 44.1 %all-to-all-start.6 = ((bf16[8,32,2304]{2,1,0:T(8,128)(2,1)}), bf16[8,32,2304]{2,1,0:T(8,128)(2,1)S(1)}, u32[]{:S(2)}, u32[]{:S(2)}) async-start(bf16[8,32,2304]{2,1,0:T(8,128)(2,1)} %bitcast.55), calls=%async_computation.6 | async-start | bytes 2359296 | tf_op jit(solution)/shard_map/all_to_all | solution.py:796
  241.8 8.5 %collective-permute-start.14 = (bf16[640,1024]{1,0:T(8,128)(2,1)}, bf16[640,1024]{1,0:T(8,128)(2,1)S(1)}, u32[]{:S(2)}, u32[]{:S(2)}) collective-permute-start(bf16[640,1024]{1,0:T(8,128)(2,1)} %get-tuple-element.103), channel_id=1, source_target_pairs={{0,1},{1,0},{2,3},{3,2},{4,5},{5,4},{6,7},{7,6},{8,9},{9,8},{10,11... | collective-permute-start | bytes 3932168 | tf_op jit(solution)/shard_map/ppermute | solution.py:792
  241.8 4.5 %collective-permute-start.11 = (bf16[480,896]{1,0:T(8,128)(2,1)}, bf16[480,896]{1,0:T(8,128)(2,1)S(1)}, u32[]{:S(2)}, u32[]{:S(2)}) collective-permute-start(bf16[480,896]{1,0:T(8,128)(2,1)} %get-tuple-element.96), channel_id=1, source_target_pairs={{0,1},{1,0},{2,3},{3,2},{4,5},{5,4},{6,7},{7,6},{8,9},{9,8},{10,11... | collective-permute-start | bytes 2580488 | tf_op jit(solution)/shard_map/ppermute | solution.py:792
  242.3 29.2 %collective-permute-start.10 = (bf16[192,3072]{1,0:T(8,128)(2,1)}, bf16[192,3072]{1,0:T(8,128)(2,1)}, u32[]{:S(2)}, u32[]{:S(2)}) collective-permute-start(bf16[192,3072]{1,0:T(8,128)(2,1)} %get-tuple-element.94), channel_id=1, source_target_pairs={{0,2},{1,3},{2,0},{3,1},{4,6},{5,7},{6,4},{7,5},{8,10},{9,11},{10,... | collective-permute-start | bytes 3538952 | tf_op jit(solution)/shard_map/ppermute | solution.py:792
  249.7 29.9 %collective-permute-start.12 = (bf16[240,896]{1,0:T(8,128)(2,1)}, bf16[240,896]{1,0:T(8,128)(2,1)S(1)}, u32[]{:S(2)}, u32[]{:S(2)}) collective-permute-start(bf16[240,896]{1,0:T(8,128)(2,1)} %get-tuple-element.98), channel_id=1, source_target_pairs={{0,2},{1,3},{2,0},{3,1},{4,6},{5,7},{6,4},{7,5},{8,10},{9,11},{10,... | collective-permute-start | bytes 1290248 | tf_op jit(solution)/shard_map/ppermute | solution.py:792
  284.1 46.7 %all-to-all-start.7 = ((bf16[8,24,3968]{2,1,0:T(8,128)(2,1)}), bf16[8,24,3968]{2,1,0:T(8,128)(2,1)S(1)}, u32[]{:S(2)}, u32[]{:S(2)}) async-start(bf16[8,24,3968]{2,1,0:T(8,128)(2,1)} %get-tuple-element.105), calls=%async_computation.7 | async-start | bytes 3047424 | tf_op jit(solution)/shard_map/all_to_all | solution.py:796
  290.1 40.7 %collective-permute-start.16 = (bf16[192,3072]{1,0:T(8,128)(2,1)}, bf16[192,3072]{1,0:T(8,128)(2,1)S(1)}, u32[]{:S(2)}, u32[]{:S(2)}) collective-permute-start(bf16[192,3072]{1,0:T(8,128)(2,1)} %get-tuple-element.111), channel_id=1, source_target_pairs={{0,2},{1,3},{2,0},{3,1},{4,6},{5,7},{6,4},{7,5},{8,10},{9,11},{10,... | collective-permute-start | bytes 3538952 | tf_op jit(solution)/shard_map/ppermute | solution.py:792
  290.7 40.1 %collective-permute-start.17 = (bf16[320,1024]{1,0:T(8,128)(2,1)}, bf16[320,1024]{1,0:T(8,128)(2,1)S(1)}, u32[]{:S(2)}, u32[]{:S(2)}) collective-permute-start(bf16[320,1024]{1,0:T(8,128)(2,1)} %get-tuple-element.112), channel_id=1, source_target_pairs={{0,2},{1,3},{2,0},{3,1},{4,6},{5,7},{6,4},{7,5},{8,10},{9,11},{10,... | collective-permute-start | bytes 1966088 | tf_op jit(solution)/shard_map/ppermute | solution.py:792
  336.8 6.8 %copy-start.35 = (bf16[128,768]{1,0:T(8,128)(2,1)S(1)}, bf16[128,768]{1,0:T(8,128)(2,1)}, u32[]{:S(2)}) copy-start(bf16[128,768]{1,0:T(8,128)(2,1)} %get-tuple-element.79) | copy-start | bytes 589828
  336.8 10.2 %copy-start.34 = (bf16[128,768]{1,0:T(8,128)(2,1)S(1)}, bf16[128,768]{1,0:T(8,128)(2,1)}, u32[]{:S(2)}) copy-start(bf16[128,768]{1,0:T(8,128)(2,1)} %get-tuple-element.80) | copy-start | bytes 589828
  336.8 12.8 %copy-start.20 = (bf16[48,768]{1,0:T(8,128)(2,1)S(1)}, bf16[48,768]{1,0:T(8,128)(2,1)}, u32[]{:S(2)}) copy-start(bf16[48,768]{1,0:T(8,128)(2,1)} %get-tuple-element.110) | copy-start | bytes 221188
  336.8 56.1 %all-to-all-start.8 = ((bf16[8,24,4096]{2,1,0:T(8,128)(2,1)}), bf16[8,24,4096]{2,1,0:T(8,128)(2,1)S(1)}, u32[]{:S(2)}, u32[]{:S(2)}) async-start(bf16[8,24,4096]{2,1,0:T(8,128)(2,1)} %get-tuple-element.113), calls=%async_computation.8 | async-start | bytes 3145728 | tf_op jit(solution)/shard_map/all_to_all | solution.py:796
  343.6 35.0 %collective-permute-start.7 = (bf16[128,768]{1,0:T(8,128)(2,1)S(1)}, bf16[128,768]{1,0:T(8,128)(2,1)S(1)}, u32[]{:S(2)}, u32[]{:S(2)}) collective-permute-start(bf16[128,768]{1,0:T(8,128)(2,1)S(1)} %copy-done.35), channel_id=1, source_target_pairs={{0,4},{4,8},{8,12},{12,16},{16,20},{20,24},{24,28},{1,5},{5,9},{9,... | collective-permute-start | bytes 589832 | tf_op jit(solution)/shard_map/ppermute | solution.py:788
  347.0 33.8 %collective-permute-start.8 = (bf16[128,768]{1,0:T(8,128)(2,1)S(1)}, bf16[128,768]{1,0:T(8,128)(2,1)S(1)}, u32[]{:S(2)}, u32[]{:S(2)}) collective-permute-start(bf16[128,768]{1,0:T(8,128)(2,1)S(1)} %copy-done.34), channel_id=1, source_target_pairs={{4,0},{8,4},{12,8},{16,12},{20,16},{24,20},{28,24},{5,1},{9,5},{13... | collective-permute-start | bytes 589832 | tf_op jit(solution)/shard_map/ppermute | solution.py:788
  349.7 37.5 %collective-permute-start.15 = (bf16[24,768]{1,0:T(8,128)(2,1)S(1)}, bf16[24,768]{1,0:T(8,128)(2,1)S(1)}, u32[]{:S(2)}, u32[]{:S(2)}) collective-permute-start(bf16[24,768]{1,0:T(8,128)(2,1)S(1)} %broadcast_select_fusion), channel_id=1, source_target_pairs={{0,4},{4,0},{8,12},{12,8},{16,20},{20,16},{24,28},{28,24},{1,5},{5... | collective-permute-start | bytes 110600 | tf_op jit(solution)/shard_map/ppermute | solution.py:1206
  378.6 2.2 copy-start.21
  (18 other events, 17.3 us)
Sparse Core Ops, SparseCore 0:
  11.2 106.5 all-gather.1
